TPU v7x, 32 devices: a whole 2x2x4 slice. The times are simulated.
32 devices in a mesh: ctx: 16 (over z, y, core), fsdp: 2 (over x).
Axes of the slice: x: 2, y: 2, z: 4, core: 2. Of those that a mesh axis runs over, the one named last changes fastest.
Arguments:
- tokens: bfloat16 [3, 2, 1024, 768], P(None, 'fsdp', 'ctx'), may hold values from -6 to 6
- offsets: int32 [3, 2, 16], P(None, 'fsdp'), may hold values from 0 to 15, each once within a row
- norm1_gain: float32 [768], replicated, may hold values from 0.5 to 1.5
- norm2_gain: float32 [768], replicated, may hold values from 0.5 to 1.5
- bias_table: float32 [32, 12], replicated, may hold values from -4 to 4
- w_query: bfloat16 [768, 768], P('fsdp'), may hold values from -0.109375 to 0.109375
- w_key: bfloat16 [768, 768], P('fsdp'), may hold values from -0.109375 to 0.109375
- w_value: bfloat16 [768, 768], P('fsdp'), may hold values from -0.21875 to 0.21875
- w_out: bfloat16 [768, 768], P('fsdp'), may hold values from -1.75 to 1.75
- w_gate: bfloat16 [768, 2048], P('fsdp'), may hold values from -0.21875 to 0.21875
- w_up: bfloat16 [768, 2048], P('fsdp'), may hold values from -0.21875 to 0.21875
- w_down: bfloat16 [2048, 768], P('fsdp'), may hold values from -0.125 to 0.125
- cotangent: bfloat16 [3, 2, 1024, 768], P(None, 'fsdp', 'ctx'), may hold values from -6 to 6
Outputs:
- out: bfloat16 [3, 2, 1024, 768], P(None, 'fsdp', 'ctx')
- x_grad: float32 [3, 2, 1024, 768], P(None, 'fsdp', 'ctx')
- norm1_gain_grad: float32 [768], P('fsdp')
- norm2_gain_grad: float32 [768], P('fsdp')
- bias_table_grad: float32 [32, 12], P('fsdp')
- w_query_grad: float32 [768, 768], P('fsdp')
- w_key_grad: float32 [768, 768], P('fsdp')
- w_value_grad: float32 [768, 768], P('fsdp')
- w_out_grad: float32 [768, 768], P('fsdp')
- w_gate_grad: float32 [768, 2048], P('fsdp')
- w_up_grad: float32 [768, 2048], P('fsdp')
- w_down_grad: float32 [2048, 768], P('fsdp')
Inputs may be any that keep to these rules, and one draw needn't show every extreme that they name: `offsets`: each row along the last dimension is a permutation of 0 to 15.
All inputs are finite; a program needn't handle non-finite values.
Results may differ from a plain program's by a relative error of at most 0.015.
The roundings to bfloat16 on the way count: a program that leaves them out, or rounds other values in their place, can miss the bound.
Values may be sent and summed in bfloat16 or wider, within the bound.
No kernel may reach another device: no remote copies, remote signals or barrier semaphores. Data moves between devices by JAX's collectives and lax.ppermute only.
A program may use at most 192 MiB of HBM per device.

v0:
```python
import functools

import jax
import jax.numpy as jnp
from jax import lax
from jax.experimental import pallas as pl
from jax.experimental.pallas import tpu as pltpu
from jax.sharding import PartitionSpec as P

EPSILON = 1e-06
GROUPS = 4
WIDE = jnp.float32
LOW = jnp.bfloat16
FAR = 91
NEAR_LEAD = 96
VMEM_LIMIT = 60 * 1024 * 1024


def dot(a, b):
    return jnp.dot(a, b, preferred_element_type=WIDE)


def dot_t(a, b):
    return lax.dot_general(a, b, (((1,), (1,)), ((), ())), preferred_element_type=WIDE)


def t_dot(a, b):
    return lax.dot_general(a, b, (((0,), (0,)), ((), ())), preferred_element_type=WIDE)


def bucket_of(relative):
    distance = jnp.abs(relative)
    squared = distance * distance
    counted = jnp.zeros_like(relative)
    for exponent in range(1, 8):
        counted = counted + (squared >= 64 * 2**exponent).astype(jnp.int32)
    within = jnp.where(distance < 8, distance, 8 + counted)
    return jnp.where(relative > 0, 16, 0).astype(jnp.int32) + within


def hop(v, axis, bit):
    size = lax.axis_size(axis)
    return lax.ppermute(v, axis, [(i, i ^ bit) for i in range(size)])


def bits_down(size):
    bit = size // 2
    while bit >= 1:
        yield bit
        bit //= 2


def bits_up(size):
    return reversed(list(bits_down(size)))


def shift(v, steps):
    size = lax.axis_size("ctx")
    stride = size // GROUPS
    return lax.ppermute(v, "ctx", [(i, (i + steps * stride) % size) for i in range(size)])


def slots_out(v, axis, count):
    slots = {0: v}
    for bit in bits_down(count):
        for j in list(slots):
            slots[j ^ bit] = hop(slots[j], axis, bit)
    return [slots[j] for j in range(count)]


def pairs_on(parts, got, count):
    own, evens, _ = parts
    have = {k: evens[k - 1].astype(WIDE) + got[k].astype(WIDE) for k in range(1, count // 2)}
    mine, sent = [(own, False), (got, True)], []
    for bit in bits_up(count // 2):
        for k in sorted(have):
            if k & bit:
                sent.append(have[k].astype(LOW))
                part = hop(sent[-1], "ctx", 2 * bit)
                if k ^ bit:
                    have[k ^ bit] = have[k ^ bit] + part.astype(WIDE)
                else:
                    mine.append((part, False))
                del have[k]
    return mine, sent


def pairs_back(own, evens, odds, count):
    return pairs_on((own, evens, odds), hop(odds, "ctx", 1), count)


def halve(v, axis, unit):
    count = v.shape[0]
    for bit in bits_down(count):
        v = v[:bit] + hop(v[bit:].astype(LOW), axis, bit * unit).astype(WIDE)
    return v[0]


def strip_kernel(blocks, table_ref, strip_ref):
    centre = 64 * (blocks - 1)
    rows = 2 * 64 * blocks
    near = 256
    start = centre - NEAR_LEAD
    chunk = 128
    heads = table_ref.shape[1]

    def relative(first, count):
        u = lax.broadcasted_iota(jnp.int32, (count, 128), 0) + first
        i = lax.broadcasted_iota(jnp.int32, (count, 128), 1)
        return u - centre - jnp.where(i >= 64, i - 64, i)

    for h in range(heads):
        strip_ref[h, : start, :] = jnp.full((start, 128), table_ref[15, h], WIDE)
        strip_ref[h, start + near :, :] = jnp.full((rows - start - near, 128), table_ref[31, h], WIDE)
    for first in range(start, start + near, chunk):
        label = bucket_of(relative(first, chunk))
        for h in range(heads):
            value = jnp.zeros((chunk, 128), WIDE)
            for b in range(32):
                value = jnp.where(label == b, table_ref[b, h], value)
            strip_ref[h, first : first + chunk, :] = value


def make_strip(table_group, blocks):
    heads = table_group.shape[1]
    return pl.pallas_call(
        functools.partial(strip_kernel, blocks),
        out_shape=jax.ShapeDtypeStruct((heads, 2 * 64 * blocks, 128), WIDE),
        in_specs=[pl.BlockSpec(memory_space=pltpu.SMEM)],
        out_specs=pl.BlockSpec(memory_space=pltpu.VMEM),
        compiler_params=pltpu.CompilerParams(vmem_limit_bytes=VMEM_LIMIT),
        name="bias_strip",
    )(table_group)


def split_heads(wide, second_upper):
    lane = lax.broadcasted_iota(jnp.int32, (wide.shape[0], 128), 1)
    low = lane < 64
    zero = jnp.zeros((wide.shape[0], 128), wide.dtype)
    first, second = wide[:, :128], wide[:, 128:]
    third = jnp.where(low, zero, second) if second_upper else jnp.where(low, second, zero)
    return [jnp.where(low, first, zero), jnp.where(low, zero, first), third]


KEY_COLS = (0, 0, 128)
VALUE_COLS = (256, 256, 128)


def sort_blocks(count, m, kplace_ref, kv_refs, sorted_ref):
    for j in range(count):
        for e in range(GROUPS):
            to = pl.multiple_of(kplace_ref[m, j, e] * 64, 64)
            sorted_ref[pl.ds(to, 64), :] = kv_refs[j][e, 0]


def bias_of(strip_ref, h, offs, half, rows, low):
    a = strip_ref[h, pl.ds(offs[2 * half], rows), :]
    b = strip_ref[h, pl.ds(offs[2 * half + 1], rows), :]
    return jnp.where(low, a, b)


def forward_kernel(count, blocks, qplace_ref, kplace_ref, strip_ref, q_ref, *refs):
    kv_refs = refs[:count]
    o_refs = refs[count : count + GROUPS]
    lse_ref, sorted_ref = refs[count + GROUPS :]
    m = pl.program_id(0)
    rows = 64 * blocks
    sort_blocks(count, m, kplace_ref, kv_refs, sorted_ref)
    offs = [pl.multiple_of((blocks - 1 - qplace_ref[m, e]) * 64, 64) for e in range(GROUPS)]
    queries = split_heads(q_ref[:, 0].reshape(GROUPS * 64, 256), False)
    low = lax.broadcasted_iota(jnp.int32, (rows, 128), 1) < 64
    mixed = []
    for h in range(3):
        keys = sorted_ref[:, KEY_COLS[h] : KEY_COLS[h] + 128]
        values = sorted_ref[:, VALUE_COLS[h] : VALUE_COLS[h] + 128]
        scores = dot_t(keys, queries[h])
        parts = []
        for half in range(2):
            s = scores[:, half * 128 : half * 128 + 128] + bias_of(strip_ref, h, offs, half, rows, low)
            top = jnp.max(s, axis=0, keepdims=True)
            e = jnp.exp(s - top)
            total = jnp.sum(e, axis=0, keepdims=True)
            lse_ref[0, h : h + 1, half * 128 : half * 128 + 128] = top + jnp.log(total)
            parts.append((e * (1.0 / total)).astype(LOW))
        weights = jnp.concatenate(parts, axis=1)
        mixed.append(t_dot(values, weights))
    sub = lax.broadcasted_iota(jnp.int32, (128, GROUPS * 64), 0) < 64
    first = jnp.where(sub, mixed[0], mixed[1]).T
    second = jnp.where(sub, 0.0, mixed[2]).T
    out = jnp.concatenate([first, second], axis=1).astype(LOW)
    for d in range(GROUPS):
        o_refs[d][0] = out[d * 64 : d * 64 + 64]


def attention_forward(places, strip, q, kv_slots, blocks):
    qplace, kplace = places
    count = len(kv_slots)
    micro = q.shape[1]
    rows = 64 * blocks
    kv_cols = kv_slots[0].shape[-1]
    by_micro = lambda width: pl.BlockSpec((GROUPS, 1, 64, width), lambda m, *_: (0, m, 0, 0))
    results = pl.pallas_call(
        functools.partial(forward_kernel, count, blocks),
        out_shape=(jax.ShapeDtypeStruct((micro, 64, 256), LOW),) * GROUPS
        + (jax.ShapeDtypeStruct((micro, 3, GROUPS * 64), WIDE),),
        grid_spec=pltpu.PrefetchScalarGridSpec(
            num_scalar_prefetch=2,
            grid=(micro,),
            in_specs=[pl.BlockSpec(strip.shape, lambda m, *_: (0, 0, 0)), by_micro(256)] + [by_micro(kv_cols)] * count,
            out_specs=(pl.BlockSpec((1, 64, 256), lambda m, *_: (m, 0, 0)),) * GROUPS
            + (pl.BlockSpec((1, 3, GROUPS * 64), lambda m, *_: (m, 0, 0)),),
            scratch_shapes=[pltpu.VMEM((rows, kv_cols), LOW)],
        ),
        compiler_params=pltpu.CompilerParams(vmem_limit_bytes=VMEM_LIMIT),
        cost_estimate=pl.CostEstimate(
            flops=micro * 3 * 2 * 2 * rows * GROUPS * 64 * 128 * 2,
            bytes_accessed=micro * rows * kv_cols * 4,
            transcendentals=micro * 3 * rows * GROUPS * 64,
        ),
        name="attention_forward",
    )(qplace, kplace, strip, q, *kv_slots)
    return list(results[:GROUPS]), results[GROUPS]


def backward_kernel(count, blocks, qplace_ref, kplace_ref, place_ref, strip_ref, q_ref, lse_ref, *refs):
    do_refs, refs = refs[:GROUPS], refs[GROUPS:]
    kv_refs = refs[:count]
    dq_ref = refs[count]
    own_ref, even_ref, odd_ref, table_ref = refs[count + 1 : count + 5]
    sorted_ref, grad_ref, lower_ref, upper_ref = refs[count + 5 :]
    m = pl.program_id(0)
    rows = 64 * blocks

    @pl.when(m == 0)
    def _():
        lower_ref[...] = jnp.zeros_like(lower_ref)
        upper_ref[...] = jnp.zeros_like(upper_ref)

    sort_blocks(count, m, kplace_ref, kv_refs, sorted_ref)
    offs = [pl.multiple_of((blocks - 1 - qplace_ref[m, e]) * 64, 64) for e in range(GROUPS)]
    queries = split_heads(q_ref[:, 0].reshape(GROUPS * 64, 256), False)
    grads = split_heads(jnp.concatenate([r[0] for r in do_refs], axis=0), True)
    low = lax.broadcasted_iota(jnp.int32, (rows, 128), 1) < 64
    query_grads, scores_grads, soft = [], [], []
    for h in range(3):
        keys = sorted_ref[:, KEY_COLS[h] : KEY_COLS[h] + 128]
        values = sorted_ref[:, VALUE_COLS[h] : VALUE_COLS[h] + 128]
        scores = dot_t(keys, queries[h])
        weight_grads = dot_t(values, grads[h])
        ds_parts, p_parts = [], []
        for half in range(2):
            cols = slice(half * 128, half * 128 + 128)
            s = scores[:, cols] + bias_of(strip_ref, h, offs, half, rows, low)
            p = jnp.exp(s - lse_ref[0, h : h + 1, cols])
            dp = weight_grads[:, cols]
            delta = jnp.sum(p * dp, axis=0, keepdims=True)
            ds = (p * (dp - delta)).astype(LOW)
            p_parts.append(p.astype(LOW))
            ds_parts.append(ds)
            wide = ds.astype(WIDE)
            at = pl.ds(offs[2 * half], rows)
            lower_ref[h, at, :] += wide
            at = pl.ds(offs[2 * half + 1], rows)
            upper_ref[h, at, :] += wide
        ds_all = jnp.concatenate(ds_parts, axis=1)
        p_all = jnp.concatenate(p_parts, axis=1)
        query_grads.append(t_dot(keys, ds_all))
        scores_grads.append(ds_all)
        soft.append(p_all)
    sub = lax.broadcasted_iota(jnp.int32, (128, GROUPS * 64), 0) < 64
    first = jnp.where(sub, query_grads[0], query_grads[1]).T
    second = jnp.where(sub, query_grads[2], 0.0).T
    dq_ref[:, 0] = jnp.concatenate([first, second], axis=1).astype(LOW).reshape(GROUPS, 64, 256)
    grad_ref[:, 0:128] = dot(scores_grads[0], queries[0]) + dot(scores_grads[1], queries[1])
    grad_ref[:, 128:256] = dot(scores_grads[2], queries[2]) + dot(soft[2], grads[2])
    grad_ref[:, 256:384] = dot(soft[0], grads[0]) + dot(soft[1], grads[1])
    for j in range(count):
        for e in range(GROUPS):
            at = pl.multiple_of(kplace_ref[m, j, e] * 64, 64)
            value = grad_ref[pl.ds(at, 64), :]
            if j == 0:
                own_ref[e, 0] = value
            elif j % 2:
                odd_ref[j // 2, e, 0] = value.astype(LOW)
            else:
                even_ref[j // 2 - 1, e, 0] = value.astype(LOW)

    @pl.when(m == pl.num_programs(0) - 1)
    def _():
        centre = 64 * (blocks - 1)
        start = centre - NEAR_LEAD
        near = 256
        sums_row = lax.broadcasted_iota(jnp.int32, (32, 128), 0)
        side = lax.broadcasted_iota(jnp.int32, (near, 128), 1)
        rel = lax.broadcasted_iota(jnp.int32, (near, 128), 0) + (start - centre) - jnp.where(side >= 64, side - 64, side)
        label = bucket_of(rel)

        def folded(h, first, size):
            lane = lax.broadcasted_iota(jnp.int32, (size, 128), 1) < 64
            return jnp.where(lane, lower_ref[h, first : first + size, :], upper_ref[h, first : first + size, :])

        table = jnp.zeros((32, 128), WIDE)
        for h in range(3):
            before = jnp.sum(folded(h, 0, start), axis=0, keepdims=True)
            last = start + near
            after = jnp.sum(folded(h, last, 2 * rows - last), axis=0, keepdims=True)
            window = folded(h, start, near)
            result = jnp.where(sums_row == 15, before, jnp.where(sums_row == 31, after, 0.0))
            for b in range(32):
                part = jnp.sum(jnp.where(label == b, window, 0.0), axis=0, keepdims=True)
                result = result + jnp.where(sums_row == b, part, 0.0)
            total = jnp.sum(result, axis=1, keepdims=True)
            lanes = lax.broadcasted_iota(jnp.int32, (32, 128), 1)
            table = jnp.where(lanes == place_ref[0] * 3 + h, total, table)
        table_ref[...] = table


def attention_backward(places, place, strip, q, kv_slots, do_slots, lse, blocks):
    qplace, kplace = places
    count = len(kv_slots)
    micro = q.shape[1]
    rows = 64 * blocks
    kv_cols = kv_slots[0].shape[-1]
    by_micro = lambda width: pl.BlockSpec((GROUPS, 1, 64, width), lambda m, *_: (0, m, 0, 0))
    kv_shape = kv_slots[0].shape
    by_part = lambda n: pl.BlockSpec((n, GROUPS, 1, 64, kv_cols), lambda m, *_: (0, 0, m, 0, 0))
    results = pl.pallas_call(
        functools.partial(backward_kernel, count, blocks),
        out_shape=(jax.ShapeDtypeStruct(q.shape, LOW),)
        + (
            jax.ShapeDtypeStruct(kv_shape, WIDE),
            jax.ShapeDtypeStruct((count // 2 - 1,) + kv_shape, LOW),
            jax.ShapeDtypeStruct((count // 2,) + kv_shape, LOW),
        )
        + (jax.ShapeDtypeStruct((32, 128), WIDE),),
        grid_spec=pltpu.PrefetchScalarGridSpec(
            num_scalar_prefetch=3,
            grid=(micro,),
            in_specs=[
                pl.BlockSpec(strip.shape, lambda m, *_: (0, 0, 0)),
                by_micro(256),
                pl.BlockSpec((1, 3, GROUPS * 64), lambda m, *_: (m, 0, 0)),
            ]
            + [pl.BlockSpec((1, 64, 256), lambda m, *_: (m, 0, 0))] * GROUPS
            + [by_micro(kv_cols)] * count,
            out_specs=(by_micro(256),)
            + (by_micro(kv_cols), by_part(count // 2 - 1), by_part(count // 2))
            + (pl.BlockSpec((32, 128), lambda m, *_: (0, 0)),),
            scratch_shapes=[
                pltpu.VMEM((rows, kv_cols), LOW),
                pltpu.VMEM((rows, kv_cols), WIDE),
                pltpu.VMEM((3, 2 * rows, 128), WIDE),
                pltpu.VMEM((3, 2 * rows, 128), WIDE),
            ],
        ),
        compiler_params=pltpu.CompilerParams(vmem_limit_bytes=VMEM_LIMIT),
        cost_estimate=pl.CostEstimate(
            flops=micro * 3 * 5 * 2 * rows * GROUPS * 64 * 128 * 2,
            bytes_accessed=micro * rows * kv_cols * 8,
            transcendentals=micro * 3 * rows * GROUPS * 64,
        ),
        name="attention_backward",
    )(qplace, kplace, place, strip, q, lse, *do_slots, *kv_slots)
    return results[0], results[1:4], results[4]


PLACE = pl.BlockSpec(memory_space=pltpu.SMEM)


def whole(count):
    return [pl.BlockSpec(memory_space=pltpu.VMEM)] * count


def first_entry(v):
    return pl.BlockSpec((1,) + v.shape[1:], lambda _: (0,) * v.ndim)


def call(kernel, name, place, operands, out_shape, scratch=(), flops=0):
    operands = [v if isinstance(v, tuple) else (v, False) for v in operands]
    grid = {"grid": (1,)} if any(first for _, first in operands) else {}
    specs = [PLACE] + [first_entry(v) if first else whole(1)[0] for v, first in operands]
    operands = [v for v, _ in operands]
    size = sum(v.size * v.dtype.itemsize for v in operands) + sum(
        v.size * jnp.dtype(v.dtype).itemsize for v in out_shape
    )
    return pl.pallas_call(
        kernel,
        out_shape=tuple(out_shape),
        **grid,
        in_specs=specs,
        out_specs=tuple(whole(len(out_shape))),
        scratch_shapes=list(scratch),
        compiler_params=pltpu.CompilerParams(vmem_limit_bytes=VMEM_LIMIT),
        cost_estimate=pl.CostEstimate(flops=flops, bytes_accessed=size, transcendentals=0),
        name=name,
    )(place, *operands)


def shaped(*shape, dtype=LOW):
    return jax.ShapeDtypeStruct(shape, dtype)


def place_rows(full_ref, slot_refs, index):
    rows = slot_refs[0].shape[0]
    for j, ref in enumerate(slot_refs):
        full_ref[pl.ds(pl.multiple_of((index ^ j) * rows, rows), rows), :] = ref[...]


def rms_scale(values):
    return lax.rsqrt(jnp.mean(values * values, axis=-1, keepdims=True) + EPSILON)


def norm_back(grad_normed, normed, scale):
    return scale * (grad_normed - normed * jnp.mean(grad_normed * normed, axis=-1, keepdims=True))


def project_kernel(parts_f, place_ref, gain_ref, *refs):
    x_refs, w_refs = refs[:GROUPS], refs[GROUPS : GROUPS + parts_f]
    act_ref, q_ref, kv_ref, full_ref = refs[GROUPS + parts_f :]
    place_rows(full_ref, w_refs, place_ref[2])
    micro, rows, width = x_refs[0].shape
    for d in range(GROUPS):
        x = x_refs[d][...].reshape(micro * rows, width).astype(WIDE)
        act = (x * rms_scale(x) * gain_ref[...]).astype(LOW)
        act_ref[d] = act
        both = dot(act, full_ref[...]).astype(LOW)
        q_ref[d] = both[:, :256].reshape(micro, rows, 256)
        kv_ref[d] = both[:, 256:].reshape(micro, rows, 384)


def project(place, gain, x_slots, w_slots):
    micro, rows, width = x_slots[0].shape
    return call(
        functools.partial(project_kernel, len(w_slots)),
        "project",
        place,
        [gain, *x_slots, *w_slots],
        [
            shaped(GROUPS, micro * rows, width),
            shaped(GROUPS, micro, rows, 256),
            shaped(GROUPS, micro, rows, 384),
        ],
        [pltpu.VMEM((width, 640), LOW)],
        flops=2 * GROUPS * micro * rows * width * 640,
    )


def group_rows(place_ref, d):
    return lax.rem(place_ref[0] + d, GROUPS) * 192


def joined_kernel(parts_f, place_ref, gain_ref, x_ref, *refs):
    o_refs, w_refs = refs[:GROUPS], refs[GROUPS : GROUPS + parts_f]
    resid_ref, act_ref, full_ref = refs[GROUPS + parts_f :]
    place_rows(full_ref, w_refs, place_ref[2])
    micro, rows, width = x_ref.shape
    total = x_ref[...].reshape(micro * rows, width).astype(WIDE)
    for d in range(GROUPS):
        o = o_refs[d][...].reshape(micro * rows, 256)
        at = group_rows(place_ref, d)
        total += dot(o[:, :128], full_ref[pl.ds(pl.multiple_of(at, 64), 128), :])
        total += dot(o[:, 128:], full_ref[pl.ds(pl.multiple_of(at + 64, 64), 128), :])
    resid_ref[...] = total
    act_ref[...] = (total * rms_scale(total) * gain_ref[...]).astype(LOW)


def joined(place, gain, x, o_slots, w_slots):
    micro, rows, width = x.shape
    return call(
        functools.partial(joined_kernel, len(w_slots)),
        "joined",
        place,
        [gain, x, *o_slots, *w_slots],
        [shaped(micro * rows, width, dtype=WIDE), shaped(micro * rows, width)],
        [pltpu.VMEM((width, width), LOW)],
        flops=2 * micro * rows * width * 1024,
    )


GELU_A = 0.7978845608028654
GELU_B = 0.044715


def put_part(refs, j, value):
    own_ref, even_ref, odd_ref = refs
    if j == 0:
        own_ref[...] = value
    elif j % 2:
        odd_ref[j // 2] = value.astype(odd_ref.dtype)
    else:
        even_ref[j // 2 - 1] = value.astype(even_ref.dtype)


def part_shapes(shape, fast):
    return [
        shaped(*shape, dtype=WIDE),
        shaped(fast // 2 - 1, *shape),
        shaped(fast // 2, *shape),
    ]


def feed_kernel(parts_f, fast, place_ref, *refs):
    act_refs, refs = refs[:fast], refs[fast:]
    g_refs, refs = refs[:fast], refs[fast:]
    pair_refs, refs = refs[:parts_f], refs[parts_f:]
    down_refs, refs = refs[:parts_f], refs[parts_f:]
    two_refs, out_refs, refs = refs[:3], refs[3:6], refs[6:]
    hid_ref, grad_ref, pair_ref, down_ref = refs
    place_rows(pair_ref, pair_refs, place_ref[2])
    place_rows(down_ref, down_refs, place_ref[2])
    cols = hid_ref.shape[-1]
    for j in range(fast):
        both = dot(act_refs[j][...], pair_ref[...])
        z, up = both[:, :cols], both[:, cols:]
        square = z * z
        t = jnp.tanh(GELU_A * (z + GELU_B * square * z))
        half = 0.5 * (1.0 + t)
        gelu = z * half
        slope = half + (0.5 * z) * (1.0 - t * t) * (GELU_A * (1.0 + 3.0 * GELU_B * square))
        hid = (gelu * up).astype(LOW)
        dh = dot_t(g_refs[j][...], down_ref[...])
        grads = jnp.concatenate([(dh * up * slope).astype(LOW), (dh * gelu).astype(LOW)], axis=1)
        hid_ref[j] = hid
        grad_ref[j] = grads
        put_part(two_refs, j, dot_t(grads, pair_ref[...]))
        put_part(out_refs, j, dot(hid, down_ref[...]))


def feed(place, act_slots, g_slots, pair_slots, down_slots):
    fast, parts_f = len(act_slots), len(pair_slots)
    rows, width = act_slots[0].shape
    cols = down_slots[0].shape[0] * parts_f
    results = call(
        functools.partial(feed_kernel, parts_f, fast),
        "feed",
        place,
        [*act_slots, *g_slots, *pair_slots, *down_slots],
        part_shapes((rows, width), fast) * 2 + [shaped(fast, rows, cols), shaped(fast, rows, 2 * cols)],
        [pltpu.VMEM((width, 2 * cols), LOW), pltpu.VMEM((cols, width), LOW)],
        flops=2 * fast * rows * width * cols * 6,
    )
    return results[:3], results[3:6], results[-2], results[-1]


def packing(piece, rows):
    if rows == 3 * piece:
        return [(0, k * 256, k * piece, 0, piece, 256) for k in range(3)]
    half = piece // 2
    return [
        (0, 0, 0, 0, piece, 512),
        (0, 512, piece, 0, half, 256),
        (half, 512, piece, 256, half, 256),
    ]


def pair_grads_kernel(fast, place_ref, *refs):
    act_refs, grad_ref, refs = refs[:fast], refs[fast], refs[fast + 1 :]
    outs, full_ref = refs[:-1], refs[-1]
    act = jnp.concatenate([r[...] for r in act_refs], axis=0)
    full_ref[...] = t_dot(act, grad_ref[...].reshape(act.shape[0], -1))
    rows = outs[0].shape[0]
    for j, out in enumerate(outs):
        at = pl.multiple_of((place_ref[2] ^ j) * rows, rows)
        out[...] = full_ref[pl.ds(at, rows), :].astype(out.dtype)


def pair_grads(place, act_slots, grads, parts_f):
    fast, rows, double = grads.shape
    width = act_slots[0].shape[1]
    types = [WIDE] + [LOW] * (parts_f - 1)
    return call(
        functools.partial(pair_grads_kernel, fast),
        "pair_grads",
        place,
        [*act_slots, grads],
        [shaped(width // parts_f, double, dtype=t) for t in types],
        [pltpu.VMEM((width, double), WIDE)],
        flops=2 * fast * rows * width * double,
    )


def down_grads_kernel(fast, place_ref, *refs):
    g_refs, hid_ref, refs = refs[:fast], refs[fast], refs[fast + 1 :]
    outs, full_ref = refs[:-1], refs[-1]
    g = jnp.concatenate([r[...] for r in g_refs], axis=0)
    full_ref[...] = t_dot(hid_ref[...].reshape(g.shape[0], -1), g)
    rows = outs[0].shape[0]
    piece = full_ref.shape[0] // len(outs)
    for j, out in enumerate(outs):
        for r, c, to_r, to_c, n, w in packing(piece, rows):
            at = pl.multiple_of((place_ref[2] ^ j) * piece + r, 8)
            out[to_r : to_r + n, to_c : to_c + w] = full_ref[pl.ds(at, n), c : c + w].astype(out.dtype)


def down_grads(place, g_slots, hid, parts_f):
    fast, rows, cols = hid.shape
    width = g_slots[0].shape[1]
    types = [WIDE] + [LOW] * (parts_f - 1)
    return call(
        functools.partial(down_grads_kernel, fast),
        "down_grads",
        place,
        [*g_slots, hid],
        [shaped(width // parts_f, cols, dtype=t) for t in types],
        [pltpu.VMEM((cols, width), WIDE)],
        flops=2 * fast * rows * width * cols,
    )


def group_split_kernel(count, place_ref, *refs):
    own_ref, send_refs = refs[count], refs[count + 1 :]
    rows = own_ref.shape[0]

    def part(d):
        at = pl.ds(pl.multiple_of(lax.rem(place_ref[0] + d, GROUPS) * rows, 8), rows)
        return sum(r[at, :].astype(WIDE) for r in refs[:count])

    own_ref[...] = part(0)
    for d, ref in enumerate(send_refs, 1):
        ref[...] = part(d).astype(ref.dtype)


def group_split(place, parts):
    rows, cols = parts[0].shape
    cut = rows // GROUPS
    results = call(
        functools.partial(group_split_kernel, len(parts)),
        "group_split",
        place,
        parts,
        [shaped(cut, cols, dtype=WIDE)] + [shaped(cut, cols)] * (GROUPS - 1),
    )
    return results[0], list(results[1:])


def group_halves_kernel(count, place_ref, *refs):
    keep_ref, send_ref = refs[count:]
    rows = keep_ref.shape[1]
    for d in range(GROUPS):
        at = pl.ds(pl.multiple_of((place_ref[0] ^ d) * rows, 8), rows)
        total = sum(r[at, :].astype(WIDE) for r in refs[:count])
        if d % 2:
            send_ref[d // 2] = total.astype(send_ref.dtype)
        else:
            keep_ref[d // 2] = total


def group_halves(place, parts):
    rows, cols = parts[0].shape
    cut = (GROUPS // 2, rows // GROUPS, cols)
    return call(
        functools.partial(group_halves_kernel, len(parts)),
        "group_halves",
        place,
        parts,
        [shaped(*cut, dtype=WIDE), shaped(*cut)],
    )


def summed(refs):
    return sum((r[0] if len(r.shape) == 3 else r[...]).astype(WIDE) for r in refs)


def branch_kernel(parts_f, count, place_ref, gain_ref, resid_ref, g_ref, *refs):
    two_refs, refs = refs[:count], refs[count:]
    w_refs, refs = refs[:parts_f], refs[parts_f:]
    grad_ref, low_ref, gain_out = refs[:3]
    do_refs, full_ref = refs[3 : 3 + GROUPS], refs[3 + GROUPS]
    place_rows(full_ref, w_refs, place_ref[2])
    micro, rows, _ = do_refs[0].shape
    grad_two = summed(two_refs)
    resid = resid_ref[...]
    scale = rms_scale(resid)
    normed = resid * scale
    gain_out[...] = jnp.sum(grad_two * normed, axis=0, keepdims=True)
    grad = g_ref[...].astype(WIDE) + norm_back(grad_two * gain_ref[...], normed, scale)
    grad_ref[...] = grad
    low = grad.astype(LOW)
    low_ref[...] = low
    for d in range(GROUPS):
        at = group_rows(place_ref, d)
        first = dot_t(low, full_ref[pl.ds(pl.multiple_of(at, 64), 128), :])
        second = dot_t(low, full_ref[pl.ds(pl.multiple_of(at + 64, 64), 128), :])
        both = jnp.concatenate([first, second], axis=1).astype(LOW)
        do_refs[d][...] = both.reshape(micro, rows, 256)


def branch(place, gain, resid, g, two_list, w_slots, micro):
    rows, width = resid.shape
    results = call(
        functools.partial(branch_kernel, len(w_slots), len(two_list)),
        "branch",
        place,
        [gain, resid, g, *two_list, *w_slots],
        [shaped(rows, width, dtype=WIDE), shaped(rows, width), shaped(1, width, dtype=WIDE)]
        + [shaped(micro, rows // micro, 256)] * GROUPS,
        [pltpu.VMEM((width, width), LOW)],
        flops=2 * rows * width * 1024,
    )
    return results[0], results[1], results[2], list(results[3:])


def with_rows(index, rows, count, action):
    if rows % 8 == 0:
        action(pl.ds(pl.multiple_of(index * rows, 8), rows))
        return
    for known in range(count):

        @pl.when(index == known)
        def _():
            action(slice(known * rows, known * rows + rows))


def write_chunks(place_ref, full_ref, keep_ref, send_ref):
    parts_f, halves, rows, _ = keep_ref.shape
    for i in range(parts_f):
        for k in range(halves):
            for odd, ref in ((0, keep_ref), (1, send_ref)):
                index = (place_ref[2] ^ i) * (2 * halves) + (place_ref[1] ^ (2 * k + odd))

                def copy(at):
                    ref[i, k] = full_ref[at, :].astype(ref.dtype)

                with_rows(index, rows, 2 * halves * parts_f, copy)


def out_grads_kernel(place_ref, low_ref, *refs):
    o_refs = refs[:GROUPS]
    keep_ref, send_ref, full_ref = refs[GROUPS:]
    micro, rows, _ = o_refs[0].shape
    low = low_ref[...]
    for d in range(GROUPS):
        both = t_dot(o_refs[d][...].reshape(micro * rows, 256), low)
        at = group_rows(place_ref, d)
        full_ref[pl.ds(pl.multiple_of(at, 64), 128), :] = both[:128]
        full_ref[pl.ds(pl.multiple_of(at + 128, 64), 64), :] = both[192:]
    write_chunks(place_ref, full_ref, keep_ref, send_ref)


def out_grads(place, low, o_slots, parts_f, fast):
    rows, width = low.shape
    chunk = (parts_f, fast // 2, width // (parts_f * fast), width)
    return call(
        out_grads_kernel,
        "out_grads",
        place,
        [low, *o_slots],
        [shaped(*chunk, dtype=WIDE), shaped(*chunk)],
        [pltpu.VMEM((width, width), WIDE)],
        flops=2 * rows * width * 1024,
    )


def input_grads_kernel(parts_f, count, place_ref, act_ref, dq_ref, *refs):
    x_refs, refs = refs[:GROUPS], refs[GROUPS:]
    dkv_refs, refs = refs[:count], refs[count:]
    w_refs, refs = refs[:parts_f], refs[parts_f:]
    one_keep, one_send, gain_out, keep_ref, send_ref, full_ref, sums_ref, both_ref, one_ref = refs
    place_rows(full_ref, w_refs, place_ref[2])
    groups, rows, width = act_ref.shape
    micro = dq_ref.shape[1]
    gain_total = jnp.zeros((1, width), WIDE)
    for d in range(GROUPS):
        dkv = sum((r[0, d] if len(r.shape) == 5 else r[d]).astype(WIDE) for r in dkv_refs)
        dkv = dkv.astype(LOW).reshape(rows, 384)
        both = jnp.concatenate([dq_ref[d].reshape(rows, 256), dkv], axis=1)
        both_ref[d] = both
        one = dot_t(both, full_ref[...])
        x = x_refs[d][...].reshape(rows, width).astype(WIDE)
        gain_total = gain_total + jnp.sum(one * (x * rms_scale(x)), axis=0, keepdims=True)
        one_ref[lax.rem(place_ref[0] + GROUPS - d, GROUPS)] = one
    for d in range(GROUPS):
        value = one_ref[place_ref[0] ^ d]
        if d % 2:
            one_send[d // 2] = value.astype(LOW)
        else:
            one_keep[d // 2] = value
    gain_out[...] = gain_total
    sums_ref[...] = t_dot(act_ref[...].reshape(groups * rows, width), both_ref[...].reshape(groups * rows, 640))
    write_chunks(place_ref, sums_ref, keep_ref, send_ref)


def input_grads(place, act, dq, x_slots, dkv_list, w_slots, fast):
    groups, rows, width = act.shape
    micro = dq.shape[1]
    parts_f = len(w_slots)
    chunk = (parts_f, fast // 2, width // (parts_f * fast), 640)
    return call(
        functools.partial(input_grads_kernel, parts_f, len(dkv_list)),
        "input_grads",
        place,
        [act, dq, *x_slots, *dkv_list, *w_slots],
        [shaped(GROUPS // 2, rows, width, dtype=WIDE), shaped(GROUPS // 2, rows, width)]
        + [shaped(1, width, dtype=WIDE), shaped(*chunk, dtype=WIDE), shaped(*chunk)],
        [
            pltpu.VMEM((width, 640), LOW),
            pltpu.VMEM((width, 640), WIDE),
            pltpu.VMEM((groups, rows, 640), LOW),
            pltpu.VMEM((groups, rows, width), WIDE),
        ],
        flops=4 * groups * rows * width * 640,
    )


def last_kernel(count, place_ref, gain_ref, x_ref, grad_ref, resid_ref, *refs):
    one_ref, got_ref, refs = refs[0], refs[1], refs[2:]
    out_refs, refs = refs[:count], refs[count:]
    x_grad_ref, out_ref = refs
    micro, rows, width = x_ref.shape
    grad_one = one_ref[...] + got_ref[...].astype(WIDE)
    x = x_ref[...].reshape(micro * rows, width).astype(WIDE)
    scale = rms_scale(x)
    normed = x * scale
    x_grad_ref[...] = grad_ref[...] + norm_back(grad_one * gain_ref[...], normed, scale)
    out_ref[...] = (resid_ref[...] + summed(out_refs)).astype(LOW)


def last(place, gain, x, grad, resid, one, one_got, out_list):
    rows, width = resid.shape
    return call(
        functools.partial(last_kernel, len(out_list)),
        "last",
        place,
        [gain, x, grad, resid, one, one_got, *out_list],
        [shaped(rows, width, dtype=WIDE), shaped(rows, width)],
    )


LOW_ORDER = (0, 2, 1, 3)


def feed_finish_kernel(parts_f, fast, place_ref, *refs):
    pair_refs, low_refs = refs[:fast], refs[fast : 2 * fast]
    gate_ref, up_ref, down_ref, pack_ref = refs[2 * fast :]
    _, rows, double = pair_refs[0].shape
    cols = double // 2
    piece = cols // parts_f
    for j in range(fast):
        other = place_ref[1] ^ j
        for d in range(GROUPS):
            at = pl.ds(pl.multiple_of(lax.rem(place_ref[0] + GROUPS - d, GROUPS) * rows, 8), rows)
            for start, ref in ((0, gate_ref), (cols, up_ref)):
                for k in range(parts_f):
                    value = pair_refs[j][d, :, start + k * piece : start + (k + 1) * piece].astype(WIDE)
                    if piece % 128 == 0:
                        to = pl.multiple_of(k * fast * piece + other * piece, 128)
                        ref[at, pl.ds(to, piece)] = value
                    else:
                        for l in range(fast):

                            @pl.when(other == l)
                            def _():
                                ref[at, (k * fast + l) * piece : (k * fast + l + 1) * piece] = value

            at = pl.ds(pl.multiple_of((place_ref[0] ^ LOW_ORDER[d]) * rows, 8), rows)
            pack_ref[at, :] = low_refs[j][d].astype(WIDE)
        for r, c, to_r, to_c, n, w in packing(piece, rows * GROUPS):
            at = pl.ds(pl.multiple_of(other * piece + r, 8), n)
            down_ref[at, c : c + w] = pack_ref[to_r : to_r + n, to_c : to_c + w]


def feed_finish(place, pair_packs, low_packs, parts_f):
    fast = len(pair_packs)
    _, rows, double = pair_packs[0].shape
    cols = double // 2
    piece = cols // parts_f
    return call(
        functools.partial(feed_finish_kernel, parts_f, fast),
        "feed_finish",
        place,
        [*pair_packs, *low_packs],
        [
            shaped(rows * GROUPS, cols * fast, dtype=WIDE),
            shaped(rows * GROUPS, cols * fast, dtype=WIDE),
            shaped(piece * fast, rows * GROUPS * parts_f, dtype=WIDE),
        ],
        [pltpu.VMEM((rows * GROUPS, cols), WIDE)],
    )


def input_finish_kernel(fast, place_ref, *refs):
    pack_refs, out_refs = refs[:fast], refs[fast : 2 * fast]
    query_ref, key_ref, value_ref, out_ref = refs[2 * fast :]
    rows = pack_refs[0].shape[0]
    for j in range(fast):
        value = out_refs[j][...].astype(WIDE)

        def place_out(at):
            out_ref[at, :] = value

        with_rows(place_ref[1] ^ j, rows, fast, place_out)
    for h in range(GROUPS):

        @pl.when(place_ref[0] == h)
        def _():
            for j in range(fast):
                starts = [(h - g) % GROUPS * 640 for g in range(GROUPS)]
                part = lambda a, b: pack_refs[j][:, a:b].astype(WIDE)
                query = jnp.concatenate([part(s, s + 192) for s in starts], axis=1)
                key = jnp.concatenate([part(s + 256, s + 448) for s in starts], axis=1)
                value = jnp.concatenate([p for s in starts for p in (part(s + 512, s + 640), part(s + 448, s + 512))], axis=1)

                def place_in(at):
                    query_ref[at, :] = query
                    key_ref[at, :] = key
                    value_ref[at, :] = value

                with_rows(place_ref[1] ^ j, rows, fast, place_in)


def input_finish(place, packs, out_all, width):
    fast = len(packs)
    return call(
        functools.partial(input_finish_kernel, fast),
        "input_finish",
        place,
        [*packs, *out_all],
        [shaped(packs[0].shape[0] * fast, width, dtype=WIDE)] * 4,
    )


def spread_groups(v):
    return [v] + [shift(v, d) for d in range(1, GROUPS)]


def gather_pack(pack, fast):
    slots = {0: pack}
    for bit in bits_down(fast):
        for j in list(slots):
            slots[j ^ bit] = hop(slots[j], "ctx", bit)
    return [slots[j] for j in range(fast)]


def after(value, *others):
    return lax.optimization_barrier((value, *others))[0]


def body(
    tokens,
    offsets,
    norm1_gain,
    norm2_gain,
    bias_table,
    w_query,
    w_key,
    w_value,
    w_out,
    w_gate,
    w_up,
    w_down,
    cotangent,
):
    micro, _, block_rows, width = tokens.shape
    blocks = lax.axis_size("ctx")
    parts_f = lax.axis_size("fsdp")
    fast = blocks // GROUPS
    ctx = lax.axis_index("ctx")
    f = lax.axis_index("fsdp")
    hi, lo = ctx // fast, ctx % fast
    group_cols = w_query.shape[1] // GROUPS
    own_rows = micro * block_rows
    hidden = w_gate.shape[1]
    piece = hidden // (parts_f * fast)
    part_rows = w_query.shape[0]
    gain_one = norm1_gain.reshape(1, width)
    gain_two = norm2_gain.reshape(1, width)
    place = jnp.stack([hi, lo, f]).astype(jnp.int32)

    own_x = tokens[:, 0]
    g_low = cotangent[:, 0].reshape(own_rows, width)
    x_slots = spread_groups(own_x)

    def group_of(matrix):
        return lax.dynamic_slice_in_dim(matrix, hi * group_cols, group_cols, axis=1)

    q_part, k_part, v_part = group_of(w_query), group_of(w_key), group_of(w_value)
    gap = jnp.zeros((part_rows, 64), LOW)
    qkv_part = jnp.concatenate([q_part, gap, k_part, v_part[:, 128:], v_part[:, :128]], axis=1)
    qkv_slots = slots_out(qkv_part, "fsdp", parts_f)

    def pieces(matrix):
        return [
            lax.dynamic_slice_in_dim(matrix, (k * fast + lo) * piece, piece, axis=1) for k in range(parts_f)
        ]

    pair_part = jnp.concatenate(pieces(w_gate) + pieces(w_up), axis=1)
    down_part = lax.dynamic_slice_in_dim(w_down, lo * piece, piece, axis=0)

    starts = offsets[:, 0]
    group_ids = (hi + GROUPS - jnp.arange(GROUPS, dtype=jnp.int32)) % GROUPS
    slot_ids = lo ^ jnp.arange(fast, dtype=jnp.int32)
    kplace = jnp.take(starts, group_ids[None, :] * fast + slot_ids[:, None], axis=1)
    table_group = lax.dynamic_slice_in_dim(bias_table, hi * 3, 3, axis=1)
    strip = make_strip(table_group, blocks)

    tick = [place]

    def fence(*values):
        tick[0], *values = lax.optimization_barrier((tick[0], *values))
        return values[0] if len(values) == 1 else values

    def shifted(parts, sign):
        return [shift(v, sign * d) for d, v in enumerate(parts, 1)]

    def to_f(parts):
        return [hop(v, "fsdp", j) for j, v in enumerate(parts, 1)]

    def groups_sum(own, parts):
        return (own + sum(v.astype(WIDE) for v in parts)).astype(LOW)

    def far_places(v):
        have = {0: v}
        for bit in bits_down(fast // 2):
            for j in list(have):
                have[j ^ (2 * bit)] = hop(have[j], "ctx", 2 * bit)
        return have

    def both_cores(have):
        return [v for j in range(0, fast, 2) for v in (have[j], hop(have[j], "ctx", 1))]

    strip, kplace = fence(strip, kplace)
    places = (kplace[:, 0], kplace)
    out_w, pair_w, x_slots, qkv_slots = fence(w_out, pair_part, x_slots, qkv_slots)
    act_one, q, kv = project(tick[0], gain_one, x_slots, qkv_slots)
    kv_slots = slots_out(kv, "ctx", fast)
    out_w_slots = slots_out(out_w, "fsdp", parts_f)
    pair_slots = slots_out(pair_w, "fsdp", parts_f)
    g_low, kv_slots = fence(g_low, kv_slots)
    g_have = {0: g_low, 1: hop(g_low, "ctx", 1)}
    for bit in bits_down(fast // 2):
        for j in [j for j in g_have if j % 2 == 0]:
            g_have[j ^ (2 * bit)] = hop(g_have[j], "ctx", 2 * bit)
    o_group, lse = attention_forward(places, strip, q, kv_slots, blocks)
    o_group, g_have, out_w_slots, down_w = fence(o_group, g_have, out_w_slots, down_part)
    o_slots = [o_group[0]] + shifted(o_group[1:], -1)
    down_slots = slots_out(down_w, "fsdp", parts_f)
    for j in range(2, fast, 2):
        g_have[j + 1] = hop(g_have[j], "ctx", 1)
    g_slots = [g_have[j] for j in range(fast)]
    resid, act_two = joined(tick[0], gain_two, own_x, o_slots, out_w_slots)
    act_two, g_slots = fence(act_two, g_slots)
    act_slots = slots_out(act_two, "ctx", fast)
    two_parts, out_parts, hid, grads = feed(tick[0], act_slots, g_slots, pair_slots, down_slots)
    two_parts, out_parts = fence(two_parts, out_parts)

    two_odd = two_parts[2]
    two_got = hop(two_odd, "ctx", 1)
    pair_keep, *pair_sends = pair_grads(tick[0], act_slots, grads, parts_f)
    two_got, pair_keep, pair_sends = fence(two_got, pair_keep, pair_sends)
    pair_got = to_f(pair_sends)
    two_list, sent = pairs_on(two_parts, two_got, fast)
    low_keep, *low_sends = down_grads(fence(tick[0], sent)[0], g_slots, hid, parts_f)
    got, low_keep, low_sends = fence([v for v, _ in two_list], low_keep, low_sends)
    two_list = [(v, first) for v, (_, first) in zip(got, two_list)]
    grad_resid, grad_low, gain_two_part, do_own = branch(
        tick[0], gain_two, resid, g_low, two_list, out_w_slots, micro
    )
    do_own = fence(*do_own)
    do_slots = [do_own[0]] + shifted(do_own[1:], 1)
    out_keep, out_send = out_grads(tick[0], grad_low, o_slots, parts_f, fast)
    out_send, pair_got = fence(out_send, pair_got)
    pair_own, pair_sends = group_split(tick[0], [pair_keep, *pair_got])
    pair_own, pair_sends, low_sends, do_slots = fence(pair_own, pair_sends, low_sends, do_slots)

    pair_parts = shifted(pair_sends, 1)
    low_got = to_f(low_sends)
    out_got = hop(out_send, "ctx", 1)
    dq, dkv_parts, table_part = attention_backward(
        places, tick[0], strip, q, kv_slots, do_slots, lse, blocks
    )
    dq, dkv_parts, pair_parts, low_got, out_got = fence(dq, dkv_parts, pair_parts, low_got, out_got)
    dkv_list, sent = pairs_on(dkv_parts, hop(dkv_parts[2], "ctx", 1), fast)
    pair_chunk, out_chunk, _ = fence(groups_sum(pair_own, pair_parts), out_keep + out_got.astype(WIDE), sent)
    pair_spread = spread_groups(pair_chunk)
    out_chunk = halve(out_chunk, "fsdp", 1)
    low_keep, low_send = group_halves(tick[0], [low_keep, *low_got])
    got, pair_spread, out_chunk, low_send = fence([v for v, _ in dkv_list], pair_spread, out_chunk, low_send)
    dkv_list = [(v, first) for v, (_, first) in zip(got, dkv_list)]

    low_got = hop(low_send, "ctx", fast)
    out_chunk = halve(out_chunk, "ctx", 2)
    one_keep, one_send, gain_one_part, in_keep, in_send = input_grads(
        tick[0], act_one, dq, x_slots, dkv_list, qkv_slots, fast
    )
    one_keep, one_send, in_keep, in_send, low_got, out_chunk = fence(
        one_keep, one_send, in_keep, in_send, low_got, out_chunk
    )
    in_got = hop(in_send, "ctx", 1)
    pair_have = far_places(jnp.stack(pair_spread))
    one_got = hop(one_send, "ctx", fast)
    in_total = fence(in_keep + in_got.astype(WIDE))
    low_sum = low_keep + low_got.astype(WIDE)
    low_got = hop(low_sum[1].astype(LOW), "ctx", 2 * fast)
    in_total, low_got = fence(halve(in_total, "fsdp", 1), low_got)
    low_two = (low_sum[0] + low_got.astype(WIDE)).astype(LOW)
    low_two = jnp.stack([low_two, hop(low_two, "ctx", 2 * fast)])
    in_chunk, pair_have, one_got, low_two = fence(
        halve(in_total, "ctx", 2).astype(LOW), pair_have, one_got, low_two
    )
    in_spread = spread_groups(in_chunk)
    low_got = hop(low_two, "ctx", fast)
    small = jnp.concatenate([gain_one_part.reshape(-1, 128), gain_two_part.reshape(-1, 128), table_part], axis=0)
    for bit in bits_up(parts_f):
        small = small + hop(small, "fsdp", bit)
    small = small + hop(small, "ctx", 1)
    in_pack, low_pack, small, one_sum, out_low, out_parts = fence(
        jnp.concatenate(in_spread, axis=1),
        jnp.concatenate([low_two, low_got]),
        small,
        one_keep + one_got.astype(WIDE),
        out_chunk.astype(LOW),
        out_parts,
    )
    in_have = far_places(in_pack)
    out_got = hop(out_low, "ctx", fast)
    small = small + hop(small, "ctx", fast)
    low_have = far_places(low_pack)
    out_low, small, one_send = fence(
        (out_low.astype(WIDE) + out_got.astype(WIDE)).astype(LOW), small, one_sum[1].astype(LOW)
    )
    out_got = hop(out_low, "ctx", 2 * fast)
    small = small + hop(small, "ctx", 2 * fast)
    one_got = hop(one_send, "ctx", 2 * fast)
    pair_packs = both_cores(pair_have)
    out_chunk, small, in_have, low_have, pair_packs = fence(
        (out_low.astype(WIDE) + out_got.astype(WIDE)).astype(LOW), small, in_have, low_have, pair_packs
    )
    low_packs = both_cores(low_have)
    in_packs = both_cores(in_have)
    out_have = far_places(out_chunk)
    for bit in bits_down(fast // 2):
        small = small + hop(small, "ctx", 2 * bit)
    w_gate_grad, w_up_grad, w_down_grad = feed_finish(tick[0], pair_packs, low_packs, parts_f)
    w_gate_grad, in_packs, out_have, small, one_got = fence(w_gate_grad, in_packs, out_have, small, one_got)
    out_all = both_cores(out_have)
    out_list, _ = pairs_back(*out_parts, fast)
    x_grad, result = last(tick[0], gain_one, own_x, grad_resid, resid, one_sum[0], one_got, out_list)
    x_grad, out_all = fence(x_grad, out_all)
    w_query_grad, w_key_grad, w_value_grad, w_out_grad = input_finish(tick[0], in_packs, out_all, width)
    head_count = bias_table.shape[1]

    lines = width // 128
    gain_rows = width // parts_f
    table_rows = bias_table.shape[0] // parts_f
    gain_one_grad = lax.dynamic_slice_in_dim(small[:lines].reshape(width), f * gain_rows, gain_rows)
    gain_two_grad = lax.dynamic_slice_in_dim(small[lines : 2 * lines].reshape(width), f * gain_rows, gain_rows)
    table_grad = lax.dynamic_slice(small, (2 * lines + f * table_rows, 0), (table_rows, head_count))

    return (
        result.reshape(micro, 1, block_rows, width),
        x_grad.reshape(micro, 1, block_rows, width),
        gain_one_grad,
        gain_two_grad,
        table_grad,
        w_query_grad,
        w_key_grad,
        w_value_grad,
        w_out_grad,
        w_gate_grad,
        w_up_grad,
        w_down_grad,
    )


def solution(mesh):
    in_specs = (
        P(None, "fsdp", "ctx", None),
        P(None, "fsdp", None),
        P(),
        P(),
        P(),
        P("fsdp", None),
        P("fsdp", None),
        P("fsdp", None),
        P("fsdp", None),
        P("fsdp", None),
        P("fsdp", None),
        P("fsdp", None),
        P(None, "fsdp", "ctx", None),
    )
    out_specs = (
        P(None, "fsdp", "ctx", None),
        P(None, "fsdp", "ctx", None),
        P("fsdp"),
        P("fsdp"),
        P("fsdp", None),
        P("fsdp", None),
        P("fsdp", None),
        P("fsdp", None),
        P("fsdp", None),
        P("fsdp", None),
        P("fsdp", None),
        P("fsdp", None),
    )
    return jax.shard_map(body, mesh=mesh, in_specs=in_specs, out_specs=out_specs, check_vma=False)
```

profile of v0, /device:TPU:0, one launch (start us, length us, event | category | flops | bytes accessed | tf_op | source)
XLA Modules:
  0.0 293.4 jit_solution(5822899861954866234)
XLA Ops:
  15.9 3.9 %bias_strip.1.strip_ref = f32[3,2048,128]{2,1,0:T(8,128)} custom-call(f32[32,3]{1,0:T(8,128)} %copy.33.table_ref), custom_call_target="tpu_custom_call" | custom-call | tf_op jit(solution)/shard_map/bias_strip/pallas_call | solution.py:126
  25.9 3.8 %project.1 = (bf16[4,192,768]{2,1,0:T(8,128)(2,1)}, bf16[4,3,64,256]{3,2,1,0:T(8,128)(2,1)}, bf16[4,3,64,384]{3,2,1,0:T(8,128)(2,1)}) custom-call(s32[3]{0:T(128)} %pad_add_fusion.place_ref, f32[1,768]{1,0:T(1,128)} %reshape.156.gain_ref, bf16[3,64,768]{2,1,0:T(8,128)(2,1)} %bitcast.61, bf16[3,64,768]{2,1,0:T(8,128)(2,1)} %copy-done.33, ...), custom_call_target="tpu_custom_call" | custom-call | flops 754974720 | bytes 4328448 | tf_op jit(solution)/shard_map/project/pallas_call | solution.py:386
  31.2 13.9 %collective-permute-done.5.refs_2_.refs_6_ = bf16[4,3,64,384]{3,2,1,0:T(8,128)(2,1)} collective-permute-done((bf16[4,3,64,384]{3,2,1,0:T(8,128)(2,1)}, bf16[4,3,64,384]{3,2,1,0:T(8,128)(2,1)}, u32[]{:S(2)}, u32[]{:S(2)}) %collective-permute-start.5) | collective-permute-done | bytes 589856 | tf_op jit(solution)/shard_map/ppermute | solution.py:43
  49.2 11.9 %attention_forward.1 = (bf16[3,64,256]{2,1,0:T(8,128)(2,1)}, bf16[3,64,256]{2,1,0:T(8,128)(2,1)}, bf16[3,64,256]{2,1,0:T(8,128)(2,1)}, bf16[3,64,256]{2,1,0:T(8,128)(2,1)}, f32[3,3,256]{2,1,0:T(4,128)}) custom-call(s32[3,4]{1,0:T(4,128)} %bitcast.82, s32[3,4,4]{2,1,0:T(4,128)} %copy-done.50, f32[3,2048,128]{2,1,0:T(8,128)} %bias_strip.1.strip_ref, ...), custom_call_target="tpu_custom_call" | custom-call | flops 2415919104 | bytes 4718592 | tf_op jit(solution)/shard_map/attention_forward/pallas_call | solution.py:202
  62.8 6.8 %collective-permute-start.10 = (bf16[3,64,256]{2,1,0:T(8,128)(2,1)}, bf16[3,64,256]{2,1,0:T(8,128)(2,1)S(1)}, u32[]{:S(2)}, u32[]{:S(2)}) collective-permute-start(bf16[3,64,256]{2,1,0:T(8,128)(2,1)} %get-tuple-element.246), channel_id=1, source_target_pairs={{0,24},{2,26},{4,28},{6,30},{8,0},{10,2},{12,4},{14,6},{16,8},{18,... | collective-permute-start | bytes 294920 | tf_op jit(solution)/shard_map/ppermute | solution.py:60
  73.2 7.3 %collective-permute-done.11.refs_2_ = bf16[3,64,256]{2,1,0:T(8,128)(2,1)S(1)} collective-permute-done((bf16[3,64,256]{2,1,0:T(8,128)(2,1)}, bf16[3,64,256]{2,1,0:T(8,128)(2,1)S(1)}, u32[]{:S(2)}, u32[]{:S(2)}) %collective-permute-start.11) | collective-permute-done | bytes 98336 | tf_op jit(solution)/shard_map/ppermute | solution.py:60
  87.0 6.7 %collective-permute-done.15.refs_2_ = bf16[192,768]{1,0:T(8,128)(2,1)S(1)} collective-permute-done((bf16[192,768]{1,0:T(8,128)(2,1)}, bf16[192,768]{1,0:T(8,128)(2,1)S(1)}, u32[]{:S(2)}, u32[]{:S(2)}) %collective-permute-start.15) | collective-permute-done | bytes 294944 | tf_op jit(solution)/shard_map/ppermute | solution.py:43
  98.1 9.4 %feed.1 = (f32[192,768]{1,0:T(8,128)}, bf16[1,192,768]{2,1,0:T(8,128)(2,1)}, bf16[2,192,768]{2,1,0:T(8,128)(2,1)}, f32[192,768]{1,0:T(8,128)}, bf16[1,192,768]{2...) custom-call(s32[3]{0:T(128)} %pad_add_fusion.place_ref, ...), custom_call_target="tpu_custom_call" | custom-call | flops 3623878656 | bytes 10027008 | tf_op jit(solution)/shard_map/feed/pallas_call | solution.py:386
  107.5 4.7 %pair_grads.1 = (f32[384,1024]{1,0:T(8,128)}, bf16[384,1024]{1,0:T(8,128)(2,1)}) custom-call(s32[3]{0:T(128)} %pad_add_fusion.place_ref, bf16[192,768]{1,0:T(8,128)(2,1)} %get-tuple-element.256.refs_0_, bf16[192,768]{1,0:T(8,128)(2,1)} %copy-done.62, bf16[192,768]{1,0:T(8,128)(2,1)} %copy-done.61, bf16[192,768]{1,0:T(8,128)(2,1)} %copy-done.63, ...), custom_call_target="tpu_custom_call" | custom-call | flops 1207959552 | bytes 5111808 | tf_op jit(solution)/shard_map/pair_grads/pallas_call | solution.py:386
  113.8 3.4 %down_grads.1 = (f32[384,512]{1,0:T(8,128)}, bf16[384,512]{1,0:T(8,128)(2,1)}) custom-call(s32[3]{0:T(128)} %pad_add_fusion.place_ref, bf16[192,768]{1,0:T(8,128)(2,1)} %bitcast.69, bf16[192,768]{1,0:T(8,128)(2,1)} %collective-permute-done.7.refs_5_.refs_1_, bf16[192,768]{1,0:T(8,128)(2,1)} %collective-permute-done.8.refs_6_.refs_2_, ...), custom_call_target="tpu_custom_call" | custom-call | flops 603979776 | bytes 3145728 | tf_op jit(solution)/shard_map/down_grads/pallas_call | solution.py:386
  117.2 4.9 %collective-permute-done.20.refs_2_ = bf16[192,768]{1,0:T(8,128)(2,1)S(1)} collective-permute-done((bf16[192,768]{1,0:T(8,128)(2,1)S(1)}, bf16[192,768]{1,0:T(8,128)(2,1)S(1)}, u32[]{:S(2)}, u32[]{:S(2)}) %collective-permute-start.20) | collective-permute-done | bytes 294944 | tf_op jit(solution)/shard_map/ppermute | solution.py:43
  122.9 3.6 %branch.1 = (f32[192,768]{1,0:T(8,128)}, bf16[192,768]{1,0:T(8,128)(2,1)}, f32[1,768]{1,0:T(1,128)}, bf16[3,64,256]{2,1,0:T(8,128)(2,1)}, bf16[3,64,256]{2,1,0:T...) custom-call(s32[3]{0:T(128)} %pad_add_fusion.place_ref, f32[1,768]{1,0:T(1,128)} %reshape.157.gain_ref, ...), custom_call_target="tpu_custom_call" | custom-call | flops 301989888 | bytes 4823040 | tf_op jit(solution)/shard_map/branch/pallas_call | solution.py:386
  143.5 18.0 %attention_backward.1 = (bf16[4,3,64,256]{3,2,1,0:T(8,128)(2,1)}, f32[4,3,64,384]{3,2,1,0:T(8,128)}, bf16[1,4,3,64,384]{4,3,2,1,0:T(8,128)(2,1)}, bf16[2,4,3,64,384]{4,3,2,1,0:T(8,128)(2,1)}, f32[32,128]{1,0:T(8,128)}) custom-call(s32[3,4]{1,0:T(4,128)} %bitcast.83, s32[3,4,4]{2,1,0:T(4,128)} %copy-done.50, s32[3]{0:T(128)} %pad_add_fusion.place_ref, ...), custom_call_target="tpu_custom_call" | custom-call | flops 6039797760 | bytes 9437184 | tf_op jit(solution)/shard_map/attention_backward/pallas_call | solution.py:327
  176.3 7.2 %collective-permute-done.33 = bf16[96,1024]{1,0:T(8,128)(2,1)S(1)} collective-permute-done((bf16[96,1024]{1,0:T(8,128)(2,1)S(1)}, bf16[96,1024]{1,0:T(8,128)(2,1)S(1)}, u32[]{:S(2)}, u32[]{:S(2)}) %collective-permute-start.33) | collective-permute-done | bytes 196640 | tf_op jit(solution)/shard_map/ppermute | solution.py:60
  184.7 3.7 %collective-permute-start.36 = (bf16[2,96,512]{2,1,0:T(8,128)(2,1)}, bf16[2,96,512]{2,1,0:T(8,128)(2,1)S(1)}, u32[]{:S(2)}, u32[]{:S(2)}) collective-permute-start(bf16[2,96,512]{2,1,0:T(8,128)(2,1)} %get-tuple-element.349), channel_id=1, source_target_pairs={{0,8},{2,10},{4,12},{6,14},{8,0},{10,2},{12,4},{14,6},{16,24},{18,... | collective-permute-start | bytes 589832 | tf_op jit(solution)/shard_map/ppermute | solution.py:43
  188.4 6.4 %input_grads.1 = (f32[2,192,768]{2,1,0:T(8,128)}, bf16[2,192,768]{2,1,0:T(8,128)(2,1)}, f32[1,768]{1,0:T(1,128)}, f32[2,2,96,640]{3,2,1,0:T(8,128)}, bf16[2,2,96,640]{3,2,1,0:T(8,128)(2,1)}) custom-call(s32[3]{0:T(128)} %pad_add_fusion.place_ref, bf16[4,192,768]{2,1,0:T(8,128)(2,1)} %get-tuple-element.340.act_ref, ...), custom_call_target="tpu_custom_call" | custom-call | flops 1509949440 | bytes 9931776 | tf_op jit(solution)/shard_map/input_grads/pallas_call | solution.py:386
  202.3 5.5 %collective-permute-done.39 = bf16[1,2,96,640]{3,2,1,0:T(8,128)(2,1)S(1)} collective-permute-done((bf16[1,2,96,640]{3,2,1,0:T(8,128)(2,1)S(1)}, bf16[1,2,96,640]{3,2,1,0:T(8,128)(2,1)S(1)}, u32[]{:S(2)}, u32[]{:S(2)}) %collective-permute-start.39) | collective-permute-done | bytes 245792 | tf_op jit(solution)/shard_map/ppermute | solution.py:43
  210.2 8.0 %collective-permute-done.44 = bf16[96,512]{1,0:T(8,128)(2,1)S(1)} collective-permute-done((bf16[96,512]{1,0:T(8,128)(2,1)S(1)}, bf16[96,512]{1,0:T(8,128)(2,1)S(1)}, u32[]{:S(2)}, u32[]{:S(2)}) %collective-permute-start.44) | collective-permute-done | bytes 98336 | tf_op jit(solution)/shard_map/ppermute | solution.py:43
  225.0 3.6 %collective-permute-done.45 = bf16[96,640]{1,0:T(8,128)(2,1)S(1)} collective-permute-done((bf16[96,640]{1,0:T(8,128)(2,1)S(1)}, bf16[96,640]{1,0:T(8,128)(2,1)S(1)}, u32[]{:S(2)}, u32[]{:S(2)}) %collective-permute-start.45) | collective-permute-done | bytes 122912 | tf_op jit(solution)/shard_map/ppermute | solution.py:60
  228.6 3.3 %collective-permute-done.46 = bf16[96,640]{1,0:T(8,128)(2,1)S(1)} collective-permute-done((bf16[96,640]{1,0:T(8,128)(2,1)S(1)}, bf16[96,640]{1,0:T(8,128)(2,1)S(1)}, u32[]{:S(2)}, u32[]{:S(2)}) %collective-permute-start.46) | collective-permute-done | bytes 122912 | tf_op jit(solution)/shard_map/ppermute | solution.py:60
  245.4 4.7 %collective-permute-done.54 = f32[44,128]{1,0:T(8,128)S(1)} collective-permute-done((f32[44,128]{1,0:T(8,128)S(1)}, f32[44,128]{1,0:T(8,128)S(1)}, u32[]{:S(2)}, u32[]{:S(2)}) %collective-permute-start.54) | collective-permute-done | bytes 22560 | tf_op jit(solution)/shard_map/ppermute | solution.py:43
  251.8 9.8 %collective-permute-done.56.refs_6_ = bf16[4,96,512]{2,1,0:T(8,128)(2,1)} collective-permute-done((bf16[4,96,512]{2,1,0:T(8,128)(2,1)S(1)}, bf16[4,96,512]{2,1,0:T(8,128)(2,1)}, u32[]{:S(2)}, u32[]{:S(2)}) %collective-permute-start.56) | collective-permute-done | bytes 393248 | tf_op jit(solution)/shard_map/ppermute | solution.py:43
  272.0 6.3 %feed_finish.1 = (f32[384,2048]{1,0:T(8,128)}, f32[384,2048]{1,0:T(8,128)}, f32[1024,768]{1,0:T(8,128)}) custom-call(s32[3]{0:T(128)} %pad_add_fusion.place_ref, bf16[4,96,1024]{2,1,0:T(8,128)(2,1)} %copy-done.2, bf16[4,96,1024]{2,1,0:T(8,128)(2,1)} %copy-done.16, bf16[4,96,1024]{2,1,0:T(8,128)(2,1)} %copy-done.14, bf16[4,96,1024]{2,1,0:T(8,128)(2,1)} %copy-done.17, ...), custom_call_target="tpu_custom_call" | custom-call | bytes 14155776 | tf_op jit(solution)/shard_map/feed_finish/pallas_call | solution.py:386
  289.1 4.3 %input_finish.1 = (f32[384,768]{1,0:T(8,128)}, f32[384,768]{1,0:T(8,128)}, f32[384,768]{1,0:T(8,128)}, f32[384,768]{1,0:T(8,128)}) custom-call(s32[3]{0:T(128)} %pad_add_fusion.place_ref, bf16[96,2560]{1,0:T(8,128)(2,1)} %copy-done.6, bf16[96,2560]{1,0:T(8,128)(2,1)} %copy-done.22, bf16[96,2560]{1,0:T(8,128)(2,1)} %collective-permute-done.55.refs_2_, ...), custom_call_target="tpu_custom_call" | custom-call | bytes 7274496 | tf_op jit(solution)/shard_map/input_finish/pallas_call | solution.py:386
  (328 shorter events, 130.4 us)
Async XLA Ops:
  0.7 22.0 %collective-permute-start = (bf16[3,64,768]{2,1,0:T(8,128)(2,1)}, bf16[3,64,768]{2,1,0:T(8,128)(2,1)S(1)}, u32[]{:S(2)}, u32[]{:S(2)}) collective-permute-start(bf16[3,64,768]{2,1,0:T(8,128)(2,1)} %bitcast.58), channel_id=1, source_target_pairs={{0,8},{2,10},{4,12},{6,14},{8,16},{10,18},{12,20},{14,22},{16,24},... | collective-permute-start | bytes 884744 | tf_op jit(solution)/shard_map/ppermute | solution.py:60
  3.7 22.1 %collective-permute-start.1 = (bf16[3,64,768]{2,1,0:T(8,128)(2,1)}, bf16[3,64,768]{2,1,0:T(8,128)(2,1)}, u32[]{:S(2)}, u32[]{:S(2)}) collective-permute-start(bf16[3,64,768]{2,1,0:T(8,128)(2,1)} %bitcast.59), channel_id=1, source_target_pairs={{0,16},{2,18},{4,20},{6,22},{8,24},{10,26},{12,28},{14,30},{16,0},... | collective-permute-start | bytes 884744 | tf_op jit(solution)/shard_map/ppermute | solution.py:60
  6.3 19.5 %collective-permute-start.2 = (bf16[3,64,768]{2,1,0:T(8,128)(2,1)}, bf16[3,64,768]{2,1,0:T(8,128)(2,1)}, u32[]{:S(2)}, u32[]{:S(2)}) collective-permute-start(bf16[3,64,768]{2,1,0:T(8,128)(2,1)} %bitcast.60), channel_id=1, source_target_pairs={{0,24},{2,26},{4,28},{6,30},{8,0},{10,2},{12,4},{14,6},{16,8},{18,... | collective-permute-start | bytes 884744 | tf_op jit(solution)/shard_map/ppermute | solution.py:60
  29.7 15.5 %collective-permute-start.5 = (bf16[4,3,64,384]{3,2,1,0:T(8,128)(2,1)}, bf16[4,3,64,384]{3,2,1,0:T(8,128)(2,1)}, u32[]{:S(2)}, u32[]{:S(2)}) collective-permute-start(bf16[4,3,64,384]{3,2,1,0:T(8,128)(2,1)} %get-tuple-element.234.refs_0_.refs_4_), channel_id=1, source_target_pairs={{0,4},{2,6},{4,0},{6,2},{8,12},{10,14},{12,8},{14,10},{16,20},{18,... | collective-permute-start | bytes 1769480 | tf_op jit(solution)/shard_map/ppermute | solution.py:43
  31.2 16.0 %collective-permute-start.4 = (bf16[4,3,64,384]{3,2,1,0:T(8,128)(2,1)}, bf16[4,3,64,384]{3,2,1,0:T(8,128)(2,1)}, u32[]{:S(2)}, u32[]{:S(2)}) collective-permute-start(bf16[4,3,64,384]{3,2,1,0:T(8,128)(2,1)} %get-tuple-element.234.refs_0_.refs_4_), channel_id=1, source_target_pairs={{0,2},{2,0},{4,6},{6,4},{8,10},{10,8},{12,14},{14,12},{16,18},{18,... | collective-permute-start | bytes 1769480 | tf_op jit(solution)/shard_map/ppermute | solution.py:43
  45.1 16.0 %collective-permute-start.9 = (bf16[384,768]{1,0:T(8,128)(2,1)S(1)}, bf16[384,768]{1,0:T(8,128)(2,1)S(1)}, u32[]{:S(2)}, u32[]{:S(2)}) collective-permute-start(bf16[384,768]{1,0:T(8,128)(2,1)S(1)} %copy-done.4), channel_id=1, source_target_pairs={{0,1},{1,0},{2,3},{3,2},{4,5},{5,4},{6,7},{7,6},{8,9},{9,8},{10,11... | collective-permute-start | bytes 1769480 | tf_op jit(solution)/shard_map/ppermute | solution.py:43
  61.2 23.9 %collective-permute-start.13 = (bf16[192,768]{1,0:T(8,128)(2,1)}, bf16[192,768]{1,0:T(8,128)(2,1)S(1)}, u32[]{:S(2)}, u32[]{:S(2)}) collective-permute-start(bf16[192,768]{1,0:T(8,128)(2,1)} %collective-permute-done.8.refs_6_.refs_2_), channel_id=1, source_target_pairs={{0,2},{2,0},{4,6},{6,4},{8,10},{10,8},{12,14},{14,12},{16,18},{18,... | collective-permute-start | bytes 884744 | tf_op jit(solution)/shard_map/ppermute | solution.py:43
  61.3 32.3 %collective-permute-start.17 = (bf16[384,1024]{1,0:T(8,128)(2,1)S(1)}, bf16[384,1024]{1,0:T(8,128)(2,1)S(1)}, u32[]{:S(2)}, u32[]{:S(2)}) collective-permute-start(bf16[384,1024]{1,0:T(8,128)(2,1)S(1)} %copy-done.19), channel_id=1, source_target_pairs={{0,1},{1,0},{2,3},{3,2},{4,5},{5,4},{6,7},{7,6},{8,9},{9,8},{10,11... | collective-permute-start | bytes 2359304 | tf_op jit(solution)/shard_map/ppermute | solution.py:43
  112.3 21.1 %collective-permute-start.21 = (bf16[384,1024]{1,0:T(8,128)(2,1)}, bf16[384,1024]{1,0:T(8,128)(2,1)S(1)}, u32[]{:S(2)}, u32[]{:S(2)}) collective-permute-start(bf16[384,1024]{1,0:T(8,128)(2,1)} %get-tuple-element.295), channel_id=1, source_target_pairs={{0,1},{1,0},{2,3},{3,2},{4,5},{5,4},{6,7},{7,6},{8,9},{9,8},{10,11... | collective-permute-start | bytes 2359304 | tf_op jit(solution)/shard_map/ppermute | solution.py:43
  133.3 28.3 %collective-permute-start.29 = (bf16[2,2,96,768]{3,2,1,0:T(8,128)(2,1)}, bf16[2,2,96,768]{3,2,1,0:T(8,128)(2,1)S(1)}, u32[]{:S(2)}, u32[]{:S(2)}) collective-permute-start(bf16[2,2,96,768]{3,2,1,0:T(8,128)(2,1)} %get-tuple-element.322), channel_id=1, source_target_pairs={{0,2},{2,0},{4,6},{6,4},{8,10},{10,8},{12,14},{14,12},{16,18},{18,... | collective-permute-start | bytes 1769480 | tf_op jit(solution)/shard_map/ppermute | solution.py:43
  137.0 24.6 %collective-permute-start.28 = (bf16[384,512]{1,0:T(8,128)(2,1)S(1)}, bf16[384,512]{1,0:T(8,128)(2,1)S(1)}, u32[]{:S(2)}, u32[]{:S(2)}) collective-permute-start(bf16[384,512]{1,0:T(8,128)(2,1)S(1)} %copy-done.58), channel_id=1, source_target_pairs={{0,1},{1,0},{2,3},{3,2},{4,5},{5,4},{6,7},{7,6},{8,9},{9,8},{10,11... | collective-permute-start | bytes 1179656 | tf_op jit(solution)/shard_map/ppermute | solution.py:43
  138.5 23.0 %collective-permute-start.25 = (bf16[96,1024]{1,0:T(8,128)(2,1)}, bf16[96,1024]{1,0:T(8,128)(2,1)S(1)}, u32[]{:S(2)}, u32[]{:S(2)}) collective-permute-start(bf16[96,1024]{1,0:T(8,128)(2,1)} %get-tuple-element.318), channel_id=1, source_target_pairs={{0,8},{2,10},{4,12},{6,14},{8,16},{10,18},{12,20},{14,22},{16,24},... | collective-permute-start | bytes 589832 | tf_op jit(solution)/shard_map/ppermute | solution.py:60
  140.1 21.4 %collective-permute-start.26 = (bf16[96,1024]{1,0:T(8,128)(2,1)}, bf16[96,1024]{1,0:T(8,128)(2,1)S(1)}, u32[]{:S(2)}, u32[]{:S(2)}) collective-permute-start(bf16[96,1024]{1,0:T(8,128)(2,1)} %get-tuple-element.319), channel_id=1, source_target_pairs={{0,16},{2,18},{4,20},{6,22},{8,24},{10,26},{12,28},{14,30},{16,0},... | collective-permute-start | bytes 589832 | tf_op jit(solution)/shard_map/ppermute | solution.py:60
  140.8 20.8 %collective-permute-start.27 = (bf16[96,1024]{1,0:T(8,128)(2,1)}, bf16[96,1024]{1,0:T(8,128)(2,1)S(1)}, u32[]{:S(2)}, u32[]{:S(2)}) collective-permute-start(bf16[96,1024]{1,0:T(8,128)(2,1)} %get-tuple-element.320), channel_id=1, source_target_pairs={{0,24},{2,26},{4,28},{6,30},{8,0},{10,2},{12,4},{14,6},{16,8},{18,... | collective-permute-start | bytes 589832 | tf_op jit(solution)/shard_map/ppermute | solution.py:60
  164.9 18.6 %collective-permute-start.31 = (bf16[4,3,64,384]{3,2,1,0:T(8,128)(2,1)S(1)}, bf16[4,3,64,384]{3,2,1,0:T(8,128)(2,1)}, u32[]{:S(2)}, u32[]{:S(2)}) collective-permute-start(bf16[4,3,64,384]{3,2,1,0:T(8,128)(2,1)S(1)} %fusion), channel_id=1, source_target_pairs={{0,4},{2,6},{4,0},{6,2},{8,12},{10,14},{12,8},{14,10},{16,20},{18,... | collective-permute-start | bytes 1769480 | tf_op jit(solution)/shard_map/ppermute | solution.py:43
  166.6 16.8 %collective-permute-start.33 = (bf16[96,1024]{1,0:T(8,128)(2,1)S(1)}, bf16[96,1024]{1,0:T(8,128)(2,1)S(1)}, u32[]{:S(2)}, u32[]{:S(2)}) collective-permute-start(bf16[96,1024]{1,0:T(8,128)(2,1)S(1)} %add_convert_fusion.3), channel_id=1, source_target_pairs={{0,16},{2,18},{4,20},{6,22},{8,24},{10,26},{12,28},{14,30},{16,0},... | collective-permute-start | bytes 589832 | tf_op jit(solution)/shard_map/ppermute | solution.py:60
  196.7 22.1 %collective-permute-start.42 = (bf16[4,96,1024]{2,1,0:T(8,128)(2,1)S(1)}, bf16[4,96,1024]{2,1,0:T(8,128)(2,1)S(1)}, u32[]{:S(2)}, u32[]{:S(2)}) collective-permute-start(bf16[4,96,1024]{2,1,0:T(8,128)(2,1)S(1)} %pad_maximum_fusion.1.refs_0_), channel_id=1, source_target_pairs={{0,4},{2,6},{4,0},{6,2},{8,12},{10,14},{12,8},{14,10},{16,20},{18,... | collective-permute-start | bytes 2359304 | tf_op jit(solution)/shard_map/ppermute | solution.py:43
  202.2 18.3 %collective-permute-start.43 = (bf16[2,192,768]{2,1,0:T(8,128)(2,1)S(1)}, bf16[2,192,768]{2,1,0:T(8,128)(2,1)S(1)}, u32[]{:S(2)}, u32[]{:S(2)}) collective-permute-start(bf16[2,192,768]{2,1,0:T(8,128)(2,1)S(1)} %copy-done.57), channel_id=1, source_target_pairs={{0,8},{2,10},{4,12},{6,14},{8,0},{10,2},{12,4},{14,6},{16,24},{18,... | collective-permute-start | bytes 1769480 | tf_op jit(solution)/shard_map/ppermute | solution.py:43
  224.8 36.8 %collective-permute-start.57 = (bf16[4,96,1024]{2,1,0:T(8,128)(2,1)S(1)}, bf16[4,96,1024]{2,1,0:T(8,128)(2,1)S(1)}, u32[]{:S(2)}, u32[]{:S(2)}) collective-permute-start(bf16[4,96,1024]{2,1,0:T(8,128)(2,1)S(1)} %pad_maximum_fusion.1.refs_0_), channel_id=1, source_target_pairs={{0,2},{2,0},{4,6},{6,4},{8,10},{10,8},{12,14},{14,12},{16,18},{18,... | collective-permute-start | bytes 2359304 | tf_op jit(solution)/shard_map/ppermute | solution.py:43
  228.6 33.1 %collective-permute-start.58 = (bf16[4,96,1024]{2,1,0:T(8,128)(2,1)S(1)}, bf16[4,96,1024]{2,1,0:T(8,128)(2,1)S(1)}, u32[]{:S(2)}, u32[]{:S(2)}) collective-permute-start(bf16[4,96,1024]{2,1,0:T(8,128)(2,1)S(1)} %copy-done.15), channel_id=1, source_target_pairs={{0,2},{2,0},{4,6},{6,4},{8,10},{10,8},{12,14},{14,12},{16,18},{18,... | collective-permute-start | bytes 2359304 | tf_op jit(solution)/shard_map/ppermute | solution.py:43
  242.1 19.5 %collective-permute-start.55 = (bf16[96,2560]{1,0:T(8,128)(2,1)S(1)}, bf16[96,2560]{1,0:T(8,128)(2,1)}, u32[]{:S(2)}, u32[]{:S(2)}) collective-permute-start(bf16[96,2560]{1,0:T(8,128)(2,1)S(1)} %pad_maximum_fusion.2.refs_0_), channel_id=1, source_target_pairs={{0,4},{2,6},{4,0},{6,2},{8,12},{10,14},{12,8},{14,10},{16,20},{18,... | collective-permute-start | bytes 1474568 | tf_op jit(solution)/shard_map/ppermute | solution.py:43
  250.0 16.3 %collective-permute-start.66 = (bf16[2,192,768]{2,1,0:T(8,128)(2,1)}, bf16[2,192,768]{2,1,0:T(8,128)(2,1)S(1)}, u32[]{:S(2)}, u32[]{:S(2)}) collective-permute-start(bf16[2,192,768]{2,1,0:T(8,128)(2,1)} %get-tuple-element.406), channel_id=1, source_target_pairs={{0,2},{2,0},{4,6},{6,4},{8,10},{10,8},{12,14},{14,12},{16,18},{18,... | collective-permute-start | bytes 1769480 | tf_op jit(solution)/shard_map/ppermute | solution.py:43
  264.5 16.7 %collective-permute-start.65 = (bf16[192,768]{1,0:T(8,128)(2,1)}, bf16[192,768]{1,0:T(8,128)(2,1)}, u32[]{:S(2)}, u32[]{:S(2)}) collective-permute-start(bf16[192,768]{1,0:T(8,128)(2,1)} %fusion.3), channel_id=1, source_target_pairs={{0,16},{2,18},{4,20},{6,22},{8,24},{10,26},{12,28},{14,30},{16,0},... | collective-permute-start | bytes 884744 | tf_op jit(solution)/shard_map/ppermute | solution.py:43
  266.3 15.7 %collective-permute-start.61 = (bf16[96,2560]{1,0:T(8,128)(2,1)S(1)}, bf16[96,2560]{1,0:T(8,128)(2,1)S(1)}, u32[]{:S(2)}, u32[]{:S(2)}) collective-permute-start(bf16[96,2560]{1,0:T(8,128)(2,1)S(1)} %pad_maximum_fusion.2.refs_0_), channel_id=1, source_target_pairs={{0,2},{2,0},{4,6},{6,4},{8,10},{10,8},{12,14},{14,12},{16,18},{18,... | collective-permute-start | bytes 1474568 | tf_op jit(solution)/shard_map/ppermute | solution.py:43
  (113 other events, 958.0 us)
where the time goes:
time: 294 us; the launch traced here: 293 us
  waiting for transfers between devices  102 us (35%)
  Pallas kernels  90.1 us (31%)
  starting transfers between devices  71 us (24%)
  local copies, waits for them, and re-layouts  21.6 us (7%)
  other arithmetic  7.4 us (3%)
    ppermute x52, waiting for transfers between devices, hop(): return lax.ppermute(v, axis, [(i, i ^ bit) for i in range(size)])  73.9 us
    pallas_call x13, Pallas kernels, call(): pl.pallas_call(kernel, out_shape=tuple(out_shape), **grid, in_specs=specs...  56.3 us
    ppermute x52, starting transfers between devices, hop(): return lax.ppermute(v, axis, [(i, i ^ bit) for i in range(size)])  38.7 us
    ppermute x18, starting transfers between devices, shift(): lax.ppermute(v, 'ctx', [(i, (i + steps * stride) % size) for i in range(s...  32.2 us
    ppermute x18, waiting for transfers between devices, shift(): lax.ppermute(v, 'ctx', [(i, (i + steps * stride) % size) for i in range(s...  27.9 us
    pallas_call x1, Pallas kernels, attention_backward(): pl.pallas_call(functools.partial(backward_kernel, count, blocks), out_sha...  18 us
    pallas_call x1, Pallas kernels, attention_forward(): pl.pallas_call(functools.partial(forward_kernel, count, blocks), out_shap...  11.9 us
    unnamed x136, local copies, waits for them, and re-layouts  10.3 us
  transfers between devices with their start and end apart: 70, of which 27 were waited for; matrix products, arithmetic and copies ran while one was open for 7% of the time, Pallas kernels for 25%

commit v1 on v0

--- a/solution.py
+++ b/solution.py
@@ -153,37 +153,52 @@
             sorted_ref[pl.ds(to, 64), :] = kv_refs[j][e, 0]
 
 
-def bias_of(strip_ref, h, offs, half, rows, low):
-    a = strip_ref[h, pl.ds(offs[2 * half], rows), :]
-    b = strip_ref[h, pl.ds(offs[2 * half + 1], rows), :]
-    return jnp.where(low, a, b)
+def rows_sum(value):
+    return jnp.sum(value.reshape(value.shape[0] // 8, 8, value.shape[1]), axis=0)
+
+
+CHUNK = 128
+
+
+def chunk_scores(strip_ref, sorted_ref, query, h, start, offs, low):
+    scores = dot_t(sorted_ref[start : start + CHUNK, KEY_COLS[h] : KEY_COLS[h] + 128], query)
+    parts = []
+    for half in range(2):
+        a = strip_ref[h, pl.ds(offs[2 * half] + start, CHUNK), :]
+        b = strip_ref[h, pl.ds(offs[2 * half + 1] + start, CHUNK), :]
+        parts.append(scores[:, half * 128 : half * 128 + 128] + jnp.where(low, a, b))
+    return jnp.concatenate(parts, axis=1)
 
 
 def forward_kernel(count, blocks, qplace_ref, kplace_ref, strip_ref, q_ref, *refs):
     kv_refs = refs[:count]
     o_refs = refs[count : count + GROUPS]
-    lse_ref, sorted_ref = refs[count + GROUPS :]
+    lse_ref, sorted_ref, score_ref, weight_ref = refs[count + GROUPS :]
     m = pl.program_id(0)
     rows = 64 * blocks
     sort_blocks(count, m, kplace_ref, kv_refs, sorted_ref)
     offs = [pl.multiple_of((blocks - 1 - qplace_ref[m, e]) * 64, 64) for e in range(GROUPS)]
     queries = split_heads(q_ref[:, 0].reshape(GROUPS * 64, 256), False)
-    low = lax.broadcasted_iota(jnp.int32, (rows, 128), 1) < 64
+    low = lax.broadcasted_iota(jnp.int32, (CHUNK, 128), 1) < 64
     mixed = []
     for h in range(3):
-        keys = sorted_ref[:, KEY_COLS[h] : KEY_COLS[h] + 128]
-        values = sorted_ref[:, VALUE_COLS[h] : VALUE_COLS[h] + 128]
-        scores = dot_t(keys, queries[h])
-        parts = []
-        for half in range(2):
-            s = scores[:, half * 128 : half * 128 + 128] + bias_of(strip_ref, h, offs, half, rows, low)
-            top = jnp.max(s, axis=0, keepdims=True)
-            e = jnp.exp(s - top)
-            total = jnp.sum(e, axis=0, keepdims=True)
-            lse_ref[0, h : h + 1, half * 128 : half * 128 + 128] = top + jnp.log(total)
-            parts.append((e * (1.0 / total)).astype(LOW))
-        weights = jnp.concatenate(parts, axis=1)
-        mixed.append(t_dot(values, weights))
+        top = jnp.full((8, GROUPS * 64), -jnp.inf, WIDE)
+        for start in range(0, rows, CHUNK):
+            s = chunk_scores(strip_ref, sorted_ref, queries[h], h, start, offs, low)
+            score_ref[start : start + CHUNK, :] = s
+            top = jnp.maximum(top, jnp.max(s.reshape(CHUNK // 8, 8, GROUPS * 64), axis=0))
+        top = jnp.max(top, axis=0, keepdims=True)
+        total = jnp.zeros((8, GROUPS * 64), WIDE)
+        for start in range(0, rows, CHUNK):
+            e = jnp.exp(score_ref[start : start + CHUNK, :] - top)
+            score_ref[start : start + CHUNK, :] = e
+            total = total + rows_sum(e)
+        total = jnp.sum(total, axis=0, keepdims=True)
+        lse_ref[0, h : h + 1, :] = top + jnp.log(total)
+        scale = 1.0 / total
+        for start in range(0, rows, CHUNK):
+            weight_ref[start : start + CHUNK, :] = (score_ref[start : start + CHUNK, :] * scale).astype(LOW)
+        mixed.append(t_dot(sorted_ref[:, VALUE_COLS[h] : VALUE_COLS[h] + 128], weight_ref[...]))
     sub = lax.broadcasted_iota(jnp.int32, (128, GROUPS * 64), 0) < 64
     first = jnp.where(sub, mixed[0], mixed[1]).T
     second = jnp.where(sub, 0.0, mixed[2]).T
@@ -209,7 +224,11 @@
             in_specs=[pl.BlockSpec(strip.shape, lambda m, *_: (0, 0, 0)), by_micro(256)] + [by_micro(kv_cols)] * count,
             out_specs=(pl.BlockSpec((1, 64, 256), lambda m, *_: (m, 0, 0)),) * GROUPS
             + (pl.BlockSpec((1, 3, GROUPS * 64), lambda m, *_: (m, 0, 0)),),
-            scratch_shapes=[pltpu.VMEM((rows, kv_cols), LOW)],
+            scratch_shapes=[
+                pltpu.VMEM((rows, kv_cols), LOW),
+                pltpu.VMEM((rows, GROUPS * 64), WIDE),
+                pltpu.VMEM((rows, GROUPS * 64), LOW),
+            ],
         ),
         compiler_params=pltpu.CompilerParams(vmem_limit_bytes=VMEM_LIMIT),
         cost_estimate=pl.CostEstimate(
@@ -227,53 +246,71 @@
     kv_refs = refs[:count]
     dq_ref = refs[count]
     own_ref, even_ref, odd_ref, table_ref = refs[count + 1 : count + 5]
-    sorted_ref, grad_ref, lower_ref, upper_ref = refs[count + 5 :]
+    sorted_ref, grad_ref, p_ref, dp_ref, soft_ref, ds_ref, wide_ref, near_ref, far_ref = refs[count + 5 :]
     m = pl.program_id(0)
     rows = 64 * blocks
+    queue = GROUPS * 64
+    near = near_ref.shape[1]
+    lead = 128
 
     @pl.when(m == 0)
     def _():
-        lower_ref[...] = jnp.zeros_like(lower_ref)
-        upper_ref[...] = jnp.zeros_like(upper_ref)
+        near_ref[...] = jnp.zeros_like(near_ref)
+        far_ref[...] = jnp.zeros_like(far_ref)
+        wide_ref[:lead, :] = jnp.zeros((lead, queue), WIDE)
+        wide_ref[lead + rows :, :] = jnp.zeros((wide_ref.shape[0] - lead - rows, queue), WIDE)
 
     sort_blocks(count, m, kplace_ref, kv_refs, sorted_ref)
     offs = [pl.multiple_of((blocks - 1 - qplace_ref[m, e]) * 64, 64) for e in range(GROUPS)]
-    queries = split_heads(q_ref[:, 0].reshape(GROUPS * 64, 256), False)
+    queries = split_heads(q_ref[:, 0].reshape(queue, 256), False)
     grads = split_heads(jnp.concatenate([r[0] for r in do_refs], axis=0), True)
-    low = lax.broadcasted_iota(jnp.int32, (rows, 128), 1) < 64
-    query_grads, scores_grads, soft = [], [], []
+    low = lax.broadcasted_iota(jnp.int32, (CHUNK, 128), 1) < 64
+    lane_block = lax.broadcasted_iota(jnp.int32, (8, queue), 1) // 64
+    own_place = jnp.zeros((8, queue), jnp.int32)
+    for e in range(GROUPS):
+        own_place = jnp.where(lane_block == e, qplace_ref[m, e], own_place)
+    near_low = lax.broadcasted_iota(jnp.int32, (near, 128), 1) < 64
+    query_grads = []
     for h in range(3):
-        keys = sorted_ref[:, KEY_COLS[h] : KEY_COLS[h] + 128]
-        values = sorted_ref[:, VALUE_COLS[h] : VALUE_COLS[h] + 128]
-        scores = dot_t(keys, queries[h])
-        weight_grads = dot_t(values, grads[h])
-        ds_parts, p_parts = [], []
+        delta = jnp.zeros((8, queue), WIDE)
+        lse = lse_ref[0, h : h + 1, :]
+        for start in range(0, rows, CHUNK):
+            at = slice(start, start + CHUNK)
+            p = jnp.exp(chunk_scores(strip_ref, sorted_ref, queries[h], h, start, offs, low) - lse)
+            dp = dot_t(sorted_ref[at, VALUE_COLS[h] : VALUE_COLS[h] + 128], grads[h])
+            p_ref[at, :] = p
+            dp_ref[at, :] = dp
+            soft_ref[h, at, :] = p.astype(LOW)
+            delta = delta + rows_sum(p * dp)
+        delta = jnp.sum(delta, axis=0, keepdims=True)
+        before = jnp.zeros((8, queue), WIDE)
+        after = jnp.zeros((8, queue), WIDE)
+        for start in range(0, rows, CHUNK):
+            at = slice(start, start + CHUNK)
+            ds = (p_ref[at, :] * (dp_ref[at, :] - delta)).astype(LOW)
+            ds_ref[h, at, :] = ds
+            wide = ds.astype(WIDE)
+            wide_ref[lead + start : lead + start + CHUNK, :] = wide
+            for k in range(CHUNK // 64):
+                block = start // 64 + k
+                part = rows_sum(wide[k * 64 : k * 64 + 64])
+                before = before + jnp.where(own_place >= block + 3, part, 0.0)
+                after = after + jnp.where(own_place <= block - 3, part, 0.0)
+        far_ref[h, 0] += before
+        far_ref[h, 1] += after
         for half in range(2):
             cols = slice(half * 128, half * 128 + 128)
-            s = scores[:, cols] + bias_of(strip_ref, h, offs, half, rows, low)
-            p = jnp.exp(s - lse_ref[0, h : h + 1, cols])
-            dp = weight_grads[:, cols]
-            delta = jnp.sum(p * dp, axis=0, keepdims=True)
-            ds = (p * (dp - delta)).astype(LOW)
-            p_parts.append(p.astype(LOW))
-            ds_parts.append(ds)
-            wide = ds.astype(WIDE)
-            at = pl.ds(offs[2 * half], rows)
-            lower_ref[h, at, :] += wide
-            at = pl.ds(offs[2 * half + 1], rows)
-            upper_ref[h, at, :] += wide
-        ds_all = jnp.concatenate(ds_parts, axis=1)
-        p_all = jnp.concatenate(p_parts, axis=1)
-        query_grads.append(t_dot(keys, ds_all))
-        scores_grads.append(ds_all)
-        soft.append(p_all)
-    sub = lax.broadcasted_iota(jnp.int32, (128, GROUPS * 64), 0) < 64
+            a = wide_ref[pl.ds(pl.multiple_of(qplace_ref[m, 2 * half] * 64, 64), near), cols]
+            b = wide_ref[pl.ds(pl.multiple_of(qplace_ref[m, 2 * half + 1] * 64, 64), near), cols]
+            near_ref[h] += jnp.where(near_low, a, b)
+        query_grads.append(t_dot(sorted_ref[:, KEY_COLS[h] : KEY_COLS[h] + 128], ds_ref[h]))
+    sub = lax.broadcasted_iota(jnp.int32, (128, queue), 0) < 64
     first = jnp.where(sub, query_grads[0], query_grads[1]).T
     second = jnp.where(sub, query_grads[2], 0.0).T
     dq_ref[:, 0] = jnp.concatenate([first, second], axis=1).astype(LOW).reshape(GROUPS, 64, 256)
-    grad_ref[:, 0:128] = dot(scores_grads[0], queries[0]) + dot(scores_grads[1], queries[1])
-    grad_ref[:, 128:256] = dot(scores_grads[2], queries[2]) + dot(soft[2], grads[2])
-    grad_ref[:, 256:384] = dot(soft[0], grads[0]) + dot(soft[1], grads[1])
+    grad_ref[:, 0:128] = dot(ds_ref[0], queries[0]) + dot(ds_ref[1], queries[1])
+    grad_ref[:, 128:256] = dot(ds_ref[2], queries[2]) + dot(soft_ref[2], grads[2])
+    grad_ref[:, 256:384] = dot(soft_ref[0], grads[0]) + dot(soft_ref[1], grads[1])
     for j in range(count):
         for e in range(GROUPS):
             at = pl.multiple_of(kplace_ref[m, j, e] * 64, 64)
@@ -287,30 +324,20 @@
 
     @pl.when(m == pl.num_programs(0) - 1)
     def _():
-        centre = 64 * (blocks - 1)
-        start = centre - NEAR_LEAD
-        near = 256
         sums_row = lax.broadcasted_iota(jnp.int32, (32, 128), 0)
+        lanes = lax.broadcasted_iota(jnp.int32, (32, 128), 1)
         side = lax.broadcasted_iota(jnp.int32, (near, 128), 1)
-        rel = lax.broadcasted_iota(jnp.int32, (near, 128), 0) + (start - centre) - jnp.where(side >= 64, side - 64, side)
+        rel = lax.broadcasted_iota(jnp.int32, (near, 128), 0) - lead - jnp.where(side >= 64, side - 64, side)
         label = bucket_of(rel)
-
-        def folded(h, first, size):
-            lane = lax.broadcasted_iota(jnp.int32, (size, 128), 1) < 64
-            return jnp.where(lane, lower_ref[h, first : first + size, :], upper_ref[h, first : first + size, :])
-
         table = jnp.zeros((32, 128), WIDE)
         for h in range(3):
-            before = jnp.sum(folded(h, 0, start), axis=0, keepdims=True)
-            last = start + near
-            after = jnp.sum(folded(h, last, 2 * rows - last), axis=0, keepdims=True)
-            window = folded(h, start, near)
-            result = jnp.where(sums_row == 15, before, jnp.where(sums_row == 31, after, 0.0))
+            far = [jnp.sum(far_ref[h, k][:, :128] + far_ref[h, k][:, 128:], axis=0, keepdims=True) for k in range(2)]
+            result = jnp.where(sums_row == 15, far[0], jnp.where(sums_row == 31, far[1], 0.0))
+            window = near_ref[h]
             for b in range(32):
                 part = jnp.sum(jnp.where(label == b, window, 0.0), axis=0, keepdims=True)
                 result = result + jnp.where(sums_row == b, part, 0.0)
             total = jnp.sum(result, axis=1, keepdims=True)
-            lanes = lax.broadcasted_iota(jnp.int32, (32, 128), 1)
             table = jnp.where(lanes == place_ref[0] * 3 + h, total, table)
         table_ref[...] = table
 
@@ -349,8 +376,13 @@
             scratch_shapes=[
                 pltpu.VMEM((rows, kv_cols), LOW),
                 pltpu.VMEM((rows, kv_cols), WIDE),
-                pltpu.VMEM((3, 2 * rows, 128), WIDE),
-                pltpu.VMEM((3, 2 * rows, 128), WIDE),
+                pltpu.VMEM((rows, GROUPS * 64), WIDE),
+                pltpu.VMEM((rows, GROUPS * 64), WIDE),
+                pltpu.VMEM((3, rows, GROUPS * 64), LOW),
+                pltpu.VMEM((3, rows, GROUPS * 64), LOW),
+                pltpu.VMEM((rows + 256, GROUPS * 64), WIDE),
+                pltpu.VMEM((3, 320, 128), WIDE),
+                pltpu.VMEM((3, 2, 8, GROUPS * 64), WIDE),
             ],
         ),
         compiler_params=pltpu.CompilerParams(vmem_limit_bytes=VMEM_LIMIT),
@@ -421,11 +453,10 @@
     micro, rows, width = x_refs[0].shape
     for d in range(GROUPS):
         x = x_refs[d][...].reshape(micro * rows, width).astype(WIDE)
-        act = (x * rms_scale(x) * gain_ref[...]).astype(LOW)
-        act_ref[d] = act
-        both = dot(act, full_ref[...]).astype(LOW)
-        q_ref[d] = both[:, :256].reshape(micro, rows, 256)
-        kv_ref[d] = both[:, 256:].reshape(micro, rows, 384)
+        act_ref[d] = (x * rms_scale(x) * gain_ref[...]).astype(LOW)
+    both = dot(act_ref[...].reshape(GROUPS * micro * rows, width), full_ref[...]).astype(LOW)
+    q_ref[...] = both[:, :256].reshape(GROUPS, micro, rows, 256)
+    kv_ref[...] = both[:, 256:].reshape(GROUPS, micro, rows, 384)
 
 
 def project(place, gain, x_slots, w_slots):
@@ -449,30 +480,44 @@
     return lax.rem(place_ref[0] + d, GROUPS) * 192
 
 
-def joined_kernel(parts_f, place_ref, gain_ref, x_ref, *refs):
-    o_refs, w_refs = refs[:GROUPS], refs[GROUPS : GROUPS + parts_f]
-    resid_ref, act_ref, full_ref = refs[GROUPS + parts_f :]
+def arrange_kernel(parts_f, place_ref, *refs):
+    w_refs, (out_ref, full_ref) = refs[:parts_f], refs[parts_f:]
     place_rows(full_ref, w_refs, place_ref[2])
+    for d in range(GROUPS):
+        at = group_rows(place_ref, d)
+        out_ref[d * 256 : d * 256 + 128, :] = full_ref[pl.ds(pl.multiple_of(at, 64), 128), :]
+        out_ref[d * 256 + 128 : d * 256 + 256, :] = full_ref[pl.ds(pl.multiple_of(at + 64, 64), 128), :]
+
+
+def arrange(place, w_slots):
+    width = w_slots[0].shape[1]
+    return call(
+        functools.partial(arrange_kernel, len(w_slots)),
+        "arrange",
+        place,
+        w_slots,
+        [shaped(GROUPS * 256, width)],
+        [pltpu.VMEM((width, width), LOW)],
+    )[0]
+
+
+def joined_kernel(place_ref, gain_ref, x_ref, w_ref, *refs):
+    o_refs, (resid_ref, act_ref) = refs[:GROUPS], refs[GROUPS:]
     micro, rows, width = x_ref.shape
-    total = x_ref[...].reshape(micro * rows, width).astype(WIDE)
-    for d in range(GROUPS):
-        o = o_refs[d][...].reshape(micro * rows, 256)
-        at = group_rows(place_ref, d)
-        total += dot(o[:, :128], full_ref[pl.ds(pl.multiple_of(at, 64), 128), :])
-        total += dot(o[:, 128:], full_ref[pl.ds(pl.multiple_of(at + 64, 64), 128), :])
+    o = jnp.concatenate([r[...].reshape(micro * rows, 256) for r in o_refs], axis=1)
+    total = x_ref[...].reshape(micro * rows, width).astype(WIDE) + dot(o, w_ref[...])
     resid_ref[...] = total
     act_ref[...] = (total * rms_scale(total) * gain_ref[...]).astype(LOW)
 
 
-def joined(place, gain, x, o_slots, w_slots):
+def joined(place, gain, x, o_slots, w_rel):
     micro, rows, width = x.shape
     return call(
-        functools.partial(joined_kernel, len(w_slots)),
+        joined_kernel,
         "joined",
         place,
-        [gain, x, *o_slots, *w_slots],
+        [gain, x, w_rel, *o_slots],
         [shaped(micro * rows, width, dtype=WIDE), shaped(micro * rows, width)],
-        [pltpu.VMEM((width, width), LOW)],
         flops=2 * micro * rows * width * 1024,
     )
 
@@ -509,21 +554,27 @@
     place_rows(pair_ref, pair_refs, place_ref[2])
     place_rows(down_ref, down_refs, place_ref[2])
     cols = hid_ref.shape[-1]
+    rows = act_refs[0].shape[0]
+    act = jnp.concatenate([r[...] for r in act_refs], axis=0)
+    g = jnp.concatenate([r[...] for r in g_refs], axis=0)
+    both = dot(act, pair_ref[...])
+    dh = dot_t(g, down_ref[...])
     for j in range(fast):
-        both = dot(act_refs[j][...], pair_ref[...])
-        z, up = both[:, :cols], both[:, cols:]
+        at = slice(j * rows, j * rows + rows)
+        z, up = both[at, :cols], both[at, cols:]
         square = z * z
         t = jnp.tanh(GELU_A * (z + GELU_B * square * z))
         half = 0.5 * (1.0 + t)
         gelu = z * half
         slope = half + (0.5 * z) * (1.0 - t * t) * (GELU_A * (1.0 + 3.0 * GELU_B * square))
-        hid = (gelu * up).astype(LOW)
-        dh = dot_t(g_refs[j][...], down_ref[...])
-        grads = jnp.concatenate([(dh * up * slope).astype(LOW), (dh * gelu).astype(LOW)], axis=1)
-        hid_ref[j] = hid
-        grad_ref[j] = grads
-        put_part(two_refs, j, dot_t(grads, pair_ref[...]))
-        put_part(out_refs, j, dot(hid, down_ref[...]))
+        hid_ref[j] = (gelu * up).astype(LOW)
+        grad_ref[j, :, :cols] = (dh[at] * up * slope).astype(LOW)
+        grad_ref[j, :, cols:] = (dh[at] * gelu).astype(LOW)
+    two = dot_t(grad_ref[...].reshape(fast * rows, 2 * cols), pair_ref[...])
+    out = dot(hid_ref[...].reshape(fast * rows, cols), down_ref[...])
+    for j in range(fast):
+        put_part(two_refs, j, two[j * rows : j * rows + rows])
+        put_part(out_refs, j, out[j * rows : j * rows + rows])
 
 
 def feed(place, act_slots, g_slots, pair_slots, down_slots):
@@ -661,12 +712,10 @@
     return sum((r[0] if len(r.shape) == 3 else r[...]).astype(WIDE) for r in refs)
 
 
-def branch_kernel(parts_f, count, place_ref, gain_ref, resid_ref, g_ref, *refs):
+def branch_kernel(count, place_ref, gain_ref, resid_ref, g_ref, w_ref, *refs):
     two_refs, refs = refs[:count], refs[count:]
-    w_refs, refs = refs[:parts_f], refs[parts_f:]
     grad_ref, low_ref, gain_out = refs[:3]
-    do_refs, full_ref = refs[3 : 3 + GROUPS], refs[3 + GROUPS]
-    place_rows(full_ref, w_refs, place_ref[2])
+    do_refs = refs[3:]
     micro, rows, _ = do_refs[0].shape
     grad_two = summed(two_refs)
     resid = resid_ref[...]
@@ -677,24 +726,20 @@
     grad_ref[...] = grad
     low = grad.astype(LOW)
     low_ref[...] = low
+    both = dot_t(low, w_ref[...]).astype(LOW)
     for d in range(GROUPS):
-        at = group_rows(place_ref, d)
-        first = dot_t(low, full_ref[pl.ds(pl.multiple_of(at, 64), 128), :])
-        second = dot_t(low, full_ref[pl.ds(pl.multiple_of(at + 64, 64), 128), :])
-        both = jnp.concatenate([first, second], axis=1).astype(LOW)
-        do_refs[d][...] = both.reshape(micro, rows, 256)
-
-
-def branch(place, gain, resid, g, two_list, w_slots, micro):
+        do_refs[d][...] = both[:, d * 256 : d * 256 + 256].reshape(micro, rows, 256)
+
+
+def branch(place, gain, resid, g, two_list, w_rel, micro):
     rows, width = resid.shape
     results = call(
-        functools.partial(branch_kernel, len(w_slots), len(two_list)),
+        functools.partial(branch_kernel, len(two_list)),
         "branch",
         place,
-        [gain, resid, g, *two_list, *w_slots],
+        [gain, resid, g, w_rel, *two_list],
         [shaped(rows, width, dtype=WIDE), shaped(rows, width), shaped(1, width, dtype=WIDE)]
         + [shaped(micro, rows // micro, 256)] * GROUPS,
-        [pltpu.VMEM((width, width), LOW)],
         flops=2 * rows * width * 1024,
     )
     return results[0], results[1], results[2], list(results[3:])
@@ -807,12 +852,13 @@
     out_refs, refs = refs[:count], refs[count:]
     x_grad_ref, out_ref = refs
     micro, rows, width = x_ref.shape
-    grad_one = one_ref[...] + got_ref[...].astype(WIDE)
+    grad_one = one_ref[...] + got_ref[: micro * rows, :].astype(WIDE)
     x = x_ref[...].reshape(micro * rows, width).astype(WIDE)
     scale = rms_scale(x)
     normed = x * scale
     x_grad_ref[...] = grad_ref[...] + norm_back(grad_one * gain_ref[...], normed, scale)
-    out_ref[...] = (resid_ref[...] + summed(out_refs)).astype(LOW)
+    parts = [(r[0] if len(r.shape) == 3 else r[r.shape[0] - micro * rows :, :]).astype(WIDE) for r in out_refs]
+    out_ref[...] = (resid_ref[...] + sum(parts)).astype(LOW)
 
 
 def last(place, gain, x, grad, resid, one, one_got, out_list):
@@ -826,12 +872,8 @@
     )
 
 
-LOW_ORDER = (0, 2, 1, 3)
-
-
-def feed_finish_kernel(parts_f, fast, place_ref, *refs):
-    pair_refs, low_refs = refs[:fast], refs[fast : 2 * fast]
-    gate_ref, up_ref, down_ref, pack_ref = refs[2 * fast :]
+def pair_finish_kernel(parts_f, fast, place_ref, *refs):
+    pair_refs, (gate_ref, up_ref) = refs[:fast], refs[fast:]
     _, rows, double = pair_refs[0].shape
     cols = double // 2
     piece = cols // parts_f
@@ -852,38 +894,39 @@
                             def _():
                                 ref[at, (k * fast + l) * piece : (k * fast + l + 1) * piece] = value
 
-            at = pl.ds(pl.multiple_of((place_ref[0] ^ LOW_ORDER[d]) * rows, 8), rows)
+
+def low_finish_kernel(parts_f, fast, place_ref, *refs):
+    low_refs, (down_ref, pack_ref) = refs[:fast], refs[fast:]
+    _, rows, cols = low_refs[0].shape
+    piece = cols // parts_f
+    for j in range(fast):
+        for d in range(GROUPS):
+            at = pl.ds(pl.multiple_of(lax.rem(place_ref[0] + GROUPS - d, GROUPS) * rows, 8), rows)
             pack_ref[at, :] = low_refs[j][d].astype(WIDE)
         for r, c, to_r, to_c, n, w in packing(piece, rows * GROUPS):
-            at = pl.ds(pl.multiple_of(other * piece + r, 8), n)
+            at = pl.ds(pl.multiple_of((place_ref[1] ^ j) * piece + r, 8), n)
             down_ref[at, c : c + w] = pack_ref[to_r : to_r + n, to_c : to_c + w]
 
 
-def feed_finish(place, pair_packs, low_packs, parts_f):
-    fast = len(pair_packs)
-    _, rows, double = pair_packs[0].shape
-    cols = double // 2
-    piece = cols // parts_f
+def low_finish(place, packs, parts_f):
+    fast = len(packs)
+    _, rows, cols = packs[0].shape
     return call(
-        functools.partial(feed_finish_kernel, parts_f, fast),
-        "feed_finish",
-        place,
-        [*pair_packs, *low_packs],
-        [
-            shaped(rows * GROUPS, cols * fast, dtype=WIDE),
-            shaped(rows * GROUPS, cols * fast, dtype=WIDE),
-            shaped(piece * fast, rows * GROUPS * parts_f, dtype=WIDE),
-        ],
+        functools.partial(low_finish_kernel, parts_f, fast),
+        "low_finish",
+        place,
+        packs,
+        [shaped(cols // parts_f * fast, rows * GROUPS * parts_f, dtype=WIDE)],
         [pltpu.VMEM((rows * GROUPS, cols), WIDE)],
-    )
+    )[0]
 
 
 def input_finish_kernel(fast, place_ref, *refs):
-    pack_refs, out_refs = refs[:fast], refs[fast : 2 * fast]
-    query_ref, key_ref, value_ref, out_ref = refs[2 * fast :]
+    pack_refs = refs[:fast]
+    query_ref, key_ref, value_ref, out_ref = refs[fast:]
     rows = pack_refs[0].shape[0]
     for j in range(fast):
-        value = out_refs[j][...].astype(WIDE)
+        value = pack_refs[j][:, GROUPS * 640 :].astype(WIDE)
 
         def place_out(at):
             out_ref[at, :] = value
@@ -908,14 +951,22 @@
                 with_rows(place_ref[1] ^ j, rows, fast, place_in)
 
 
-def input_finish(place, packs, out_all, width):
+def most_finish_kernel(parts_f, fast, place_ref, *refs):
+    pair_refs, pack_refs, refs = refs[:fast], refs[fast : 2 * fast], refs[2 * fast :]
+    pair_finish_kernel(parts_f, fast, place_ref, *pair_refs, *refs[:2])
+    input_finish_kernel(fast, place_ref, *pack_refs, *refs[2:])
+
+
+def most_finish(place, pair_packs, packs, parts_f, width):
     fast = len(packs)
+    _, rows, double = pair_packs[0].shape
     return call(
-        functools.partial(input_finish_kernel, fast),
-        "input_finish",
-        place,
-        [*packs, *out_all],
-        [shaped(packs[0].shape[0] * fast, width, dtype=WIDE)] * 4,
+        functools.partial(most_finish_kernel, parts_f, fast),
+        "most_finish",
+        place,
+        [*pair_packs, *packs],
+        [shaped(rows * GROUPS, double // 2 * fast, dtype=WIDE)] * 2
+        + [shaped(packs[0].shape[0] * fast, width, dtype=WIDE)] * 4,
     )
 
 
@@ -1037,7 +1088,9 @@
     for j in range(2, fast, 2):
         g_have[j + 1] = hop(g_have[j], "ctx", 1)
     g_slots = [g_have[j] for j in range(fast)]
-    resid, act_two = joined(tick[0], gain_two, own_x, o_slots, out_w_slots)
+    w_rel = arrange(tick[0], out_w_slots)
+    o_slots, w_rel = fence(o_slots, w_rel)
+    resid, act_two = joined(tick[0], gain_two, own_x, o_slots, w_rel)
     act_two, g_slots = fence(act_two, g_slots)
     act_slots = slots_out(act_two, "ctx", fast)
     two_parts, out_parts, hid, grads = feed(tick[0], act_slots, g_slots, pair_slots, down_slots)
@@ -1046,105 +1099,126 @@
     two_odd = two_parts[2]
     two_got = hop(two_odd, "ctx", 1)
     pair_keep, *pair_sends = pair_grads(tick[0], act_slots, grads, parts_f)
-    two_got, pair_keep, pair_sends = fence(two_got, pair_keep, pair_sends)
+    out_got_one = hop(out_parts[2], "ctx", 1)
+    two_got, pair_keep, pair_sends, out_got_one = fence(two_got, pair_keep, pair_sends, out_got_one)
     pair_got = to_f(pair_sends)
     two_list, sent = pairs_on(two_parts, two_got, fast)
     low_keep, *low_sends = down_grads(fence(tick[0], sent)[0], g_slots, hid, parts_f)
     got, low_keep, low_sends = fence([v for v, _ in two_list], low_keep, low_sends)
     two_list = [(v, first) for v, (_, first) in zip(got, two_list)]
     grad_resid, grad_low, gain_two_part, do_own = branch(
-        tick[0], gain_two, resid, g_low, two_list, out_w_slots, micro
+        tick[0], gain_two, resid, g_low, two_list, w_rel, micro
     )
     do_own = fence(*do_own)
     do_slots = [do_own[0]] + shifted(do_own[1:], 1)
     out_keep, out_send = out_grads(tick[0], grad_low, o_slots, parts_f, fast)
-    out_send, pair_got = fence(out_send, pair_got)
+    out_keep, out_send, do_slots, pair_got = fence(out_keep, out_send, do_slots, pair_got)
+    out_got = hop(out_send, "ctx", 1)
     pair_own, pair_sends = group_split(tick[0], [pair_keep, *pair_got])
-    pair_own, pair_sends, low_sends, do_slots = fence(pair_own, pair_sends, low_sends, do_slots)
+    pair_own, pair_sends, low_sends, out_total = fence(
+        pair_own, pair_sends, low_sends, out_keep + out_got.astype(WIDE)
+    )
 
     pair_parts = shifted(pair_sends, 1)
     low_got = to_f(low_sends)
-    out_got = hop(out_send, "ctx", 1)
+    out_total = halve(out_total, "fsdp", 1)
     dq, dkv_parts, table_part = attention_backward(
         places, tick[0], strip, q, kv_slots, do_slots, lse, blocks
     )
-    dq, dkv_parts, pair_parts, low_got, out_got = fence(dq, dkv_parts, pair_parts, low_got, out_got)
+    dq, dkv_parts, pair_parts, low_got, out_total = fence(dq, dkv_parts, pair_parts, low_got, out_total)
     dkv_list, sent = pairs_on(dkv_parts, hop(dkv_parts[2], "ctx", 1), fast)
-    pair_chunk, out_chunk, _ = fence(groups_sum(pair_own, pair_parts), out_keep + out_got.astype(WIDE), sent)
+    low_keep, low_send = group_halves(tick[0], [low_keep, *low_got])
+    pair_chunk, low_send, out_total, _ = fence(groups_sum(pair_own, pair_parts), low_send, out_total, sent)
     pair_spread = spread_groups(pair_chunk)
-    out_chunk = halve(out_chunk, "fsdp", 1)
-    low_keep, low_send = group_halves(tick[0], [low_keep, *low_got])
-    got, pair_spread, out_chunk, low_send = fence([v for v, _ in dkv_list], pair_spread, out_chunk, low_send)
+    if fast == 4:
+        out_far = (out_parts[1][0].astype(WIDE) + out_got_one[1].astype(WIDE)).astype(LOW)
+        far = jnp.concatenate([out_total[1].astype(LOW), out_far])
+        far = hop(far, "ctx", 2)
+    got = fence([v for v, _ in dkv_list])
     dkv_list = [(v, first) for v, (_, first) in zip(got, dkv_list)]
-
-    low_got = hop(low_send, "ctx", fast)
-    out_chunk = halve(out_chunk, "ctx", 2)
     one_keep, one_send, gain_one_part, in_keep, in_send = input_grads(
         tick[0], act_one, dq, x_slots, dkv_list, qkv_slots, fast
     )
-    one_keep, one_send, in_keep, in_send, low_got, out_chunk = fence(
-        one_keep, one_send, in_keep, in_send, low_got, out_chunk
-    )
+    one_keep, one_send, in_keep, in_send, low_send, pair_spread = fence(
+        one_keep, one_send, in_keep, in_send, low_send, pair_spread
+    )
+    if fast == 4:
+        far = fence(far)
+        chunk = out_total.shape[1]
+        out_low = (out_total[0] + far[:chunk].astype(WIDE)).astype(LOW)
+        out_list = [(out_parts[0], False), (out_got_one, True), (far, False)]
+    else:
+        out_low = halve(out_total, "ctx", 2).astype(LOW)
+        out_list, _ = pairs_on(out_parts, out_got_one, fast)
+
+    def send_small(v, small, bit):
+        high = small.astype(LOW)
+        rest = (small - high.astype(WIDE)).astype(LOW)
+        return hop(jnp.concatenate([v, high, rest]), "ctx", bit), high.astype(WIDE) + rest.astype(WIDE)
+
+    def take_small(got, own):
+        lines = own.shape[0]
+        count = got.shape[0] - 2 * lines
+        return got[:count], own + got[count : count + lines].astype(WIDE) + got[count + lines :].astype(WIDE)
+
+    def two_hops(a, b, bit):
+        if a.shape[:-1] != b.shape[:-1]:
+            return hop(a, "ctx", bit), hop(b, "ctx", bit)
+        got = hop(jnp.concatenate([a, b], axis=-1), "ctx", bit)
+        return got[..., : a.shape[-1]], got[..., a.shape[-1] :]
+
+    head_count = bias_table.shape[1]
+    table_row = table_part[:, :head_count].reshape(1, -1)
+    table_row = jnp.pad(table_row, ((0, 5), (0, width - table_row.shape[1])))
+    small = jnp.concatenate([gain_one_part, gain_two_part, table_row])
     in_got = hop(in_send, "ctx", 1)
-    pair_have = far_places(jnp.stack(pair_spread))
-    one_got = hop(one_send, "ctx", fast)
-    in_total = fence(in_keep + in_got.astype(WIDE))
+    out_two = jnp.stack([out_low[:, : width // 2], out_low[:, width // 2 :]])
+    low_got, out_got = two_hops(low_send, out_two, fast)
+    small = small + hop(small, "ctx", 1)
+    in_total, pair_send, small = fence(in_keep + in_got.astype(WIDE), jnp.stack(pair_spread), small)
+    in_total = halve(jnp.swapaxes(in_total, 0, 1), "ctx", 2)
+    for bit in bits_down(fast // 2):
+        small = small + hop(small, "ctx", 2 * bit)
+    in_total, low_got, out_got, small = fence(in_total, low_got, out_got, small)
     low_sum = low_keep + low_got.astype(WIDE)
-    low_got = hop(low_sum[1].astype(LOW), "ctx", 2 * fast)
-    in_total, low_got = fence(halve(in_total, "fsdp", 1), low_got)
-    low_two = (low_sum[0] + low_got.astype(WIDE)).astype(LOW)
-    low_two = jnp.stack([low_two, hop(low_two, "ctx", 2 * fast)])
-    in_chunk, pair_have, one_got, low_two = fence(
-        halve(in_total, "ctx", 2).astype(LOW), pair_have, one_got, low_two
-    )
-    in_spread = spread_groups(in_chunk)
-    low_got = hop(low_two, "ctx", fast)
-    small = jnp.concatenate([gain_one_part.reshape(-1, 128), gain_two_part.reshape(-1, 128), table_part], axis=0)
+    out_two = (out_two.astype(WIDE) + out_got.astype(WIDE)).astype(LOW)
+    out_low = jnp.concatenate([out_two[0], out_two[1]], axis=1)
+    low_got, out_got = two_hops(low_sum[1].astype(LOW), out_low, 2 * fast)
+    pair_have = far_places(pair_send)
     for bit in bits_up(parts_f):
         small = small + hop(small, "fsdp", bit)
-    small = small + hop(small, "ctx", 1)
-    in_pack, low_pack, small, one_sum, out_low, out_parts = fence(
-        jnp.concatenate(in_spread, axis=1),
-        jnp.concatenate([low_two, low_got]),
-        small,
-        one_keep + one_got.astype(WIDE),
-        out_chunk.astype(LOW),
-        out_parts,
-    )
+    in_chunk, small = fence(halve(in_total, "fsdp", 1).astype(LOW), small)
+    in_spread = spread_groups(in_chunk)
+    in_spread, low_got, out_got, pair_have = fence(in_spread, low_got, out_got, pair_have)
+    low_spread = spread_groups((low_sum[0] + low_got.astype(WIDE)).astype(LOW))
+    out_low = (out_low.astype(WIDE) + out_got.astype(WIDE)).astype(LOW)
+    in_pack, one_send = fence(jnp.concatenate([*in_spread, out_low], axis=1), one_send)
     in_have = far_places(in_pack)
-    out_got = hop(out_low, "ctx", fast)
-    small = small + hop(small, "ctx", fast)
-    low_have = far_places(low_pack)
-    out_low, small, one_send = fence(
-        (out_low.astype(WIDE) + out_got.astype(WIDE)).astype(LOW), small, one_sum[1].astype(LOW)
-    )
-    out_got = hop(out_low, "ctx", 2 * fast)
-    small = small + hop(small, "ctx", 2 * fast)
-    one_got = hop(one_send, "ctx", 2 * fast)
+    one_got, small = send_small(one_send.reshape(-1, width), small, fast)
+    low_spread, one_got, pair_have, in_have = fence(low_spread, one_got, pair_have, in_have)
+    one_got, small = take_small(one_got, small)
+    one_got = one_got.reshape(one_keep.shape)
+    one_sum = one_keep[0] + one_got[0].astype(WIDE)
+    one_got, small = send_small((one_keep[1] + one_got[1].astype(WIDE)).astype(LOW), small, 2 * fast)
+    low_have = far_places(jnp.stack(low_spread))
     pair_packs = both_cores(pair_have)
-    out_chunk, small, in_have, low_have, pair_packs = fence(
-        (out_low.astype(WIDE) + out_got.astype(WIDE)).astype(LOW), small, in_have, low_have, pair_packs
-    )
+    in_packs, pair_packs = fence(both_cores(in_have), pair_packs)
+    w_gate_grad, w_up_grad, w_query_grad, w_key_grad, w_value_grad, w_out_grad = most_finish(
+        tick[0], pair_packs, in_packs, parts_f, width
+    )
+    w_query_grad, one_got, low_have = fence(w_query_grad, one_got, low_have)
     low_packs = both_cores(low_have)
-    in_packs = both_cores(in_have)
-    out_have = far_places(out_chunk)
-    for bit in bits_down(fast // 2):
-        small = small + hop(small, "ctx", 2 * bit)
-    w_gate_grad, w_up_grad, w_down_grad = feed_finish(tick[0], pair_packs, low_packs, parts_f)
-    w_gate_grad, in_packs, out_have, small, one_got = fence(w_gate_grad, in_packs, out_have, small, one_got)
-    out_all = both_cores(out_have)
-    out_list, _ = pairs_back(*out_parts, fast)
-    x_grad, result = last(tick[0], gain_one, own_x, grad_resid, resid, one_sum[0], one_got, out_list)
-    x_grad, out_all = fence(x_grad, out_all)
-    w_query_grad, w_key_grad, w_value_grad, w_out_grad = input_finish(tick[0], in_packs, out_all, width)
-    head_count = bias_table.shape[1]
-
-    lines = width // 128
+    x_grad, result = last(tick[0], gain_one, own_x, grad_resid, resid, one_sum, one_got, out_list)
+    x_grad, low_packs = fence(x_grad, low_packs)
+    w_down_grad = low_finish(tick[0], low_packs, parts_f)
+    small = take_small(one_got, small)[1]
+
     gain_rows = width // parts_f
     table_rows = bias_table.shape[0] // parts_f
-    gain_one_grad = lax.dynamic_slice_in_dim(small[:lines].reshape(width), f * gain_rows, gain_rows)
-    gain_two_grad = lax.dynamic_slice_in_dim(small[lines : 2 * lines].reshape(width), f * gain_rows, gain_rows)
-    table_grad = lax.dynamic_slice(small, (2 * lines + f * table_rows, 0), (table_rows, head_count))
+    gain_one_grad = lax.dynamic_slice_in_dim(small[0], f * gain_rows, gain_rows)
+    gain_two_grad = lax.dynamic_slice_in_dim(small[1], f * gain_rows, gain_rows)
+    table_grad = small[2, : bias_table.size].reshape(bias_table.shape)
+    table_grad = lax.dynamic_slice_in_dim(table_grad, f * table_rows, table_rows)
 
     return (
         result.reshape(micro, 1, block_rows, width),

time: 294 us -> 286 us (0.973)
  waiting for transfers between devices: 102 us -> 98.5 us
    ppermute x52 -> x42, waiting for transfers between devices: 73.9 us -> 68.3 us  [hop(): return lax.ppermute(v, axis, [(i, i ^ bit) for i in range(size)])]
    ppermute x52 -> x42, starting transfers between devices: 38.7 us -> 33.3 us  [hop(): return lax.ppermute(v, axis, [(i, i ^ bit) for i in range(size)])]
    ppermute x18 -> x21, starting transfers between devices: 32.2 us -> 37.1 us  [shift(): lax.ppermute(v, 'ctx', [(i, (i + steps * stride) % size) for i in range(s...]
    ppermute x18 -> x21, waiting for transfers between devices: 27.9 us -> 30.2 us  [shift(): lax.ppermute(v, 'ctx', [(i, (i + steps * stride) % size) for i in range(s...]
    unnamed x136 -> x114, local copies, waits for them, and re-layouts: 10.3 us -> 9.1 us
    pallas_call x13 -> x14, Pallas kernels: 56.3 us -> 57.5 us  [call(): pl.pallas_call(kernel, out_shape=tuple(out_shape), **grid, in_specs=specs...]
  transfers between devices with their start and end apart: 70 -> 63, of which waited for: 27 -> 20; matrix products, arithmetic and copies ran while one was open for 7% -> 6% of each run, Pallas kernels for 25% -> 25%
where the time goes in v1:
time: 286 us
  waiting for transfers between devices  98.5 us (34%)
  Pallas kernels  87.9 us (31%)
  starting transfers between devices  70.4 us (25%)
  local copies, waits for them, and re-layouts  20 us (7%)
  other arithmetic  7.28 us (3%)
    ppermute x42, waiting for transfers between devices, hop(): return lax.ppermute(v, axis, [(i, i ^ bit) for i in range(size)])  68.3 us
    pallas_call x14, Pallas kernels, call(): pl.pallas_call(kernel, out_shape=tuple(out_shape), **grid, in_specs=specs...  57.5 us
    ppermute x21, starting transfers between devices, shift(): lax.ppermute(v, 'ctx', [(i, (i + steps * stride) % size) for i in range(s...  37.1 us
    ppermute x42, starting transfers between devices, hop(): return lax.ppermute(v, axis, [(i, i ^ bit) for i in range(size)])  33.3 us
    ppermute x21, waiting for transfers between devices, shift(): lax.ppermute(v, 'ctx', [(i, (i + steps * stride) % size) for i in range(s...  30.2 us
    pallas_call x1, Pallas kernels, attention_backward(): pl.pallas_call(functools.partial(backward_kernel, count, blocks), out_sha...  16.4 us
    pallas_call x1, Pallas kernels, attention_forward(): pl.pallas_call(functools.partial(forward_kernel, count, blocks), out_shap...  10.1 us
    unnamed x114, local copies, waits for them, and re-layouts  9.1 us
  transfers between devices with their start and end apart: 63, of which 20 were waited for; matrix products, arithmetic and copies ran while one was open for 6% of the time, Pallas kernels for 25%

profile of v1, /device:TPU:0, one launch (start us, length us, event | category | flops | bytes accessed | tf_op | source)
XLA Modules:
  0.0 285.5 jit_solution(16620851388438476567)
XLA Ops:
  16.0 3.9 %bias_strip.1.strip_ref = f32[3,2048,128]{2,1,0:T(8,128)} custom-call(f32[32,3]{1,0:T(8,128)} %copy.42.table_ref), custom_call_target="tpu_custom_call" | custom-call | tf_op jit(solution)/shard_map/bias_strip/pallas_call | solution.py:126
  21.8 4.0 %collective-permute-done.1.refs_2_ = bf16[3,64,768]{2,1,0:T(8,128)(2,1)} collective-permute-done((bf16[3,64,768]{2,1,0:T(8,128)(2,1)}, bf16[3,64,768]{2,1,0:T(8,128)(2,1)}, u32[]{:S(2)}, u32[]{:S(2)}) %collective-permute-start.1) | collective-permute-done | bytes 294944 | tf_op jit(solution)/shard_map/ppermute | solution.py:60
  25.9 3.7 %project.1 = (bf16[4,192,768]{2,1,0:T(8,128)(2,1)}, bf16[4,3,64,256]{3,2,1,0:T(8,128)(2,1)}, bf16[4,3,64,384]{3,2,1,0:T(8,128)(2,1)}) custom-call(s32[3]{0:T(128)} %pad_add_fusion.place_ref, f32[1,768]{1,0:T(1,128)} %reshape.157.gain_ref, bf16[3,64,768]{2,1,0:T(8,128)(2,1)} %bitcast.76, bf16[3,64,768]{2,1,0:T(8,128)(2,1)} %collective-permute-done.refs_1_, ...), custom_call_target="tpu_custom_call" | custom-call | flops 754974720 | bytes 4328448 | tf_op jit(solution)/shard_map/project/pallas_call | solution.py:418
  31.1 13.9 %collective-permute-done.5.refs_2_.refs_6_ = bf16[4,3,64,384]{3,2,1,0:T(8,128)(2,1)} collective-permute-done((bf16[4,3,64,384]{3,2,1,0:T(8,128)(2,1)}, bf16[4,3,64,384]{3,2,1,0:T(8,128)(2,1)}, u32[]{:S(2)}, u32[]{:S(2)}) %collective-permute-start.5) | collective-permute-done | bytes 589856 | tf_op jit(solution)/shard_map/ppermute | solution.py:43
  49.1 10.1 %attention_forward.1 = (bf16[3,64,256]{2,1,0:T(8,128)(2,1)}, bf16[3,64,256]{2,1,0:T(8,128)(2,1)}, bf16[3,64,256]{2,1,0:T(8,128)(2,1)}, bf16[3,64,256]{2,1,0:T(8,128)(2,1)}, f32[3,3,256]{2,1,0:T(4,128)}) custom-call(s32[3,4]{1,0:T(4,128)} %bitcast.97, s32[3,4,4]{2,1,0:T(4,128)} %copy-done.40, f32[3,2048,128]{2,1,0:T(8,128)} %bias_strip.1.strip_ref, ...), custom_call_target="tpu_custom_call" | custom-call | flops 2415919104 | bytes 4718592 | tf_op jit(solution)/shard_map/attention_forward/pallas_call | solution.py:217
  63.1 6.8 %collective-permute-start.10 = (bf16[3,64,256]{2,1,0:T(8,128)(2,1)}, bf16[3,64,256]{2,1,0:T(8,128)(2,1)S(1)}, u32[]{:S(2)}, u32[]{:S(2)}) collective-permute-start(bf16[3,64,256]{2,1,0:T(8,128)(2,1)} %get-tuple-element.257), channel_id=1, source_target_pairs={{0,24},{2,26},{4,28},{6,30},{8,0},{10,2},{12,4},{14,6},{16,8},{18,... | collective-permute-start | bytes 294920 | tf_op jit(solution)/shard_map/ppermute | solution.py:60
  74.6 6.2 %collective-permute-done.11.refs_2_ = bf16[3,64,256]{2,1,0:T(8,128)(2,1)S(1)} collective-permute-done((bf16[3,64,256]{2,1,0:T(8,128)(2,1)}, bf16[3,64,256]{2,1,0:T(8,128)(2,1)S(1)}, u32[]{:S(2)}, u32[]{:S(2)}) %collective-permute-start.11) | collective-permute-done | bytes 98336 | tf_op jit(solution)/shard_map/ppermute | solution.py:60
  87.3 6.5 %collective-permute-done.15.refs_2_ = bf16[192,768]{1,0:T(8,128)(2,1)S(1)} collective-permute-done((bf16[192,768]{1,0:T(8,128)(2,1)}, bf16[192,768]{1,0:T(8,128)(2,1)S(1)}, u32[]{:S(2)}, u32[]{:S(2)}) %collective-permute-start.15) | collective-permute-done | bytes 294944 | tf_op jit(solution)/shard_map/ppermute | solution.py:43
  93.8 3.1 %collective-permute-done.18.refs_11_ = bf16[256,768]{1,0:T(8,128)(2,1)S(1)} collective-permute-done((bf16[256,768]{1,0:T(8,128)(2,1)S(1)}, bf16[256,768]{1,0:T(8,128)(2,1)S(1)}, u32[]{:S(2)}, u32[]{:S(2)}) %collective-permute-start.18) | collective-permute-done | bytes 393248 | tf_op jit(solution)/shard_map/ppermute | solution.py:43
  98.5 7.9 %feed.1 = (f32[192,768]{1,0:T(8,128)}, bf16[1,192,768]{2,1,0:T(8,128)(2,1)}, bf16[2,192,768]{2,1,0:T(8,128)(2,1)}, f32[192,768]{1,0:T(8,128)}, bf16[1,192,768]{2...) custom-call(s32[3]{0:T(128)} %pad_add_fusion.place_ref, ...), custom_call_target="tpu_custom_call" | custom-call | flops 3623878656 | bytes 10027008 | tf_op jit(solution)/shard_map/feed/pallas_call | solution.py:418
  106.9 4.7 %pair_grads.1 = (f32[384,1024]{1,0:T(8,128)}, bf16[384,1024]{1,0:T(8,128)(2,1)}) custom-call(s32[3]{0:T(128)} %pad_add_fusion.place_ref, bf16[192,768]{1,0:T(8,128)(2,1)} %get-tuple-element.273.refs_0_, bf16[192,768]{1,0:T(8,128)(2,1)} %copy-done.49, bf16[192,768]{1,0:T(8,128)(2,1)} %copy-done.48, bf16[192,768]{1,0:T(8,128)(2,1)} %copy-done.50, ...), custom_call_target="tpu_custom_call" | custom-call | flops 1207959552 | bytes 5111808 | tf_op jit(solution)/shard_map/pair_grads/pallas_call | solution.py:418
  112.9 3.4 %down_grads.1 = (f32[384,512]{1,0:T(8,128)}, bf16[384,512]{1,0:T(8,128)(2,1)}) custom-call(s32[3]{0:T(128)} %pad_add_fusion.place_ref, bf16[192,768]{1,0:T(8,128)(2,1)} %bitcast.87, bf16[192,768]{1,0:T(8,128)(2,1)} %copy-done.46, bf16[192,768]{1,0:T(8,128)(2,1)} %collective-permute-done.8.refs_6_.refs_2_, bf16[192,768]{1,0:T(8,128)(2,1)} %copy-done.47, ...), custom_call_target="tpu_custom_call" | custom-call | flops 603979776 | bytes 3145728 | tf_op jit(solution)/shard_map/down_grads/pallas_call | solution.py:418
  116.4 4.8 %collective-permute-done.21.refs_2_ = bf16[192,768]{1,0:T(8,128)(2,1)S(1)} collective-permute-done((bf16[192,768]{1,0:T(8,128)(2,1)S(1)}, bf16[192,768]{1,0:T(8,128)(2,1)S(1)}, u32[]{:S(2)}, u32[]{:S(2)}) %collective-permute-start.21) | collective-permute-done | bytes 294944 | tf_op jit(solution)/shard_map/ppermute | solution.py:43
  121.8 3.6 %branch.1 = (f32[192,768]{1,0:T(8,128)}, bf16[192,768]{1,0:T(8,128)(2,1)}, f32[1,768]{1,0:T(1,128)}, bf16[3,64,256]{2,1,0:T(8,128)(2,1)}, bf16[3,64,256]{2,1,0:T...) custom-call(s32[3]{0:T(128)} %pad_add_fusion.place_ref, f32[1,768]{1,0:T(1,128)} %reshape.158.gain_ref, ...), custom_call_target="tpu_custom_call" | custom-call | flops 301989888 | bytes 5216256 | tf_op jit(solution)/shard_map/branch/pallas_call | solution.py:418
  147.0 16.4 %attention_backward.1 = (bf16[4,3,64,256]{3,2,1,0:T(8,128)(2,1)}, f32[4,3,64,384]{3,2,1,0:T(8,128)}, bf16[1,4,3,64,384]{4,3,2,1,0:T(8,128)(2,1)}, bf16[2,4,3,64,384]{4,3,2,1,0:T(8,128)(2,1)}, f32[32,128]{1,0:T(8,128)}) custom-call(s32[3,4]{1,0:T(4,128)} %bitcast.98, s32[3,4,4]{2,1,0:T(4,128)} %copy-done.40, s32[3]{0:T(128)} %pad_add_fusion.place_ref, ...), custom_call_target="tpu_custom_call" | custom-call | flops 6039797760 | bytes 9437184 | tf_op jit(solution)/shard_map/attention_backward/pallas_call | solution.py:354
  177.1 6.7 %collective-permute-done.33.refs_6_ = bf16[4,3,64,384]{3,2,1,0:T(8,128)(2,1)} collective-permute-done((bf16[4,3,64,384]{3,2,1,0:T(8,128)(2,1)S(1)}, bf16[4,3,64,384]{3,2,1,0:T(8,128)(2,1)}, u32[]{:S(2)}, u32[]{:S(2)}) %collective-permute-start.33) | collective-permute-done | bytes 589856 | tf_op jit(solution)/shard_map/ppermute | solution.py:43
  183.8 6.4 %input_grads.1 = (f32[2,192,768]{2,1,0:T(8,128)}, bf16[2,192,768]{2,1,0:T(8,128)(2,1)}, f32[1,768]{1,0:T(1,128)}, f32[2,2,96,640]{3,2,1,0:T(8,128)}, bf16[2,2,96,640]{3,2,1,0:T(8,128)(2,1)}) custom-call(s32[3]{0:T(128)} %pad_add_fusion.place_ref, bf16[4,192,768]{2,1,0:T(8,128)(2,1)} %get-tuple-element.358.act_ref, ...), custom_call_target="tpu_custom_call" | custom-call | flops 1509949440 | bytes 9931776 | tf_op jit(solution)/shard_map/input_grads/pallas_call | solution.py:418
  197.4 6.3 %collective-permute-done.41 = bf16[2,96,896]{2,1,0:T(8,128)(2,1)S(1)} collective-permute-done((bf16[2,96,896]{2,1,0:T(8,128)(2,1)S(1)}, bf16[2,96,896]{2,1,0:T(8,128)(2,1)S(1)}, u32[]{:S(2)}, u32[]{:S(2)}) %collective-permute-start.41) | collective-permute-done | bytes 344096 | tf_op jit(solution)/shard_map/ppermute | solution.py:43
  215.4 11.9 %collective-permute-done.48 = bf16[96,1280]{1,0:T(8,128)(2,1)S(1)} collective-permute-done((bf16[96,1280]{1,0:T(8,128)(2,1)S(1)}, bf16[96,1280]{1,0:T(8,128)(2,1)S(1)}, u32[]{:S(2)}, u32[]{:S(2)}) %collective-permute-start.48) | collective-permute-done | bytes 245792 | tf_op jit(solution)/shard_map/ppermute | solution.py:43
  237.7 13.2 %collective-permute-done.50 = bf16[96,512]{1,0:T(8,128)(2,1)S(1)} collective-permute-done((bf16[96,512]{1,0:T(8,128)(2,1)S(1)}, bf16[96,512]{1,0:T(8,128)(2,1)S(1)}, u32[]{:S(2)}, u32[]{:S(2)}) %collective-permute-start.50) | collective-permute-done | bytes 98336 | tf_op jit(solution)/shard_map/ppermute | solution.py:60
  259.3 7.7 %most_finish.1 = (f32[384,2048]{1,0:T(8,128)}, f32[384,2048]{1,0:T(8,128)}, f32[384,768]{1,0:T(8,128)}, f32[384,768]{1,0:T(8,128)}, f32[384,768]{1,0:T(8,128)}, /*index=5*/f32[384,768]{1,0:T(8,128)}) custom-call(s32[3]{0:T(128)} %pad_add_fusion.place_ref, bf16[4,96,1024]{2,1,0:T(8,128)(2,1)} %copy-done.2, ...), custom_call_target="tpu_custom_call" | custom-call | bytes 16711680 | tf_op jit(solution)/shard_map/most_finish/pallas_call | solution.py:418
  267.0 7.7 %collective-permute-done.59.refs_1_ = bf16[208,768]{1,0:T(8,128)(2,1)} collective-permute-done((bf16[208,768]{1,0:T(8,128)(2,1)}, bf16[208,768]{1,0:T(8,128)(2,1)}, u32[]{:S(2)}, u32[]{:S(2)}) %collective-permute-start.59) | collective-permute-done | bytes 319520 | tf_op jit(solution)/shard_map/ppermute | solution.py:43
  276.1 3.2 %last.1 = (f32[192,768]{1,0:T(8,128)}, bf16[192,768]{1,0:T(8,128)(2,1)}) custom-call(s32[3]{0:T(128)} %pad_add_fusion.place_ref, f32[1,768]{1,0:T(1,128)} %reshape.157.gain_ref, bf16[3,64,768]{2,1,0:T(8,128)(2,1)} %bitcast.79, f32[192,768]{1,0:T(8,128)} %get-tuple-element.433.grad_ref, f32[192,768]{1,0:T(8,128)} %get-tuple-element.302.resid_ref, ...), custom_call_target="tpu_custom_call" | custom-call | bytes 4893696 | tf_op jit(solution)/shard_map/last/pallas_call | solution.py:418
  282.0 3.5 %low_finish.1 = f32[1024,768]{1,0:T(8,128)} custom-call(s32[3]{0:T(128)} %pad_add_fusion.place_ref, bf16[4,96,512]{2,1,0:T(8,128)(2,1)} %copy-done.5, bf16[4,96,512]{2,1,0:T(8,128)(2,1)} %copy-done.21, bf16[4,96,512]{2,1,0:T(8,128)(2,1)} %copy-done.20, bf16[4,96,512]{2,1,0:T(8,128)(2,1)} %copy-done.22), custom_call_target="tpu_custom_call" | custom-call | bytes 4718592 | tf_op jit(solution)/shard_map/low_finish/pallas_call | solution.py:418
  (303 shorter events, 118.3 us)
Async XLA Ops:
  0.7 21.2 %collective-permute-start = (bf16[3,64,768]{2,1,0:T(8,128)(2,1)}, bf16[3,64,768]{2,1,0:T(8,128)(2,1)}, u32[]{:S(2)}, u32[]{:S(2)}) collective-permute-start(bf16[3,64,768]{2,1,0:T(8,128)(2,1)} %bitcast.73), channel_id=1, source_target_pairs={{0,8},{2,10},{4,12},{6,14},{8,16},{10,18},{12,20},{14,22},{16,24},... | collective-permute-start | bytes 884744 | tf_op jit(solution)/shard_map/ppermute | solution.py:60
  3.7 22.1 %collective-permute-start.1 = (bf16[3,64,768]{2,1,0:T(8,128)(2,1)}, bf16[3,64,768]{2,1,0:T(8,128)(2,1)}, u32[]{:S(2)}, u32[]{:S(2)}) collective-permute-start(bf16[3,64,768]{2,1,0:T(8,128)(2,1)} %bitcast.74), channel_id=1, source_target_pairs={{0,16},{2,18},{4,20},{6,22},{8,24},{10,26},{12,28},{14,30},{16,0},... | collective-permute-start | bytes 884744 | tf_op jit(solution)/shard_map/ppermute | solution.py:60
  6.3 19.5 %collective-permute-start.2 = (bf16[3,64,768]{2,1,0:T(8,128)(2,1)}, bf16[3,64,768]{2,1,0:T(8,128)(2,1)}, u32[]{:S(2)}, u32[]{:S(2)}) collective-permute-start(bf16[3,64,768]{2,1,0:T(8,128)(2,1)} %bitcast.75), channel_id=1, source_target_pairs={{0,24},{2,26},{4,28},{6,30},{8,0},{10,2},{12,4},{14,6},{16,8},{18,... | collective-permute-start | bytes 884744 | tf_op jit(solution)/shard_map/ppermute | solution.py:60
  61.6 23.6 %collective-permute-start.13 = (bf16[192,768]{1,0:T(8,128)(2,1)}, bf16[192,768]{1,0:T(8,128)(2,1)S(1)}, u32[]{:S(2)}, u32[]{:S(2)}) collective-permute-start(bf16[192,768]{1,0:T(8,128)(2,1)} %collective-permute-done.8.refs_6_.refs_2_), channel_id=1, source_target_pairs={{0,2},{2,0},{4,6},{6,4},{8,10},{10,8},{12,14},{14,12},{16,18},{18,... | collective-permute-start | bytes 884744 | tf_op jit(solution)/shard_map/ppermute | solution.py:43
  61.6 32.2 %collective-permute-start.17 = (bf16[384,1024]{1,0:T(8,128)(2,1)S(1)}, bf16[384,1024]{1,0:T(8,128)(2,1)S(1)}, u32[]{:S(2)}, u32[]{:S(2)}) collective-permute-start(bf16[384,1024]{1,0:T(8,128)(2,1)S(1)} %pad_maximum_fusion.refs_8_), channel_id=1, source_target_pairs={{0,1},{1,0},{2,3},{3,2},{4,5},{5,4},{6,7},{7,6},{8,9},{9,8},{10,11... | collective-permute-start | bytes 2359304 | tf_op jit(solution)/shard_map/ppermute | solution.py:43
  111.7 23.7 %collective-permute-start.25 = (bf16[384,1024]{1,0:T(8,128)(2,1)}, bf16[384,1024]{1,0:T(8,128)(2,1)S(1)}, u32[]{:S(2)}, u32[]{:S(2)}) collective-permute-start(bf16[384,1024]{1,0:T(8,128)(2,1)} %get-tuple-element.318), channel_id=1, source_target_pairs={{0,1},{1,0},{2,3},{3,2},{4,5},{5,4},{6,7},{7,6},{8,9},{9,8},{10,11... | collective-permute-start | bytes 2359304 | tf_op jit(solution)/shard_map/ppermute | solution.py:43
  140.2 23.2 %collective-permute-start.31 = (bf16[1,2,96,768]{3,2,1,0:T(8,128)(2,1)S(1)}, bf16[1,2,96,768]{3,2,1,0:T(8,128)(2,1)S(1)}, u32[]{:S(2)}, u32[]{:S(2)}) collective-permute-start(bf16[1,2,96,768]{3,2,1,0:T(8,128)(2,1)S(1)} %slice.226), channel_id=1, source_target_pairs={{0,1},{1,0},{2,3},{3,2},{4,5},{5,4},{6,7},{7,6},{8,9},{9,8},{10,11... | collective-permute-start | bytes 884744 | tf_op jit(solution)/shard_map/ppermute | solution.py:43
  141.8 21.7 %collective-permute-start.30 = (bf16[384,512]{1,0:T(8,128)(2,1)}, bf16[384,512]{1,0:T(8,128)(2,1)S(1)}, u32[]{:S(2)}, u32[]{:S(2)}) collective-permute-start(bf16[384,512]{1,0:T(8,128)(2,1)} %get-tuple-element.342), channel_id=1, source_target_pairs={{0,1},{1,0},{2,3},{3,2},{4,5},{5,4},{6,7},{7,6},{8,9},{9,8},{10,11... | collective-permute-start | bytes 1179656 | tf_op jit(solution)/shard_map/ppermute | solution.py:43
  142.3 21.2 %collective-permute-start.27 = (bf16[96,1024]{1,0:T(8,128)(2,1)}, bf16[96,1024]{1,0:T(8,128)(2,1)S(1)}, u32[]{:S(2)}, u32[]{:S(2)}) collective-permute-start(bf16[96,1024]{1,0:T(8,128)(2,1)} %get-tuple-element.339), channel_id=1, source_target_pairs={{0,8},{2,10},{4,12},{6,14},{8,16},{10,18},{12,20},{14,22},{16,24},... | collective-permute-start | bytes 589832 | tf_op jit(solution)/shard_map/ppermute | solution.py:60
  144.6 18.9 %collective-permute-start.28 = (bf16[96,1024]{1,0:T(8,128)(2,1)}, bf16[96,1024]{1,0:T(8,128)(2,1)S(1)}, u32[]{:S(2)}, u32[]{:S(2)}) collective-permute-start(bf16[96,1024]{1,0:T(8,128)(2,1)} %get-tuple-element.340), channel_id=1, source_target_pairs={{0,16},{2,18},{4,20},{6,22},{8,24},{10,26},{12,28},{14,30},{16,0},... | collective-permute-start | bytes 589832 | tf_op jit(solution)/shard_map/ppermute | solution.py:60
  145.3 18.2 %collective-permute-start.29 = (bf16[96,1024]{1,0:T(8,128)(2,1)}, bf16[96,1024]{1,0:T(8,128)(2,1)S(1)}, u32[]{:S(2)}, u32[]{:S(2)}) collective-permute-start(bf16[96,1024]{1,0:T(8,128)(2,1)} %get-tuple-element.341), channel_id=1, source_target_pairs={{0,24},{2,26},{4,28},{6,30},{8,0},{10,2},{12,4},{14,6},{16,8},{18,... | collective-permute-start | bytes 589832 | tf_op jit(solution)/shard_map/ppermute | solution.py:60
  171.5 21.2 %collective-permute-start.37 = (bf16[288,768]{1,0:T(8,128)(2,1)S(1)}, bf16[288,768]{1,0:T(8,128)(2,1)S(1)}, u32[]{:S(2)}, u32[]{:S(2)}) collective-permute-start(bf16[288,768]{1,0:T(8,128)(2,1)S(1)} %pad_maximum_fusion.3), channel_id=1, source_target_pairs={{0,4},{2,6},{4,0},{6,2},{8,12},{10,14},{12,8},{14,10},{16,20},{18,... | collective-permute-start | bytes 1327112 | tf_op jit(solution)/shard_map/ppermute | solution.py:43
  172.9 18.1 %collective-permute-start.34 = (bf16[96,1024]{1,0:T(8,128)(2,1)S(1)}, bf16[96,1024]{1,0:T(8,128)(2,1)S(1)}, u32[]{:S(2)}, u32[]{:S(2)}) collective-permute-start(bf16[96,1024]{1,0:T(8,128)(2,1)S(1)} %add_convert_fusion.3), channel_id=1, source_target_pairs={{0,8},{2,10},{4,12},{6,14},{8,16},{10,18},{12,20},{14,22},{16,24},... | collective-permute-start | bytes 589832 | tf_op jit(solution)/shard_map/ppermute | solution.py:60
  173.4 17.7 %collective-permute-start.35 = (bf16[96,1024]{1,0:T(8,128)(2,1)S(1)}, bf16[96,1024]{1,0:T(8,128)(2,1)S(1)}, u32[]{:S(2)}, u32[]{:S(2)}) collective-permute-start(bf16[96,1024]{1,0:T(8,128)(2,1)S(1)} %add_convert_fusion.3), channel_id=1, source_target_pairs={{0,16},{2,18},{4,20},{6,22},{8,24},{10,26},{12,28},{14,30},{16,0},... | collective-permute-start | bytes 589832 | tf_op jit(solution)/shard_map/ppermute | solution.py:60
  203.8 26.2 %collective-permute-start.49 = (bf16[4,96,1024]{2,1,0:T(8,128)(2,1)S(1)}, bf16[4,96,1024]{2,1,0:T(8,128)(2,1)S(1)}, u32[]{:S(2)}, u32[]{:S(2)}) collective-permute-start(bf16[4,96,1024]{2,1,0:T(8,128)(2,1)S(1)} %pad_maximum_fusion.1.refs_0_), channel_id=1, source_target_pairs={{0,4},{2,6},{4,0},{6,2},{8,12},{10,14},{12,8},{14,10},{16,20},{18,... | collective-permute-start | bytes 2359304 | tf_op jit(solution)/shard_map/ppermute | solution.py:43
  207.8 19.5 %collective-permute-start.48 = (bf16[96,1280]{1,0:T(8,128)(2,1)S(1)}, bf16[96,1280]{1,0:T(8,128)(2,1)S(1)}, u32[]{:S(2)}, u32[]{:S(2)}) collective-permute-start(bf16[96,1280]{1,0:T(8,128)(2,1)S(1)} %pad_maximum_fusion.6), channel_id=1, source_target_pairs={{0,16},{2,18},{4,20},{6,22},{8,24},{10,26},{12,28},{14,30},{16,0},... | collective-permute-start | bytes 737288 | tf_op jit(solution)/shard_map/ppermute | solution.py:43
  213.0 17.0 %collective-permute-start.46 = (bf16[96,640]{1,0:T(8,128)(2,1)S(1)}, bf16[96,640]{1,0:T(8,128)(2,1)S(1)}, u32[]{:S(2)}, u32[]{:S(2)}) collective-permute-start(bf16[96,640]{1,0:T(8,128)(2,1)S(1)} %fusion.10), channel_id=1, source_target_pairs={{0,16},{2,18},{4,20},{6,22},{8,24},{10,26},{12,28},{14,30},{16,0},... | collective-permute-start | bytes 368648 | tf_op jit(solution)/shard_map/ppermute | solution.py:60
  230.1 21.8 %collective-permute-start.54 = (bf16[96,3328]{1,0:T(8,128)(2,1)S(1)}, bf16[96,3328]{1,0:T(8,128)(2,1)}, u32[]{:S(2)}, u32[]{:S(2)}) collective-permute-start(bf16[96,3328]{1,0:T(8,128)(2,1)S(1)} %fusion.8.refs_4_), channel_id=1, source_target_pairs={{0,4},{2,6},{4,0},{6,2},{8,12},{10,14},{12,8},{14,10},{16,20},{18,... | collective-permute-start | bytes 1916936 | tf_op jit(solution)/shard_map/ppermute | solution.py:43
  230.8 21.2 %collective-permute-start.53 = (bf16[400,768]{1,0:T(8,128)(2,1)S(1)}, bf16[400,768]{1,0:T(8,128)(2,1)S(1)}, u32[]{:S(2)}, u32[]{:S(2)}) collective-permute-start(bf16[400,768]{1,0:T(8,128)(2,1)S(1)} %pad_maximum_fusion.2), channel_id=1, source_target_pairs={{0,8},{2,10},{4,12},{6,14},{8,0},{10,2},{12,4},{14,6},{16,24},{18,... | collective-permute-start | bytes 1843208 | tf_op jit(solution)/shard_map/ppermute | solution.py:43
  232.9 18.0 %collective-permute-start.50 = (bf16[96,512]{1,0:T(8,128)(2,1)S(1)}, bf16[96,512]{1,0:T(8,128)(2,1)S(1)}, u32[]{:S(2)}, u32[]{:S(2)}) collective-permute-start(bf16[96,512]{1,0:T(8,128)(2,1)S(1)} %fusion.7), channel_id=1, source_target_pairs={{0,8},{2,10},{4,12},{6,14},{8,16},{10,18},{12,20},{14,22},{16,24},... | collective-permute-start | bytes 294920 | tf_op jit(solution)/shard_map/ppermute | solution.py:60
  233.0 18.0 %collective-permute-start.51 = (bf16[96,512]{1,0:T(8,128)(2,1)S(1)}, bf16[96,512]{1,0:T(8,128)(2,1)S(1)}, u32[]{:S(2)}, u32[]{:S(2)}) collective-permute-start(bf16[96,512]{1,0:T(8,128)(2,1)S(1)} %fusion.7), channel_id=1, source_target_pairs={{0,16},{2,18},{4,20},{6,22},{8,24},{10,26},{12,28},{14,30},{16,0},... | collective-permute-start | bytes 294920 | tf_op jit(solution)/shard_map/ppermute | solution.py:60
  234.9 17.1 %collective-permute-start.52 = (bf16[96,512]{1,0:T(8,128)(2,1)S(1)}, bf16[96,512]{1,0:T(8,128)(2,1)S(1)}, u32[]{:S(2)}, u32[]{:S(2)}) collective-permute-start(bf16[96,512]{1,0:T(8,128)(2,1)S(1)} %fusion.7), channel_id=1, source_target_pairs={{0,24},{2,26},{4,28},{6,30},{8,0},{10,2},{12,4},{14,6},{16,8},{18,... | collective-permute-start | bytes 294920 | tf_op jit(solution)/shard_map/ppermute | solution.py:60
  252.0 22.6 %collective-permute-start.60 = (bf16[4,96,512]{2,1,0:T(8,128)(2,1)S(1)}, bf16[4,96,512]{2,1,0:T(8,128)(2,1)S(1)}, u32[]{:S(2)}, u32[]{:S(2)}) collective-permute-start(bf16[4,96,512]{2,1,0:T(8,128)(2,1)S(1)} %pad_maximum_fusion.4.refs_0_), channel_id=1, source_target_pairs={{0,4},{2,6},{4,0},{6,2},{8,12},{10,14},{12,8},{14,10},{16,20},{18,... | collective-permute-start | bytes 1179656 | tf_op jit(solution)/shard_map/ppermute | solution.py:43
  256.9 17.8 %collective-permute-start.59 = (bf16[208,768]{1,0:T(8,128)(2,1)}, bf16[208,768]{1,0:T(8,128)(2,1)}, u32[]{:S(2)}, u32[]{:S(2)}) collective-permute-start(bf16[208,768]{1,0:T(8,128)(2,1)} %pad_maximum_fusion.5), channel_id=1, source_target_pairs={{0,16},{2,18},{4,20},{6,22},{8,24},{10,26},{12,28},{14,30},{16,0},... | collective-permute-start | bytes 958472 | tf_op jit(solution)/shard_map/ppermute | solution.py:43
  (93 other events, 937.7 us)

commit v2 on v1

--- a/solution.py
+++ b/solution.py
@@ -1174,33 +1174,30 @@
     in_got = hop(in_send, "ctx", 1)
     out_two = jnp.stack([out_low[:, : width // 2], out_low[:, width // 2 :]])
     low_got, out_got = two_hops(low_send, out_two, fast)
-    small = small + hop(small, "ctx", 1)
-    in_total, pair_send, small = fence(in_keep + in_got.astype(WIDE), jnp.stack(pair_spread), small)
-    in_total = halve(jnp.swapaxes(in_total, 0, 1), "ctx", 2)
-    for bit in bits_down(fast // 2):
-        small = small + hop(small, "ctx", 2 * bit)
-    in_total, low_got, out_got, small = fence(in_total, low_got, out_got, small)
+    pair_have = far_places(jnp.stack(pair_spread))
+    one_got, small = send_small(one_send.reshape(-1, width), small, fast)
+    in_total = fence(in_keep + in_got.astype(WIDE))
+    in_total, low_got, out_got = fence(halve(in_total, "fsdp", 1), low_got, out_got)
     low_sum = low_keep + low_got.astype(WIDE)
     out_two = (out_two.astype(WIDE) + out_got.astype(WIDE)).astype(LOW)
     out_low = jnp.concatenate([out_two[0], out_two[1]], axis=1)
     low_got, out_got = two_hops(low_sum[1].astype(LOW), out_low, 2 * fast)
-    pair_have = far_places(pair_send)
-    for bit in bits_up(parts_f):
-        small = small + hop(small, "fsdp", bit)
-    in_chunk, small = fence(halve(in_total, "fsdp", 1).astype(LOW), small)
+    in_chunk, pair_have = fence(halve(in_total, "ctx", 2).astype(LOW), pair_have)
     in_spread = spread_groups(in_chunk)
-    in_spread, low_got, out_got, pair_have = fence(in_spread, low_got, out_got, pair_have)
+    in_spread, low_got, out_got, one_got = fence(in_spread, low_got, out_got, one_got)
     low_spread = spread_groups((low_sum[0] + low_got.astype(WIDE)).astype(LOW))
     out_low = (out_low.astype(WIDE) + out_got.astype(WIDE)).astype(LOW)
-    in_pack, one_send = fence(jnp.concatenate([*in_spread, out_low], axis=1), one_send)
-    in_have = far_places(in_pack)
-    one_got, small = send_small(one_send.reshape(-1, width), small, fast)
-    low_spread, one_got, pair_have, in_have = fence(low_spread, one_got, pair_have, in_have)
+    in_have = far_places(jnp.concatenate([*in_spread, out_low], axis=1))
     one_got, small = take_small(one_got, small)
     one_got = one_got.reshape(one_keep.shape)
     one_sum = one_keep[0] + one_got[0].astype(WIDE)
-    one_got, small = send_small((one_keep[1] + one_got[1].astype(WIDE)).astype(LOW), small, 2 * fast)
+    one_send = (one_keep[1] + one_got[1].astype(WIDE)).astype(LOW)
+    small = small + hop(small, "ctx", 1)
+    for bit in bits_up(parts_f):
+        small = small + hop(small, "fsdp", bit)
+    low_spread, one_send, pair_have, small = fence(low_spread, one_send, pair_have, small)
     low_have = far_places(jnp.stack(low_spread))
+    one_got, small = send_small(one_send, small, 2 * fast)
     pair_packs = both_cores(pair_have)
     in_packs, pair_packs = fence(both_cores(in_have), pair_packs)
     w_gate_grad, w_up_grad, w_query_grad, w_key_grad, w_value_grad, w_out_grad = most_finish(
@@ -1208,10 +1205,12 @@
     )
     w_query_grad, one_got, low_have = fence(w_query_grad, one_got, low_have)
     low_packs = both_cores(low_have)
+    small = take_small(one_got, small)[1]
+    for bit in bits_down(fast // 2):
+        small = small + hop(small, "ctx", 2 * bit)
     x_grad, result = last(tick[0], gain_one, own_x, grad_resid, resid, one_sum, one_got, out_list)
     x_grad, low_packs = fence(x_grad, low_packs)
     w_down_grad = low_finish(tick[0], low_packs, parts_f)
-    small = take_small(one_got, small)[1]
 
     gain_rows = width // parts_f
     table_rows = bias_table.shape[0] // parts_f

time: 286 us -> 279 us (0.976)
  waiting for transfers between devices: 98.5 us -> 93.5 us
    ppermute x21, waiting for transfers between devices: 30.2 us -> 24.9 us  [shift(): lax.ppermute(v, 'ctx', [(i, (i + steps * stride) % size) for i in range(s...]
    ppermute x42, starting transfers between devices: 33.3 us -> 29.4 us  [hop(): return lax.ppermute(v, axis, [(i, i ^ bit) for i in range(size)])]
    unnamed x114 -> x124, local copies, waits for them, and re-layouts: 9.1 us -> 9.49 us
  transfers between devices with their start and end apart: 63 -> 63, of which waited for: 20 -> 22; matrix products, arithmetic and copies ran while one was open for 6% -> 6% of each run, Pallas kernels for 25% -> 26%
where the time goes in v2:
time: 279 us; the launch traced here: 278 us
  waiting for transfers between devices  93.5 us (34%)
  Pallas kernels  87.9 us (32%)
  starting transfers between devices  67.9 us (24%)
  local copies, waits for them, and re-layouts  20.1 us (7%)
  other arithmetic  6.67 us (2%)
    ppermute x42, waiting for transfers between devices, hop(): return lax.ppermute(v, axis, [(i, i ^ bit) for i in range(size)])  68.7 us
    pallas_call x14, Pallas kernels, call(): pl.pallas_call(kernel, out_shape=tuple(out_shape), **grid, in_specs=specs...  57.6 us
    ppermute x21, starting transfers between devices, shift(): lax.ppermute(v, 'ctx', [(i, (i + steps * stride) % size) for i in range(s...  38.4 us
    ppermute x42, starting transfers between devices, hop(): return lax.ppermute(v, axis, [(i, i ^ bit) for i in range(size)])  29.4 us
    ppermute x21, waiting for transfers between devices, shift(): lax.ppermute(v, 'ctx', [(i, (i + steps * stride) % size) for i in range(s...  24.9 us
    pallas_call x1, Pallas kernels, attention_backward(): pl.pallas_call(functools.partial(backward_kernel, count, blocks), out_sha...  16.4 us
    pallas_call x1, Pallas kernels, attention_forward(): pl.pallas_call(functools.partial(forward_kernel, count, blocks), out_shap...  10.1 us
    unnamed x124, local copies, waits for them, and re-layouts  9.49 us
  transfers between devices with their start and end apart: 63, of which 22 were waited for; matrix products, arithmetic and copies ran while one was open for 6% of the time, Pallas kernels for 26%

profile of v2, /device:TPU:0, one launch (start us, length us, event | category | flops | bytes accessed | tf_op | source)
XLA Modules:
  0.0 277.7 jit_solution(12090992871752554003)
XLA Ops:
  16.0 3.9 %bias_strip.1.strip_ref = f32[3,2048,128]{2,1,0:T(8,128)} custom-call(f32[32,3]{1,0:T(8,128)} %copy.38.table_ref), custom_call_target="tpu_custom_call" | custom-call | tf_op jit(solution)/shard_map/bias_strip/pallas_call | solution.py:126
  21.8 4.0 %collective-permute-done.1.refs_2_ = bf16[3,64,768]{2,1,0:T(8,128)(2,1)} collective-permute-done((bf16[3,64,768]{2,1,0:T(8,128)(2,1)}, bf16[3,64,768]{2,1,0:T(8,128)(2,1)}, u32[]{:S(2)}, u32[]{:S(2)}) %collective-permute-start.1) | collective-permute-done | bytes 294944 | tf_op jit(solution)/shard_map/ppermute | solution.py:60
  25.9 3.7 %project.1 = (bf16[4,192,768]{2,1,0:T(8,128)(2,1)}, bf16[4,3,64,256]{3,2,1,0:T(8,128)(2,1)}, bf16[4,3,64,384]{3,2,1,0:T(8,128)(2,1)}) custom-call(s32[3]{0:T(128)} %pad_add_fusion.place_ref, f32[1,768]{1,0:T(1,128)} %reshape.157.gain_ref, bf16[3,64,768]{2,1,0:T(8,128)(2,1)} %bitcast.73, bf16[3,64,768]{2,1,0:T(8,128)(2,1)} %collective-permute-done.refs_1_, ...), custom_call_target="tpu_custom_call" | custom-call | flops 754974720 | bytes 4328448 | tf_op jit(solution)/shard_map/project/pallas_call | solution.py:418
  31.1 13.9 %collective-permute-done.5.refs_2_.refs_6_ = bf16[4,3,64,384]{3,2,1,0:T(8,128)(2,1)} collective-permute-done((bf16[4,3,64,384]{3,2,1,0:T(8,128)(2,1)}, bf16[4,3,64,384]{3,2,1,0:T(8,128)(2,1)}, u32[]{:S(2)}, u32[]{:S(2)}) %collective-permute-start.5) | collective-permute-done | bytes 589856 | tf_op jit(solution)/shard_map/ppermute | solution.py:43
  49.1 10.1 %attention_forward.1 = (bf16[3,64,256]{2,1,0:T(8,128)(2,1)}, bf16[3,64,256]{2,1,0:T(8,128)(2,1)}, bf16[3,64,256]{2,1,0:T(8,128)(2,1)}, bf16[3,64,256]{2,1,0:T(8,128)(2,1)}, f32[3,3,256]{2,1,0:T(4,128)}) custom-call(s32[3,4]{1,0:T(4,128)} %bitcast.94, s32[3,4,4]{2,1,0:T(4,128)} %copy-done.45, f32[3,2048,128]{2,1,0:T(8,128)} %bias_strip.1.strip_ref, ...), custom_call_target="tpu_custom_call" | custom-call | flops 2415919104 | bytes 4718592 | tf_op jit(solution)/shard_map/attention_forward/pallas_call | solution.py:217
  63.1 6.8 %collective-permute-start.10 = (bf16[3,64,256]{2,1,0:T(8,128)(2,1)}, bf16[3,64,256]{2,1,0:T(8,128)(2,1)S(1)}, u32[]{:S(2)}, u32[]{:S(2)}) collective-permute-start(bf16[3,64,256]{2,1,0:T(8,128)(2,1)} %get-tuple-element.250), channel_id=1, source_target_pairs={{0,24},{2,26},{4,28},{6,30},{8,0},{10,2},{12,4},{14,6},{16,8},{18,... | collective-permute-start | bytes 294920 | tf_op jit(solution)/shard_map/ppermute | solution.py:60
  74.6 6.2 %collective-permute-done.11.refs_2_ = bf16[3,64,256]{2,1,0:T(8,128)(2,1)S(1)} collective-permute-done((bf16[3,64,256]{2,1,0:T(8,128)(2,1)}, bf16[3,64,256]{2,1,0:T(8,128)(2,1)S(1)}, u32[]{:S(2)}, u32[]{:S(2)}) %collective-permute-start.11) | collective-permute-done | bytes 98336 | tf_op jit(solution)/shard_map/ppermute | solution.py:60
  87.3 6.5 %collective-permute-done.15.refs_2_ = bf16[192,768]{1,0:T(8,128)(2,1)S(1)} collective-permute-done((bf16[192,768]{1,0:T(8,128)(2,1)}, bf16[192,768]{1,0:T(8,128)(2,1)S(1)}, u32[]{:S(2)}, u32[]{:S(2)}) %collective-permute-start.15) | collective-permute-done | bytes 294944 | tf_op jit(solution)/shard_map/ppermute | solution.py:43
  98.5 7.9 %feed.1 = (f32[192,768]{1,0:T(8,128)}, bf16[1,192,768]{2,1,0:T(8,128)(2,1)}, bf16[2,192,768]{2,1,0:T(8,128)(2,1)}, f32[192,768]{1,0:T(8,128)}, bf16[1,192,768]{2...) custom-call(s32[3]{0:T(128)} %pad_add_fusion.place_ref, ...), custom_call_target="tpu_custom_call" | custom-call | flops 3623878656 | bytes 10027008 | tf_op jit(solution)/shard_map/feed/pallas_call | solution.py:418
  106.9 4.7 %pair_grads.1 = (f32[384,1024]{1,0:T(8,128)}, bf16[384,1024]{1,0:T(8,128)(2,1)}) custom-call(s32[3]{0:T(128)} %pad_add_fusion.place_ref, bf16[192,768]{1,0:T(8,128)(2,1)} %get-tuple-element.266.refs_0_, bf16[192,768]{1,0:T(8,128)(2,1)} %copy-done.54, bf16[192,768]{1,0:T(8,128)(2,1)} %copy-done.53, bf16[192,768]{1,0:T(8,128)(2,1)} %copy-done.55, ...), custom_call_target="tpu_custom_call" | custom-call | flops 1207959552 | bytes 5111808 | tf_op jit(solution)/shard_map/pair_grads/pallas_call | solution.py:418
  112.9 3.4 %down_grads.1 = (f32[384,512]{1,0:T(8,128)}, bf16[384,512]{1,0:T(8,128)(2,1)}) custom-call(s32[3]{0:T(128)} %pad_add_fusion.place_ref, bf16[192,768]{1,0:T(8,128)(2,1)} %bitcast.84, bf16[192,768]{1,0:T(8,128)(2,1)} %copy-done.51, bf16[192,768]{1,0:T(8,128)(2,1)} %collective-permute-done.8.refs_6_.refs_2_, bf16[192,768]{1,0:T(8,128)(2,1)} %copy-done.52, ...), custom_call_target="tpu_custom_call" | custom-call | flops 603979776 | bytes 3145728 | tf_op jit(solution)/shard_map/down_grads/pallas_call | solution.py:418
  116.3 4.8 %collective-permute-done.21.refs_2_ = bf16[192,768]{1,0:T(8,128)(2,1)S(1)} collective-permute-done((bf16[192,768]{1,0:T(8,128)(2,1)S(1)}, bf16[192,768]{1,0:T(8,128)(2,1)S(1)}, u32[]{:S(2)}, u32[]{:S(2)}) %collective-permute-start.21) | collective-permute-done | bytes 294944 | tf_op jit(solution)/shard_map/ppermute | solution.py:43
  121.8 3.6 %branch.1 = (f32[192,768]{1,0:T(8,128)}, bf16[192,768]{1,0:T(8,128)(2,1)}, f32[1,768]{1,0:T(1,128)}, bf16[3,64,256]{2,1,0:T(8,128)(2,1)}, bf16[3,64,256]{2,1,0:T...) custom-call(s32[3]{0:T(128)} %pad_add_fusion.place_ref, f32[1,768]{1,0:T(1,128)} %reshape.158.gain_ref, ...), custom_call_target="tpu_custom_call" | custom-call | flops 301989888 | bytes 5216256 | tf_op jit(solution)/shard_map/branch/pallas_call | solution.py:418
  146.9 16.4 %attention_backward.1 = (bf16[4,3,64,256]{3,2,1,0:T(8,128)(2,1)}, f32[4,3,64,384]{3,2,1,0:T(8,128)}, bf16[1,4,3,64,384]{4,3,2,1,0:T(8,128)(2,1)}, bf16[2,4,3,64,384]{4,3,2,1,0:T(8,128)(2,1)}, f32[32,128]{1,0:T(8,128)}) custom-call(s32[3,4]{1,0:T(4,128)} %bitcast.95, s32[3,4,4]{2,1,0:T(4,128)} %copy-done.45, s32[3]{0:T(128)} %pad_add_fusion.place_ref, ...), custom_call_target="tpu_custom_call" | custom-call | flops 6039797760 | bytes 9437184 | tf_op jit(solution)/shard_map/attention_backward/pallas_call | solution.py:354
  175.8 8.4 %collective-permute-done.33.refs_6_ = bf16[4,3,64,384]{3,2,1,0:T(8,128)(2,1)} collective-permute-done((bf16[4,3,64,384]{3,2,1,0:T(8,128)(2,1)S(1)}, bf16[4,3,64,384]{3,2,1,0:T(8,128)(2,1)}, u32[]{:S(2)}, u32[]{:S(2)}) %collective-permute-start.33) | collective-permute-done | bytes 589856 | tf_op jit(solution)/shard_map/ppermute | solution.py:43
  184.2 6.5 %input_grads.1 = (f32[2,192,768]{2,1,0:T(8,128)}, bf16[2,192,768]{2,1,0:T(8,128)(2,1)}, f32[1,768]{1,0:T(1,128)}, f32[2,2,96,640]{3,2,1,0:T(8,128)}, bf16[2,2,96,640]{3,2,1,0:T(8,128)(2,1)}) custom-call(s32[3]{0:T(128)} %pad_add_fusion.place_ref, bf16[4,192,768]{2,1,0:T(8,128)(2,1)} %get-tuple-element.351.act_ref, ...), custom_call_target="tpu_custom_call" | custom-call | flops 1509949440 | bytes 9931776 | tf_op jit(solution)/shard_map/input_grads/pallas_call | solution.py:418
  198.1 6.0 %collective-permute-done.40 = bf16[2,96,896]{2,1,0:T(8,128)(2,1)S(1)} collective-permute-done((bf16[2,96,896]{2,1,0:T(8,128)(2,1)S(1)}, bf16[2,96,896]{2,1,0:T(8,128)(2,1)S(1)}, u32[]{:S(2)}, u32[]{:S(2)}) %collective-permute-start.40) | collective-permute-done | bytes 344096 | tf_op jit(solution)/shard_map/ppermute | solution.py:43
  206.7 12.2 %collective-permute-done.41 = bf16[1,96,640]{2,1,0:T(8,128)(2,1)S(1)} collective-permute-done((bf16[1,96,640]{2,1,0:T(8,128)(2,1)S(1)}, bf16[1,96,640]{2,1,0:T(8,128)(2,1)S(1)}, u32[]{:S(2)}, u32[]{:S(2)}) %collective-permute-start.41) | collective-permute-done | bytes 122912 | tf_op jit(solution)/shard_map/ppermute | solution.py:43
  223.9 3.2 %collective-permute-done.43 = bf16[96,640]{1,0:T(8,128)(2,1)S(1)} collective-permute-done((bf16[96,640]{1,0:T(8,128)(2,1)S(1)}, bf16[96,640]{1,0:T(8,128)(2,1)S(1)}, u32[]{:S(2)}, u32[]{:S(2)}) %collective-permute-start.43) | collective-permute-done | bytes 122912 | tf_op jit(solution)/shard_map/ppermute | solution.py:60
  227.1 3.7 %collective-permute-done.44 = bf16[96,640]{1,0:T(8,128)(2,1)S(1)} collective-permute-done((bf16[96,640]{1,0:T(8,128)(2,1)S(1)}, bf16[96,640]{1,0:T(8,128)(2,1)S(1)}, u32[]{:S(2)}, u32[]{:S(2)}) %collective-permute-start.44) | collective-permute-done | bytes 122912 | tf_op jit(solution)/shard_map/ppermute | solution.py:60
  241.0 3.6 %collective-permute-done.49 = bf16[96,512]{1,0:T(8,128)(2,1)S(1)} collective-permute-done((bf16[96,512]{1,0:T(8,128)(2,1)S(1)}, bf16[96,512]{1,0:T(8,128)(2,1)S(1)}, u32[]{:S(2)}, u32[]{:S(2)}) %collective-permute-start.49) | collective-permute-done | bytes 98336 | tf_op jit(solution)/shard_map/ppermute | solution.py:60
  252.5 7.7 %most_finish.1 = (f32[384,2048]{1,0:T(8,128)}, f32[384,2048]{1,0:T(8,128)}, f32[384,768]{1,0:T(8,128)}, f32[384,768]{1,0:T(8,128)}, f32[384,768]{1,0:T(8,128)}, /*index=5*/f32[384,768]{1,0:T(8,128)}) custom-call(s32[3]{0:T(128)} %pad_add_fusion.place_ref, bf16[4,96,1024]{2,1,0:T(8,128)(2,1)} %copy-done.2, bf16[4,96,1024]{2,1,0:T(8,128)(2,1)} %copy-done.16, ...), custom_call_target="tpu_custom_call" | custom-call | bytes 16711680 | tf_op jit(solution)/shard_map/most_finish/pallas_call | solution.py:418
  260.1 6.5 %collective-permute-done.58.refs_1_ = bf16[208,768]{1,0:T(8,128)(2,1)S(1)} collective-permute-done((bf16[208,768]{1,0:T(8,128)(2,1)}, bf16[208,768]{1,0:T(8,128)(2,1)S(1)}, u32[]{:S(2)}, u32[]{:S(2)}) %collective-permute-start.58) | collective-permute-done | bytes 319520 | tf_op jit(solution)/shard_map/ppermute | solution.py:43
  274.1 3.5 %low_finish.1 = f32[1024,768]{1,0:T(8,128)} custom-call(s32[3]{0:T(128)} %pad_add_fusion.place_ref, bf16[4,96,512]{2,1,0:T(8,128)(2,1)} %copy-done.5, bf16[4,96,512]{2,1,0:T(8,128)(2,1)} %copy-done.24, bf16[4,96,512]{2,1,0:T(8,128)(2,1)} %copy-done.23, bf16[4,96,512]{2,1,0:T(8,128)(2,1)} %copy-done.25), custom_call_target="tpu_custom_call" | custom-call | bytes 4718592 | tf_op jit(solution)/shard_map/low_finish/pallas_call | solution.py:418
  (313 shorter events, 118.9 us)
Async XLA Ops:
  0.7 21.2 %collective-permute-start = (bf16[3,64,768]{2,1,0:T(8,128)(2,1)}, bf16[3,64,768]{2,1,0:T(8,128)(2,1)}, u32[]{:S(2)}, u32[]{:S(2)}) collective-permute-start(bf16[3,64,768]{2,1,0:T(8,128)(2,1)} %bitcast.70), channel_id=1, source_target_pairs={{0,8},{2,10},{4,12},{6,14},{8,16},{10,18},{12,20},{14,22},{16,24},... | collective-permute-start | bytes 884744 | tf_op jit(solution)/shard_map/ppermute | solution.py:60
  3.7 22.1 %collective-permute-start.1 = (bf16[3,64,768]{2,1,0:T(8,128)(2,1)}, bf16[3,64,768]{2,1,0:T(8,128)(2,1)}, u32[]{:S(2)}, u32[]{:S(2)}) collective-permute-start(bf16[3,64,768]{2,1,0:T(8,128)(2,1)} %bitcast.71), channel_id=1, source_target_pairs={{0,16},{2,18},{4,20},{6,22},{8,24},{10,26},{12,28},{14,30},{16,0},... | collective-permute-start | bytes 884744 | tf_op jit(solution)/shard_map/ppermute | solution.py:60
  6.3 19.5 %collective-permute-start.2 = (bf16[3,64,768]{2,1,0:T(8,128)(2,1)}, bf16[3,64,768]{2,1,0:T(8,128)(2,1)}, u32[]{:S(2)}, u32[]{:S(2)}) collective-permute-start(bf16[3,64,768]{2,1,0:T(8,128)(2,1)} %bitcast.72), channel_id=1, source_target_pairs={{0,24},{2,26},{4,28},{6,30},{8,0},{10,2},{12,4},{14,6},{16,8},{18,... | collective-permute-start | bytes 884744 | tf_op jit(solution)/shard_map/ppermute | solution.py:60
  31.1 16.0 %collective-permute-start.4 = (bf16[4,3,64,384]{3,2,1,0:T(8,128)(2,1)}, bf16[4,3,64,384]{3,2,1,0:T(8,128)(2,1)}, u32[]{:S(2)}, u32[]{:S(2)}) collective-permute-start(bf16[4,3,64,384]{3,2,1,0:T(8,128)(2,1)} %get-tuple-element.238.refs_0_.refs_4_), channel_id=1, source_target_pairs={{0,2},{2,0},{4,6},{6,4},{8,10},{10,8},{12,14},{14,12},{16,18},{18,... | collective-permute-start | bytes 1769480 | tf_op jit(solution)/shard_map/ppermute | solution.py:43
  45.1 15.8 %collective-permute-start.9 = (bf16[384,768]{1,0:T(8,128)(2,1)S(1)}, bf16[384,768]{1,0:T(8,128)(2,1)}, u32[]{:S(2)}, u32[]{:S(2)}) collective-permute-start(bf16[384,768]{1,0:T(8,128)(2,1)S(1)} %copy-done.22), channel_id=1, source_target_pairs={{0,1},{1,0},{2,3},{3,2},{4,5},{5,4},{6,7},{7,6},{8,9},{9,8},{10,11... | collective-permute-start | bytes 1769480 | tf_op jit(solution)/shard_map/ppermute | solution.py:43
  61.6 23.6 %collective-permute-start.13 = (bf16[192,768]{1,0:T(8,128)(2,1)}, bf16[192,768]{1,0:T(8,128)(2,1)S(1)}, u32[]{:S(2)}, u32[]{:S(2)}) collective-permute-start(bf16[192,768]{1,0:T(8,128)(2,1)} %collective-permute-done.8.refs_6_.refs_2_), channel_id=1, source_target_pairs={{0,2},{2,0},{4,6},{6,4},{8,10},{10,8},{12,14},{14,12},{16,18},{18,... | collective-permute-start | bytes 884744 | tf_op jit(solution)/shard_map/ppermute | solution.py:43
  61.6 32.2 %collective-permute-start.17 = (bf16[384,1024]{1,0:T(8,128)(2,1)S(1)}, bf16[384,1024]{1,0:T(8,128)(2,1)S(1)}, u32[]{:S(2)}, u32[]{:S(2)}) collective-permute-start(bf16[384,1024]{1,0:T(8,128)(2,1)S(1)} %pad_maximum_fusion.refs_8_), channel_id=1, source_target_pairs={{0,1},{1,0},{2,3},{3,2},{4,5},{5,4},{6,7},{7,6},{8,9},{9,8},{10,11... | collective-permute-start | bytes 2359304 | tf_op jit(solution)/shard_map/ppermute | solution.py:43
  111.7 23.7 %collective-permute-start.25 = (bf16[384,1024]{1,0:T(8,128)(2,1)}, bf16[384,1024]{1,0:T(8,128)(2,1)S(1)}, u32[]{:S(2)}, u32[]{:S(2)}) collective-permute-start(bf16[384,1024]{1,0:T(8,128)(2,1)} %get-tuple-element.311), channel_id=1, source_target_pairs={{0,1},{1,0},{2,3},{3,2},{4,5},{5,4},{6,7},{7,6},{8,9},{9,8},{10,11... | collective-permute-start | bytes 2359304 | tf_op jit(solution)/shard_map/ppermute | solution.py:43
  140.2 23.1 %collective-permute-start.31 = (bf16[1,2,96,768]{3,2,1,0:T(8,128)(2,1)S(1)}, bf16[1,2,96,768]{3,2,1,0:T(8,128)(2,1)S(1)}, u32[]{:S(2)}, u32[]{:S(2)}) collective-permute-start(bf16[1,2,96,768]{3,2,1,0:T(8,128)(2,1)S(1)} %slice.215), channel_id=1, source_target_pairs={{0,1},{1,0},{2,3},{3,2},{4,5},{5,4},{6,7},{7,6},{8,9},{9,8},{10,11... | collective-permute-start | bytes 884744 | tf_op jit(solution)/shard_map/ppermute | solution.py:43
  141.8 21.7 %collective-permute-start.30 = (bf16[384,512]{1,0:T(8,128)(2,1)}, bf16[384,512]{1,0:T(8,128)(2,1)S(1)}, u32[]{:S(2)}, u32[]{:S(2)}) collective-permute-start(bf16[384,512]{1,0:T(8,128)(2,1)} %get-tuple-element.335), channel_id=1, source_target_pairs={{0,1},{1,0},{2,3},{3,2},{4,5},{5,4},{6,7},{7,6},{8,9},{9,8},{10,11... | collective-permute-start | bytes 1179656 | tf_op jit(solution)/shard_map/ppermute | solution.py:43
  142.3 21.1 %collective-permute-start.27 = (bf16[96,1024]{1,0:T(8,128)(2,1)}, bf16[96,1024]{1,0:T(8,128)(2,1)S(1)}, u32[]{:S(2)}, u32[]{:S(2)}) collective-permute-start(bf16[96,1024]{1,0:T(8,128)(2,1)} %get-tuple-element.332), channel_id=1, source_target_pairs={{0,8},{2,10},{4,12},{6,14},{8,16},{10,18},{12,20},{14,22},{16,24},... | collective-permute-start | bytes 589832 | tf_op jit(solution)/shard_map/ppermute | solution.py:60
  144.5 18.9 %collective-permute-start.28 = (bf16[96,1024]{1,0:T(8,128)(2,1)}, bf16[96,1024]{1,0:T(8,128)(2,1)S(1)}, u32[]{:S(2)}, u32[]{:S(2)}) collective-permute-start(bf16[96,1024]{1,0:T(8,128)(2,1)} %get-tuple-element.333), channel_id=1, source_target_pairs={{0,16},{2,18},{4,20},{6,22},{8,24},{10,26},{12,28},{14,30},{16,0},... | collective-permute-start | bytes 589832 | tf_op jit(solution)/shard_map/ppermute | solution.py:60
  145.3 18.2 %collective-permute-start.29 = (bf16[96,1024]{1,0:T(8,128)(2,1)}, bf16[96,1024]{1,0:T(8,128)(2,1)S(1)}, u32[]{:S(2)}, u32[]{:S(2)}) collective-permute-start(bf16[96,1024]{1,0:T(8,128)(2,1)} %get-tuple-element.334), channel_id=1, source_target_pairs={{0,24},{2,26},{4,28},{6,30},{8,0},{10,2},{12,4},{14,6},{16,8},{18,... | collective-permute-start | bytes 589832 | tf_op jit(solution)/shard_map/ppermute | solution.py:60
  167.8 16.3 %collective-permute-start.33 = (bf16[4,3,64,384]{3,2,1,0:T(8,128)(2,1)S(1)}, bf16[4,3,64,384]{3,2,1,0:T(8,128)(2,1)}, u32[]{:S(2)}, u32[]{:S(2)}) collective-permute-start(bf16[4,3,64,384]{3,2,1,0:T(8,128)(2,1)S(1)} %fusion), channel_id=1, source_target_pairs={{0,4},{2,6},{4,0},{6,2},{8,12},{10,14},{12,8},{14,10},{16,20},{18,... | collective-permute-start | bytes 1769480 | tf_op jit(solution)/shard_map/ppermute | solution.py:43
  169.5 23.5 %collective-permute-start.37 = (bf16[288,768]{1,0:T(8,128)(2,1)}, bf16[288,768]{1,0:T(8,128)(2,1)S(1)}, u32[]{:S(2)}, u32[]{:S(2)}) collective-permute-start(bf16[288,768]{1,0:T(8,128)(2,1)} %pad_maximum_fusion.3), channel_id=1, source_target_pairs={{0,4},{2,6},{4,0},{6,2},{8,12},{10,14},{12,8},{14,10},{16,20},{18,... | collective-permute-start | bytes 1327112 | tf_op jit(solution)/shard_map/ppermute | solution.py:43
  170.8 19.9 %collective-permute-start.34 = (bf16[96,1024]{1,0:T(8,128)(2,1)S(1)}, bf16[96,1024]{1,0:T(8,128)(2,1)S(1)}, u32[]{:S(2)}, u32[]{:S(2)}) collective-permute-start(bf16[96,1024]{1,0:T(8,128)(2,1)S(1)} %add_convert_fusion.3), channel_id=1, source_target_pairs={{0,8},{2,10},{4,12},{6,14},{8,16},{10,18},{12,20},{14,22},{16,24},... | collective-permute-start | bytes 589832 | tf_op jit(solution)/shard_map/ppermute | solution.py:60
  171.2 19.5 %collective-permute-start.35 = (bf16[96,1024]{1,0:T(8,128)(2,1)S(1)}, bf16[96,1024]{1,0:T(8,128)(2,1)S(1)}, u32[]{:S(2)}, u32[]{:S(2)}) collective-permute-start(bf16[96,1024]{1,0:T(8,128)(2,1)S(1)} %add_convert_fusion.3), channel_id=1, source_target_pairs={{0,16},{2,18},{4,20},{6,22},{8,24},{10,26},{12,28},{14,30},{16,0},... | collective-permute-start | bytes 589832 | tf_op jit(solution)/shard_map/ppermute | solution.py:60
  173.3 17.3 %collective-permute-start.36 = (bf16[96,1024]{1,0:T(8,128)(2,1)S(1)}, bf16[96,1024]{1,0:T(8,128)(2,1)S(1)}, u32[]{:S(2)}, u32[]{:S(2)}) collective-permute-start(bf16[96,1024]{1,0:T(8,128)(2,1)S(1)} %add_convert_fusion.3), channel_id=1, source_target_pairs={{0,24},{2,26},{4,28},{6,30},{8,0},{10,2},{12,4},{14,6},{16,8},{18,... | collective-permute-start | bytes 589832 | tf_op jit(solution)/shard_map/ppermute | solution.py:60
  196.3 27.6 %collective-permute-start.47 = (bf16[400,768]{1,0:T(8,128)(2,1)S(1)}, bf16[400,768]{1,0:T(8,128)(2,1)S(1)}, u32[]{:S(2)}, u32[]{:S(2)}) collective-permute-start(bf16[400,768]{1,0:T(8,128)(2,1)S(1)} %pad_maximum_fusion.2), channel_id=1, source_target_pairs={{0,8},{2,10},{4,12},{6,14},{8,0},{10,2},{12,4},{14,6},{16,24},{18,... | collective-permute-start | bytes 1843208 | tf_op jit(solution)/shard_map/ppermute | solution.py:43
  197.2 21.8 %collective-permute-start.42 = (bf16[4,96,1024]{2,1,0:T(8,128)(2,1)S(1)}, bf16[4,96,1024]{2,1,0:T(8,128)(2,1)S(1)}, u32[]{:S(2)}, u32[]{:S(2)}) collective-permute-start(bf16[4,96,1024]{2,1,0:T(8,128)(2,1)S(1)} %pad_maximum_fusion.1.refs_0_), channel_id=1, source_target_pairs={{0,4},{2,6},{4,0},{6,2},{8,12},{10,14},{12,8},{14,10},{16,20},{18,... | collective-permute-start | bytes 2359304 | tf_op jit(solution)/shard_map/ppermute | solution.py:43
  205.2 18.6 %collective-permute-start.46 = (bf16[96,1280]{1,0:T(8,128)(2,1)S(1)}, bf16[96,1280]{1,0:T(8,128)(2,1)S(1)}, u32[]{:S(2)}, u32[]{:S(2)}) collective-permute-start(bf16[96,1280]{1,0:T(8,128)(2,1)S(1)} %pad_maximum_fusion.6), channel_id=1, source_target_pairs={{0,16},{2,18},{4,20},{6,22},{8,24},{10,26},{12,28},{14,30},{16,0},... | collective-permute-start | bytes 737288 | tf_op jit(solution)/shard_map/ppermute | solution.py:43
  231.1 16.8 %collective-permute-start.54 = (bf16[96,3328]{1,0:T(8,128)(2,1)S(1)}, bf16[96,3328]{1,0:T(8,128)(2,1)S(1)}, u32[]{:S(2)}, u32[]{:S(2)}) collective-permute-start(bf16[96,3328]{1,0:T(8,128)(2,1)S(1)} %fusion.7.refs_4_), channel_id=1, source_target_pairs={{0,4},{2,6},{4,0},{6,2},{8,12},{10,14},{12,8},{14,10},{16,20},{18,... | collective-permute-start | bytes 1916936 | tf_op jit(solution)/shard_map/ppermute | solution.py:43
  245.2 21.4 %collective-permute-start.59 = (bf16[4,96,512]{2,1,0:T(8,128)(2,1)S(1)}, bf16[4,96,512]{2,1,0:T(8,128)(2,1)S(1)}, u32[]{:S(2)}, u32[]{:S(2)}) collective-permute-start(bf16[4,96,512]{2,1,0:T(8,128)(2,1)S(1)} %pad_maximum_fusion.4.refs_0_), channel_id=1, source_target_pairs={{0,4},{2,6},{4,0},{6,2},{8,12},{10,14},{12,8},{14,10},{16,20},{18,... | collective-permute-start | bytes 1179656 | tf_op jit(solution)/shard_map/ppermute | solution.py:43
  248.8 17.8 %collective-permute-start.58 = (bf16[208,768]{1,0:T(8,128)(2,1)}, bf16[208,768]{1,0:T(8,128)(2,1)S(1)}, u32[]{:S(2)}, u32[]{:S(2)}) collective-permute-start(bf16[208,768]{1,0:T(8,128)(2,1)} %pad_maximum_fusion.5), channel_id=1, source_target_pairs={{0,16},{2,18},{4,20},{6,22},{8,24},{10,26},{12,28},{14,30},{16,0},... | collective-permute-start | bytes 958472 | tf_op jit(solution)/shard_map/ppermute | solution.py:43
  (98 other events, 846.5 us)

commit v3 on v2

--- a/solution.py
+++ b/solution.py
@@ -847,29 +847,18 @@
     )
 
 
-def last_kernel(count, place_ref, gain_ref, x_ref, grad_ref, resid_ref, *refs):
-    one_ref, got_ref, refs = refs[0], refs[1], refs[2:]
-    out_refs, refs = refs[:count], refs[count:]
-    x_grad_ref, out_ref = refs
+def last_kernel(place_ref, gain_ref, x_ref, grad_ref, one_ref, got_ref, x_grad_ref):
     micro, rows, width = x_ref.shape
     grad_one = one_ref[...] + got_ref[: micro * rows, :].astype(WIDE)
     x = x_ref[...].reshape(micro * rows, width).astype(WIDE)
     scale = rms_scale(x)
-    normed = x * scale
-    x_grad_ref[...] = grad_ref[...] + norm_back(grad_one * gain_ref[...], normed, scale)
-    parts = [(r[0] if len(r.shape) == 3 else r[r.shape[0] - micro * rows :, :]).astype(WIDE) for r in out_refs]
-    out_ref[...] = (resid_ref[...] + sum(parts)).astype(LOW)
-
-
-def last(place, gain, x, grad, resid, one, one_got, out_list):
-    rows, width = resid.shape
+    x_grad_ref[...] = grad_ref[...] + norm_back(grad_one * gain_ref[...], x * scale, scale)
+
+
+def last(place, gain, x, grad, one, one_got):
     return call(
-        functools.partial(last_kernel, len(out_list)),
-        "last",
-        place,
-        [gain, x, grad, resid, one, one_got, *out_list],
-        [shaped(rows, width, dtype=WIDE), shaped(rows, width)],
-    )
+        last_kernel, "last", place, [gain, x, grad, one, one_got], [shaped(*grad.shape, dtype=WIDE)]
+    )[0]
 
 
 def pair_finish_kernel(parts_f, fast, place_ref, *refs):
@@ -953,20 +942,25 @@
 
 def most_finish_kernel(parts_f, fast, place_ref, *refs):
     pair_refs, pack_refs, refs = refs[:fast], refs[fast : 2 * fast], refs[2 * fast :]
-    pair_finish_kernel(parts_f, fast, place_ref, *pair_refs, *refs[:2])
-    input_finish_kernel(fast, place_ref, *pack_refs, *refs[2:])
-
-
-def most_finish(place, pair_packs, packs, parts_f, width):
+    pair_finish_kernel(parts_f, fast, place_ref, *pair_refs, *refs[-7:-5])
+    input_finish_kernel(fast, place_ref, *pack_refs, *refs[-5:-1])
+    resid_ref, out_refs, out_ref = refs[0], refs[1:-7], refs[-1]
+    rows = resid_ref.shape[0]
+    parts = [(r[0] if len(r.shape) == 3 else r[r.shape[0] - rows :, :]).astype(WIDE) for r in out_refs]
+    out_ref[...] = (resid_ref[...] + sum(parts)).astype(LOW)
+
+
+def most_finish(place, pair_packs, packs, resid, out_list, parts_f, width):
     fast = len(packs)
     _, rows, double = pair_packs[0].shape
     return call(
         functools.partial(most_finish_kernel, parts_f, fast),
         "most_finish",
         place,
-        [*pair_packs, *packs],
+        [*pair_packs, *packs, resid, *out_list],
         [shaped(rows * GROUPS, double // 2 * fast, dtype=WIDE)] * 2
-        + [shaped(packs[0].shape[0] * fast, width, dtype=WIDE)] * 4,
+        + [shaped(packs[0].shape[0] * fast, width, dtype=WIDE)] * 4
+        + [shaped(*resid.shape)],
     )
 
 
@@ -1071,27 +1065,22 @@
 
     strip, kplace = fence(strip, kplace)
     places = (kplace[:, 0], kplace)
-    out_w, pair_w, x_slots, qkv_slots = fence(w_out, pair_part, x_slots, qkv_slots)
+    g_have = far_places(g_low)
+    out_w, pair_w, x_slots, qkv_slots, g_have = fence(w_out, pair_part, x_slots, qkv_slots, g_have)
     act_one, q, kv = project(tick[0], gain_one, x_slots, qkv_slots)
     kv_slots = slots_out(kv, "ctx", fast)
     out_w_slots = slots_out(out_w, "fsdp", parts_f)
+    g_slots = both_cores(g_have)
+    g_low, kv_slots, out_w_slots, g_slots, pair_w = fence(g_low, kv_slots, out_w_slots, g_slots, pair_w)
     pair_slots = slots_out(pair_w, "fsdp", parts_f)
-    g_low, kv_slots = fence(g_low, kv_slots)
-    g_have = {0: g_low, 1: hop(g_low, "ctx", 1)}
-    for bit in bits_down(fast // 2):
-        for j in [j for j in g_have if j % 2 == 0]:
-            g_have[j ^ (2 * bit)] = hop(g_have[j], "ctx", 2 * bit)
     o_group, lse = attention_forward(places, strip, q, kv_slots, blocks)
-    o_group, g_have, out_w_slots, down_w = fence(o_group, g_have, out_w_slots, down_part)
+    o_group, down_w = fence(o_group, down_part)
     o_slots = [o_group[0]] + shifted(o_group[1:], -1)
     down_slots = slots_out(down_w, "fsdp", parts_f)
-    for j in range(2, fast, 2):
-        g_have[j + 1] = hop(g_have[j], "ctx", 1)
-    g_slots = [g_have[j] for j in range(fast)]
     w_rel = arrange(tick[0], out_w_slots)
     o_slots, w_rel = fence(o_slots, w_rel)
     resid, act_two = joined(tick[0], gain_two, own_x, o_slots, w_rel)
-    act_two, g_slots = fence(act_two, g_slots)
+    act_two = fence(act_two)
     act_slots = slots_out(act_two, "ctx", fast)
     two_parts, out_parts, hid, grads = feed(tick[0], act_slots, g_slots, pair_slots, down_slots)
     two_parts, out_parts = fence(two_parts, out_parts)
@@ -1200,15 +1189,15 @@
     one_got, small = send_small(one_send, small, 2 * fast)
     pair_packs = both_cores(pair_have)
     in_packs, pair_packs = fence(both_cores(in_have), pair_packs)
-    w_gate_grad, w_up_grad, w_query_grad, w_key_grad, w_value_grad, w_out_grad = most_finish(
-        tick[0], pair_packs, in_packs, parts_f, width
+    w_gate_grad, w_up_grad, w_query_grad, w_key_grad, w_value_grad, w_out_grad, result = most_finish(
+        tick[0], pair_packs, in_packs, resid, out_list, parts_f, width
     )
     w_query_grad, one_got, low_have = fence(w_query_grad, one_got, low_have)
     low_packs = both_cores(low_have)
     small = take_small(one_got, small)[1]
     for bit in bits_down(fast // 2):
         small = small + hop(small, "ctx", 2 * bit)
-    x_grad, result = last(tick[0], gain_one, own_x, grad_resid, resid, one_sum, one_got, out_list)
+    x_grad = last(tick[0], gain_one, own_x, grad_resid, one_sum, one_got)
     x_grad, low_packs = fence(x_grad, low_packs)
     w_down_grad = low_finish(tick[0], low_packs, parts_f)
 

time: 279 us -> 273 us (0.978)
  waiting for transfers between devices: 93.5 us -> 88.2 us
    ppermute x42, waiting for transfers between devices: 68.7 us -> 63.3 us  [hop(): return lax.ppermute(v, axis, [(i, i ^ bit) for i in range(size)])]
    unnamed x124 -> x118, local copies, waits for them, and re-layouts: 9.49 us -> 10.2 us
  transfers between devices with their start and end apart: 63 -> 63, of which waited for: 22 -> 24; matrix products, arithmetic and copies ran while one was open for 6% -> 6% of each run, Pallas kernels for 26% -> 27%
where the time goes in v3:
time: 273 us
  waiting for transfers between devices  88.2 us (32%)
  Pallas kernels  87.9 us (32%)
  starting transfers between devices  69 us (25%)
  local copies, waits for them, and re-layouts  20 us (7%)
  other arithmetic  5.91 us (2%)
    ppermute x42, waiting for transfers between devices, hop(): return lax.ppermute(v, axis, [(i, i ^ bit) for i in range(size)])  63.3 us
    pallas_call x14, Pallas kernels, call(): pl.pallas_call(kernel, out_shape=tuple(out_shape), **grid, in_specs=specs...  57.6 us
    ppermute x21, starting transfers between devices, shift(): lax.ppermute(v, 'ctx', [(i, (i + steps * stride) % size) for i in range(s...  38.4 us
    ppermute x42, starting transfers between devices, hop(): return lax.ppermute(v, axis, [(i, i ^ bit) for i in range(size)])  30.6 us
    ppermute x21, waiting for transfers between devices, shift(): lax.ppermute(v, 'ctx', [(i, (i + steps * stride) % size) for i in range(s...  24.9 us
    pallas_call x1, Pallas kernels, attention_backward(): pl.pallas_call(functools.partial(backward_kernel, count, blocks), out_sha...  16.4 us
    unnamed x118, local copies, waits for them, and re-layouts  10.2 us
    pallas_call x1, Pallas kernels, attention_forward(): pl.pallas_call(functools.partial(forward_kernel, count, blocks), out_shap...  10.1 us
  transfers between devices with their start and end apart: 63, of which 24 were waited for; matrix products, arithmetic and copies ran while one was open for 6% of the time, Pallas kernels for 27%

profile of v3, /device:TPU:0, one launch (start us, length us, event | category | flops | bytes accessed | tf_op | source)
XLA Modules:
  0.0 272.6 jit_solution(11421611315664289833)
XLA Ops:
  17.5 3.9 %bias_strip.1.strip_ref = f32[3,2048,128]{2,1,0:T(8,128)} custom-call(f32[32,3]{1,0:T(8,128)} %copy.38.table_ref), custom_call_target="tpu_custom_call" | custom-call | tf_op jit(solution)/shard_map/bias_strip/pallas_call | solution.py:126
  25.9 3.7 %project.1 = (bf16[4,192,768]{2,1,0:T(8,128)(2,1)}, bf16[4,3,64,256]{3,2,1,0:T(8,128)(2,1)}, bf16[4,3,64,384]{3,2,1,0:T(8,128)(2,1)}) custom-call(s32[3]{0:T(128)} %pad_add_fusion.place_ref, f32[1,768]{1,0:T(1,128)} %reshape.157.gain_ref, bf16[3,64,768]{2,1,0:T(8,128)(2,1)} %bitcast.73, bf16[3,64,768]{2,1,0:T(8,128)(2,1)} %collective-permute-done.refs_1_, ...), custom_call_target="tpu_custom_call" | custom-call | flops 754974720 | bytes 4328448 | tf_op jit(solution)/shard_map/project/pallas_call | solution.py:418
  32.6 12.5 %collective-permute-done.6.refs_2_.refs_6_ = bf16[4,3,64,384]{3,2,1,0:T(8,128)(2,1)} collective-permute-done((bf16[4,3,64,384]{3,2,1,0:T(8,128)(2,1)}, bf16[4,3,64,384]{3,2,1,0:T(8,128)(2,1)}, u32[]{:S(2)}, u32[]{:S(2)}) %collective-permute-start.6) | collective-permute-done | bytes 589856 | tf_op jit(solution)/shard_map/ppermute | solution.py:43
  49.8 10.1 %attention_forward.1 = (bf16[3,64,256]{2,1,0:T(8,128)(2,1)}, bf16[3,64,256]{2,1,0:T(8,128)(2,1)}, bf16[3,64,256]{2,1,0:T(8,128)(2,1)}, bf16[3,64,256]{2,1,0:T(8,128)(2,1)}, f32[3,3,256]{2,1,0:T(4,128)}) custom-call(s32[3,4]{1,0:T(4,128)} %bitcast.90, s32[3,4,4]{2,1,0:T(4,128)} %copy-done.44, f32[3,2048,128]{2,1,0:T(8,128)} %bias_strip.1.strip_ref, ...), custom_call_target="tpu_custom_call" | custom-call | flops 2415919104 | bytes 4718592 | tf_op jit(solution)/shard_map/attention_forward/pallas_call | solution.py:217
  59.9 6.9 %collective-permute-start.11 = (bf16[3,64,256]{2,1,0:T(8,128)(2,1)}, bf16[3,64,256]{2,1,0:T(8,128)(2,1)S(1)}, u32[]{:S(2)}, u32[]{:S(2)}) collective-permute-start(bf16[3,64,256]{2,1,0:T(8,128)(2,1)} %get-tuple-element.251), channel_id=1, source_target_pairs={{0,24},{2,26},{4,28},{6,30},{8,0},{10,2},{12,4},{14,6},{16,8},{18,... | collective-permute-start | bytes 294920 | tf_op jit(solution)/shard_map/ppermute | solution.py:60
  71.5 5.9 %collective-permute-done.12.refs_2_ = bf16[3,64,256]{2,1,0:T(8,128)(2,1)S(1)} collective-permute-done((bf16[3,64,256]{2,1,0:T(8,128)(2,1)}, bf16[3,64,256]{2,1,0:T(8,128)(2,1)S(1)}, u32[]{:S(2)}, u32[]{:S(2)}) %collective-permute-start.12) | collective-permute-done | bytes 98336 | tf_op jit(solution)/shard_map/ppermute | solution.py:60
  83.7 6.1 %collective-permute-done.15.refs_2_ = bf16[192,768]{1,0:T(8,128)(2,1)S(1)} collective-permute-done((bf16[192,768]{1,0:T(8,128)(2,1)}, bf16[192,768]{1,0:T(8,128)(2,1)S(1)}, u32[]{:S(2)}, u32[]{:S(2)}) %collective-permute-start.15) | collective-permute-done | bytes 294944 | tf_op jit(solution)/shard_map/ppermute | solution.py:43
  94.4 7.9 %feed.1 = (f32[192,768]{1,0:T(8,128)}, bf16[1,192,768]{2,1,0:T(8,128)(2,1)}, bf16[2,192,768]{2,1,0:T(8,128)(2,1)}, f32[192,768]{1,0:T(8,128)}, bf16[1,192,768]{2...) custom-call(s32[3]{0:T(128)} %pad_add_fusion.place_ref, ...), custom_call_target="tpu_custom_call" | custom-call | flops 3623878656 | bytes 10027008 | tf_op jit(solution)/shard_map/feed/pallas_call | solution.py:418
  102.8 4.7 %pair_grads.1 = (f32[384,1024]{1,0:T(8,128)}, bf16[384,1024]{1,0:T(8,128)(2,1)}) custom-call(s32[3]{0:T(128)} %pad_add_fusion.place_ref, bf16[192,768]{1,0:T(8,128)(2,1)} %get-tuple-element.264.refs_0_, bf16[192,768]{1,0:T(8,128)(2,1)} %copy-done.51, bf16[192,768]{1,0:T(8,128)(2,1)} %copy-done.50, bf16[192,768]{1,0:T(8,128)(2,1)} %copy-done.52, ...), custom_call_target="tpu_custom_call" | custom-call | flops 1207959552 | bytes 5111808 | tf_op jit(solution)/shard_map/pair_grads/pallas_call | solution.py:418
  108.9 3.4 %down_grads.1 = (f32[384,512]{1,0:T(8,128)}, bf16[384,512]{1,0:T(8,128)(2,1)}) custom-call(s32[3]{0:T(128)} %pad_add_fusion.place_ref, bf16[192,768]{1,0:T(8,128)(2,1)} %bitcast.7.refs_4_.refs_0_.g_ref, bf16[192,768]{1,0:T(8,128)(2,1)} %collective-permute-done.9.refs_5_.refs_1_, bf16[192,768]{1,0:T(8,128)(2,1)} %collective-permute-done.4.refs_6_.refs_2_, ...), custom_call_target="tpu_custom_call" | custom-call | flops 603979776 | bytes 3145728 | tf_op jit(solution)/shard_map/down_grads/pallas_call | solution.py:418
  112.3 4.7 %collective-permute-done.21.refs_2_ = bf16[192,768]{1,0:T(8,128)(2,1)S(1)} collective-permute-done((bf16[192,768]{1,0:T(8,128)(2,1)S(1)}, bf16[192,768]{1,0:T(8,128)(2,1)S(1)}, u32[]{:S(2)}, u32[]{:S(2)}) %collective-permute-start.21) | collective-permute-done | bytes 294944 | tf_op jit(solution)/shard_map/ppermute | solution.py:43
  117.7 3.6 %branch.1 = (f32[192,768]{1,0:T(8,128)}, bf16[192,768]{1,0:T(8,128)(2,1)}, f32[1,768]{1,0:T(1,128)}, bf16[3,64,256]{2,1,0:T(8,128)(2,1)}, bf16[3,64,256]{2,1,0:T...) custom-call(s32[3]{0:T(128)} %pad_add_fusion.place_ref, f32[1,768]{1,0:T(1,128)} %reshape.158.gain_ref, ...), custom_call_target="tpu_custom_call" | custom-call | flops 301989888 | bytes 5216256 | tf_op jit(solution)/shard_map/branch/pallas_call | solution.py:418
  121.9 3.2 %collective-permute-start.24 = (bf16[3,64,256]{2,1,0:T(8,128)(2,1)}, bf16[3,64,256]{2,1,0:T(8,128)(2,1)S(1)}, u32[]{:S(2)}, u32[]{:S(2)}) collective-permute-start(bf16[3,64,256]{2,1,0:T(8,128)(2,1)} %get-tuple-element.309), channel_id=1, source_target_pairs={{0,24},{2,26},{4,28},{6,30},{8,0},{10,2},{12,4},{14,6},{16,8},{18,... | collective-permute-start | bytes 294920 | tf_op jit(solution)/shard_map/ppermute | solution.py:60
  142.3 16.4 %attention_backward.1 = (bf16[4,3,64,256]{3,2,1,0:T(8,128)(2,1)}, f32[4,3,64,384]{3,2,1,0:T(8,128)}, bf16[1,4,3,64,384]{4,3,2,1,0:T(8,128)(2,1)}, bf16[2,4,3,64,384]{4,3,2,1,0:T(8,128)(2,1)}, f32[32,128]{1,0:T(8,128)}) custom-call(s32[3,4]{1,0:T(4,128)} %bitcast.91, s32[3,4,4]{2,1,0:T(4,128)} %copy-done.44, s32[3]{0:T(128)} %pad_add_fusion.place_ref, ...), custom_call_target="tpu_custom_call" | custom-call | flops 6039797760 | bytes 9437184 | tf_op jit(solution)/shard_map/attention_backward/pallas_call | solution.py:354
  171.1 8.6 %collective-permute-done.33.refs_6_ = bf16[4,3,64,384]{3,2,1,0:T(8,128)(2,1)} collective-permute-done((bf16[4,3,64,384]{3,2,1,0:T(8,128)(2,1)S(1)}, bf16[4,3,64,384]{3,2,1,0:T(8,128)(2,1)}, u32[]{:S(2)}, u32[]{:S(2)}) %collective-permute-start.33) | collective-permute-done | bytes 589856 | tf_op jit(solution)/shard_map/ppermute | solution.py:43
  179.6 6.5 %input_grads.1 = (f32[2,192,768]{2,1,0:T(8,128)}, bf16[2,192,768]{2,1,0:T(8,128)(2,1)}, f32[1,768]{1,0:T(1,128)}, f32[2,2,96,640]{3,2,1,0:T(8,128)}, bf16[2,2,96,640]{3,2,1,0:T(8,128)(2,1)}) custom-call(s32[3]{0:T(128)} %pad_add_fusion.place_ref, bf16[4,192,768]{2,1,0:T(8,128)(2,1)} %get-tuple-element.350.act_ref, ...), custom_call_target="tpu_custom_call" | custom-call | flops 1509949440 | bytes 9931776 | tf_op jit(solution)/shard_map/input_grads/pallas_call | solution.py:418
  193.6 5.9 %collective-permute-done.40 = bf16[2,96,896]{2,1,0:T(8,128)(2,1)S(1)} collective-permute-done((bf16[2,96,896]{2,1,0:T(8,128)(2,1)S(1)}, bf16[2,96,896]{2,1,0:T(8,128)(2,1)S(1)}, u32[]{:S(2)}, u32[]{:S(2)}) %collective-permute-start.40) | collective-permute-done | bytes 344096 | tf_op jit(solution)/shard_map/ppermute | solution.py:43
  202.4 9.6 %collective-permute-done.41 = bf16[1,96,640]{2,1,0:T(8,128)(2,1)S(1)} collective-permute-done((bf16[1,96,640]{2,1,0:T(8,128)(2,1)S(1)}, bf16[1,96,640]{2,1,0:T(8,128)(2,1)S(1)}, u32[]{:S(2)}, u32[]{:S(2)}) %collective-permute-start.41) | collective-permute-done | bytes 122912 | tf_op jit(solution)/shard_map/ppermute | solution.py:43
  218.0 3.9 %collective-permute-done.43 = bf16[96,640]{1,0:T(8,128)(2,1)S(1)} collective-permute-done((bf16[96,640]{1,0:T(8,128)(2,1)S(1)}, bf16[96,640]{1,0:T(8,128)(2,1)S(1)}, u32[]{:S(2)}, u32[]{:S(2)}) %collective-permute-start.43) | collective-permute-done | bytes 122912 | tf_op jit(solution)/shard_map/ppermute | solution.py:60
  222.0 4.9 %collective-permute-done.44 = bf16[96,640]{1,0:T(8,128)(2,1)S(1)} collective-permute-done((bf16[96,640]{1,0:T(8,128)(2,1)S(1)}, bf16[96,640]{1,0:T(8,128)(2,1)S(1)}, u32[]{:S(2)}, u32[]{:S(2)}) %collective-permute-start.44) | collective-permute-done | bytes 122912 | tf_op jit(solution)/shard_map/ppermute | solution.py:60
  237.3 3.5 %collective-permute-done.49 = bf16[96,512]{1,0:T(8,128)(2,1)S(1)} collective-permute-done((bf16[96,512]{1,0:T(8,128)(2,1)S(1)}, bf16[96,512]{1,0:T(8,128)(2,1)S(1)}, u32[]{:S(2)}, u32[]{:S(2)}) %collective-permute-start.49) | collective-permute-done | bytes 98336 | tf_op jit(solution)/shard_map/ppermute | solution.py:60
  248.3 8.3 %most_finish.1 = (f32[384,2048]{1,0:T(8,128)}, f32[384,2048]{1,0:T(8,128)}, f32[384,768]{1,0:T(8,128)}, f32[384,768]{1,0:T(8,128)}, f32[384,768]{1,0:T(8,128)}, ...) custom-call(s32[3]{0:T(128)} %pad_add_fusion.place_ref, bf16[4,96,1024]{2,1,0:T(8,128)(2,1)} %copy-done.2, ...), custom_call_target="tpu_custom_call" | custom-call | bytes 19218432 | tf_op jit(solution)/shard_map/most_finish/pallas_call | solution.py:418
  256.6 5.2 %collective-permute-done.58.got_ref = bf16[208,768]{1,0:T(8,128)(2,1)S(1)} collective-permute-done((bf16[208,768]{1,0:T(8,128)(2,1)S(1)}, bf16[208,768]{1,0:T(8,128)(2,1)S(1)}, u32[]{:S(2)}, u32[]{:S(2)}) %collective-permute-start.58) | collective-permute-done | bytes 319520 | tf_op jit(solution)/shard_map/ppermute | solution.py:43
  269.1 3.5 %low_finish.1 = f32[1024,768]{1,0:T(8,128)} custom-call(s32[3]{0:T(128)} %pad_add_fusion.place_ref, bf16[4,96,512]{2,1,0:T(8,128)(2,1)} %copy-done.5, bf16[4,96,512]{2,1,0:T(8,128)(2,1)} %copy-done.24, bf16[4,96,512]{2,1,0:T(8,128)(2,1)} %copy-done.23, bf16[4,96,512]{2,1,0:T(8,128)(2,1)} %copy-done.25), custom_call_target="tpu_custom_call" | custom-call | bytes 4718592 | tf_op jit(solution)/shard_map/low_finish/pallas_call | solution.py:418
  (307 shorter events, 118.3 us)
Async XLA Ops:
  0.7 22.7 %collective-permute-start = (bf16[3,64,768]{2,1,0:T(8,128)(2,1)}, bf16[3,64,768]{2,1,0:T(8,128)(2,1)}, u32[]{:S(2)}, u32[]{:S(2)}) collective-permute-start(bf16[3,64,768]{2,1,0:T(8,128)(2,1)} %bitcast.70), channel_id=1, source_target_pairs={{0,8},{2,10},{4,12},{6,14},{8,16},{10,18},{12,20},{14,22},{16,24},... | collective-permute-start | bytes 884744 | tf_op jit(solution)/shard_map/ppermute | solution.py:60
  3.7 22.1 %collective-permute-start.1 = (bf16[3,64,768]{2,1,0:T(8,128)(2,1)}, bf16[3,64,768]{2,1,0:T(8,128)(2,1)}, u32[]{:S(2)}, u32[]{:S(2)}) collective-permute-start(bf16[3,64,768]{2,1,0:T(8,128)(2,1)} %bitcast.71), channel_id=1, source_target_pairs={{0,16},{2,18},{4,20},{6,22},{8,24},{10,26},{12,28},{14,30},{16,0},... | collective-permute-start | bytes 884744 | tf_op jit(solution)/shard_map/ppermute | solution.py:60
  6.3 19.5 %collective-permute-start.2 = (bf16[3,64,768]{2,1,0:T(8,128)(2,1)}, bf16[3,64,768]{2,1,0:T(8,128)(2,1)}, u32[]{:S(2)}, u32[]{:S(2)}) collective-permute-start(bf16[3,64,768]{2,1,0:T(8,128)(2,1)} %bitcast.72), channel_id=1, source_target_pairs={{0,24},{2,26},{4,28},{6,30},{8,0},{10,2},{12,4},{14,6},{16,8},{18,... | collective-permute-start | bytes 884744 | tf_op jit(solution)/shard_map/ppermute | solution.py:60
  29.6 15.5 %collective-permute-start.6 = (bf16[4,3,64,384]{3,2,1,0:T(8,128)(2,1)}, bf16[4,3,64,384]{3,2,1,0:T(8,128)(2,1)}, u32[]{:S(2)}, u32[]{:S(2)}) collective-permute-start(bf16[4,3,64,384]{3,2,1,0:T(8,128)(2,1)} %get-tuple-element.241.refs_0_.refs_4_), channel_id=1, source_target_pairs={{0,4},{2,6},{4,0},{6,2},{8,12},{10,14},{12,8},{14,10},{16,20},{18,... | collective-permute-start | bytes 1769480 | tf_op jit(solution)/shard_map/ppermute | solution.py:43
  31.1 17.1 %collective-permute-start.5 = (bf16[4,3,64,384]{3,2,1,0:T(8,128)(2,1)}, bf16[4,3,64,384]{3,2,1,0:T(8,128)(2,1)}, u32[]{:S(2)}, u32[]{:S(2)}) collective-permute-start(bf16[4,3,64,384]{3,2,1,0:T(8,128)(2,1)} %get-tuple-element.241.refs_0_.refs_4_), channel_id=1, source_target_pairs={{0,2},{2,0},{4,6},{6,4},{8,10},{10,8},{12,14},{14,12},{16,18},{18,... | collective-permute-start | bytes 1769480 | tf_op jit(solution)/shard_map/ppermute | solution.py:43
  31.1 17.1 %collective-permute-start.8 = (bf16[384,768]{1,0:T(8,128)(2,1)S(1)}, bf16[384,768]{1,0:T(8,128)(2,1)}, u32[]{:S(2)}, u32[]{:S(2)}) collective-permute-start(bf16[384,768]{1,0:T(8,128)(2,1)S(1)} %copy-done.22), channel_id=1, source_target_pairs={{0,1},{1,0},{2,3},{3,2},{4,5},{5,4},{6,7},{7,6},{8,9},{9,8},{10,11... | collective-permute-start | bytes 1769480 | tf_op jit(solution)/shard_map/ppermute | solution.py:43
  48.3 44.4 %collective-permute-start.17 = (bf16[384,1024]{1,0:T(8,128)(2,1)S(1)}, bf16[384,1024]{1,0:T(8,128)(2,1)S(1)}, u32[]{:S(2)}, u32[]{:S(2)}) collective-permute-start(bf16[384,1024]{1,0:T(8,128)(2,1)S(1)} %pad_maximum_fusion.refs_8_), channel_id=1, source_target_pairs={{0,1},{1,0},{2,3},{3,2},{4,5},{5,4},{6,7},{7,6},{8,9},{9,8},{10,11... | collective-permute-start | bytes 2359304 | tf_op jit(solution)/shard_map/ppermute | solution.py:43
  107.6 23.7 %collective-permute-start.25 = (bf16[384,1024]{1,0:T(8,128)(2,1)}, bf16[384,1024]{1,0:T(8,128)(2,1)S(1)}, u32[]{:S(2)}, u32[]{:S(2)}) collective-permute-start(bf16[384,1024]{1,0:T(8,128)(2,1)} %get-tuple-element.310), channel_id=1, source_target_pairs={{0,1},{1,0},{2,3},{3,2},{4,5},{5,4},{6,7},{7,6},{8,9},{9,8},{10,11... | collective-permute-start | bytes 2359304 | tf_op jit(solution)/shard_map/ppermute | solution.py:43
  136.1 22.7 %collective-permute-start.27 = (bf16[96,1024]{1,0:T(8,128)(2,1)}, bf16[96,1024]{1,0:T(8,128)(2,1)S(1)}, u32[]{:S(2)}, u32[]{:S(2)}) collective-permute-start(bf16[96,1024]{1,0:T(8,128)(2,1)} %get-tuple-element.331), channel_id=1, source_target_pairs={{0,8},{2,10},{4,12},{6,14},{8,16},{10,18},{12,20},{14,22},{16,24},... | collective-permute-start | bytes 589832 | tf_op jit(solution)/shard_map/ppermute | solution.py:60
  137.8 21.1 %collective-permute-start.28 = (bf16[96,1024]{1,0:T(8,128)(2,1)}, bf16[96,1024]{1,0:T(8,128)(2,1)S(1)}, u32[]{:S(2)}, u32[]{:S(2)}) collective-permute-start(bf16[96,1024]{1,0:T(8,128)(2,1)} %get-tuple-element.332), channel_id=1, source_target_pairs={{0,16},{2,18},{4,20},{6,22},{8,24},{10,26},{12,28},{14,30},{16,0},... | collective-permute-start | bytes 589832 | tf_op jit(solution)/shard_map/ppermute | solution.py:60
  139.0 19.9 %collective-permute-start.29 = (bf16[96,1024]{1,0:T(8,128)(2,1)}, bf16[96,1024]{1,0:T(8,128)(2,1)S(1)}, u32[]{:S(2)}, u32[]{:S(2)}) collective-permute-start(bf16[96,1024]{1,0:T(8,128)(2,1)} %get-tuple-element.333), channel_id=1, source_target_pairs={{0,24},{2,26},{4,28},{6,30},{8,0},{10,2},{12,4},{14,6},{16,8},{18,... | collective-permute-start | bytes 589832 | tf_op jit(solution)/shard_map/ppermute | solution.py:60
  140.2 18.7 %collective-permute-start.30 = (bf16[384,512]{1,0:T(8,128)(2,1)}, bf16[384,512]{1,0:T(8,128)(2,1)S(1)}, u32[]{:S(2)}, u32[]{:S(2)}) collective-permute-start(bf16[384,512]{1,0:T(8,128)(2,1)} %get-tuple-element.334), channel_id=1, source_target_pairs={{0,1},{1,0},{2,3},{3,2},{4,5},{5,4},{6,7},{7,6},{8,9},{9,8},{10,11... | collective-permute-start | bytes 1179656 | tf_op jit(solution)/shard_map/ppermute | solution.py:43
  141.7 17.0 %collective-permute-start.31 = (bf16[1,2,96,768]{3,2,1,0:T(8,128)(2,1)S(1)}, bf16[1,2,96,768]{3,2,1,0:T(8,128)(2,1)S(1)}, u32[]{:S(2)}, u32[]{:S(2)}) collective-permute-start(bf16[1,2,96,768]{3,2,1,0:T(8,128)(2,1)S(1)} %slice.215), channel_id=1, source_target_pairs={{0,1},{1,0},{2,3},{3,2},{4,5},{5,4},{6,7},{7,6},{8,9},{9,8},{10,11... | collective-permute-start | bytes 884744 | tf_op jit(solution)/shard_map/ppermute | solution.py:43
  163.3 16.3 %collective-permute-start.33 = (bf16[4,3,64,384]{3,2,1,0:T(8,128)(2,1)S(1)}, bf16[4,3,64,384]{3,2,1,0:T(8,128)(2,1)}, u32[]{:S(2)}, u32[]{:S(2)}) collective-permute-start(bf16[4,3,64,384]{3,2,1,0:T(8,128)(2,1)S(1)} %fusion), channel_id=1, source_target_pairs={{0,4},{2,6},{4,0},{6,2},{8,12},{10,14},{12,8},{14,10},{16,20},{18,... | collective-permute-start | bytes 1769480 | tf_op jit(solution)/shard_map/ppermute | solution.py:43
  164.8 23.6 %collective-permute-start.37 = (bf16[288,768]{1,0:T(8,128)(2,1)}, bf16[288,768]{1,0:T(8,128)(2,1)S(1)}, u32[]{:S(2)}, u32[]{:S(2)}) collective-permute-start(bf16[288,768]{1,0:T(8,128)(2,1)} %pad_maximum_fusion.3), channel_id=1, source_target_pairs={{0,4},{2,6},{4,0},{6,2},{8,12},{10,14},{12,8},{14,10},{16,20},{18,... | collective-permute-start | bytes 1327112 | tf_op jit(solution)/shard_map/ppermute | solution.py:43
  166.2 19.9 %collective-permute-start.34 = (bf16[96,1024]{1,0:T(8,128)(2,1)S(1)}, bf16[96,1024]{1,0:T(8,128)(2,1)S(1)}, u32[]{:S(2)}, u32[]{:S(2)}) collective-permute-start(bf16[96,1024]{1,0:T(8,128)(2,1)S(1)} %add_convert_fusion.3), channel_id=1, source_target_pairs={{0,8},{2,10},{4,12},{6,14},{8,16},{10,18},{12,20},{14,22},{16,24},... | collective-permute-start | bytes 589832 | tf_op jit(solution)/shard_map/ppermute | solution.py:60
  167.0 19.1 %collective-permute-start.35 = (bf16[96,1024]{1,0:T(8,128)(2,1)S(1)}, bf16[96,1024]{1,0:T(8,128)(2,1)S(1)}, u32[]{:S(2)}, u32[]{:S(2)}) collective-permute-start(bf16[96,1024]{1,0:T(8,128)(2,1)S(1)} %add_convert_fusion.3), channel_id=1, source_target_pairs={{0,16},{2,18},{4,20},{6,22},{8,24},{10,26},{12,28},{14,30},{16,0},... | collective-permute-start | bytes 589832 | tf_op jit(solution)/shard_map/ppermute | solution.py:60
  168.7 17.4 %collective-permute-start.36 = (bf16[96,1024]{1,0:T(8,128)(2,1)S(1)}, bf16[96,1024]{1,0:T(8,128)(2,1)S(1)}, u32[]{:S(2)}, u32[]{:S(2)}) collective-permute-start(bf16[96,1024]{1,0:T(8,128)(2,1)S(1)} %add_convert_fusion.3), channel_id=1, source_target_pairs={{0,24},{2,26},{4,28},{6,30},{8,0},{10,2},{12,4},{14,6},{16,8},{18,... | collective-permute-start | bytes 589832 | tf_op jit(solution)/shard_map/ppermute | solution.py:60
  189.6 22.4 %collective-permute-start.42 = (bf16[4,96,1024]{2,1,0:T(8,128)(2,1)S(1)}, bf16[4,96,1024]{2,1,0:T(8,128)(2,1)S(1)}, u32[]{:S(2)}, u32[]{:S(2)}) collective-permute-start(bf16[4,96,1024]{2,1,0:T(8,128)(2,1)S(1)} %pad_maximum_fusion.1.refs_0_), channel_id=1, source_target_pairs={{0,4},{2,6},{4,0},{6,2},{8,12},{10,14},{12,8},{14,10},{16,20},{18,... | collective-permute-start | bytes 2359304 | tf_op jit(solution)/shard_map/ppermute | solution.py:43
  192.3 25.7 %collective-permute-start.47 = (bf16[400,768]{1,0:T(8,128)(2,1)S(1)}, bf16[400,768]{1,0:T(8,128)(2,1)S(1)}, u32[]{:S(2)}, u32[]{:S(2)}) collective-permute-start(bf16[400,768]{1,0:T(8,128)(2,1)S(1)} %pad_maximum_fusion.2), channel_id=1, source_target_pairs={{0,8},{2,10},{4,12},{6,14},{8,0},{10,2},{12,4},{14,6},{16,24},{18,... | collective-permute-start | bytes 1843208 | tf_op jit(solution)/shard_map/ppermute | solution.py:43
  200.5 16.2 %collective-permute-start.46 = (bf16[96,1280]{1,0:T(8,128)(2,1)S(1)}, bf16[96,1280]{1,0:T(8,128)(2,1)S(1)}, u32[]{:S(2)}, u32[]{:S(2)}) collective-permute-start(bf16[96,1280]{1,0:T(8,128)(2,1)S(1)} %pad_maximum_fusion.6), channel_id=1, source_target_pairs={{0,16},{2,18},{4,20},{6,22},{8,24},{10,26},{12,28},{14,30},{16,0},... | collective-permute-start | bytes 737288 | tf_op jit(solution)/shard_map/ppermute | solution.py:43
  227.1 16.8 %collective-permute-start.54 = (bf16[96,3328]{1,0:T(8,128)(2,1)S(1)}, bf16[96,3328]{1,0:T(8,128)(2,1)S(1)}, u32[]{:S(2)}, u32[]{:S(2)}) collective-permute-start(bf16[96,3328]{1,0:T(8,128)(2,1)S(1)} %fusion.7.refs_4_), channel_id=1, source_target_pairs={{0,4},{2,6},{4,0},{6,2},{8,12},{10,14},{12,8},{14,10},{16,20},{18,... | collective-permute-start | bytes 1916936 | tf_op jit(solution)/shard_map/ppermute | solution.py:43
  241.4 20.3 %collective-permute-start.59 = (bf16[4,96,512]{2,1,0:T(8,128)(2,1)S(1)}, bf16[4,96,512]{2,1,0:T(8,128)(2,1)S(1)}, u32[]{:S(2)}, u32[]{:S(2)}) collective-permute-start(bf16[4,96,512]{2,1,0:T(8,128)(2,1)S(1)} %pad_maximum_fusion.4.refs_0_), channel_id=1, source_target_pairs={{0,4},{2,6},{4,0},{6,2},{8,12},{10,14},{12,8},{14,10},{16,20},{18,... | collective-permute-start | bytes 1179656 | tf_op jit(solution)/shard_map/ppermute | solution.py:43
  244.0 17.7 %collective-permute-start.58 = (bf16[208,768]{1,0:T(8,128)(2,1)S(1)}, bf16[208,768]{1,0:T(8,128)(2,1)S(1)}, u32[]{:S(2)}, u32[]{:S(2)}) collective-permute-start(bf16[208,768]{1,0:T(8,128)(2,1)S(1)} %pad_maximum_fusion.5), channel_id=1, source_target_pairs={{0,16},{2,18},{4,20},{6,22},{8,24},{10,26},{12,28},{14,30},{16,0},... | collective-permute-start | bytes 958472 | tf_op jit(solution)/shard_map/ppermute | solution.py:43
  (95 other events, 773.5 us)

commit v4 on v3

--- a/solution.py
+++ b/solution.py
@@ -1100,8 +1100,12 @@
     )
     do_own = fence(*do_own)
     do_slots = [do_own[0]] + shifted(do_own[1:], 1)
+    out_list, _ = pairs_on(out_parts, out_got_one, fast)
     out_keep, out_send = out_grads(tick[0], grad_low, o_slots, parts_f, fast)
-    out_keep, out_send, do_slots, pair_got = fence(out_keep, out_send, do_slots, pair_got)
+    out_keep, out_send, do_slots, pair_got, got = fence(
+        out_keep, out_send, do_slots, pair_got, [v for v, _ in out_list]
+    )
+    out_list = [(v, first) for v, (_, first) in zip(got, out_list)]
     out_got = hop(out_send, "ctx", 1)
     pair_own, pair_sends = group_split(tick[0], [pair_keep, *pair_got])
     pair_own, pair_sends, low_sends, out_total = fence(
@@ -1119,27 +1123,15 @@
     low_keep, low_send = group_halves(tick[0], [low_keep, *low_got])
     pair_chunk, low_send, out_total, _ = fence(groups_sum(pair_own, pair_parts), low_send, out_total, sent)
     pair_spread = spread_groups(pair_chunk)
-    if fast == 4:
-        out_far = (out_parts[1][0].astype(WIDE) + out_got_one[1].astype(WIDE)).astype(LOW)
-        far = jnp.concatenate([out_total[1].astype(LOW), out_far])
-        far = hop(far, "ctx", 2)
+    out_low = halve(out_total, "ctx", 2).astype(LOW)
     got = fence([v for v, _ in dkv_list])
     dkv_list = [(v, first) for v, (_, first) in zip(got, dkv_list)]
     one_keep, one_send, gain_one_part, in_keep, in_send = input_grads(
         tick[0], act_one, dq, x_slots, dkv_list, qkv_slots, fast
     )
-    one_keep, one_send, in_keep, in_send, low_send, pair_spread = fence(
-        one_keep, one_send, in_keep, in_send, low_send, pair_spread
-    )
-    if fast == 4:
-        far = fence(far)
-        chunk = out_total.shape[1]
-        out_low = (out_total[0] + far[:chunk].astype(WIDE)).astype(LOW)
-        out_list = [(out_parts[0], False), (out_got_one, True), (far, False)]
-    else:
-        out_low = halve(out_total, "ctx", 2).astype(LOW)
-        out_list, _ = pairs_on(out_parts, out_got_one, fast)
-
+    one_keep, one_send, in_keep, in_send, low_send, pair_spread, out_low = fence(
+        one_keep, one_send, in_keep, in_send, low_send, pair_spread, out_low
+    )
     def send_small(v, small, bit):
         high = small.astype(LOW)
         rest = (small - high.astype(WIDE)).astype(LOW)

time: 273 us -> 272 us (level)
    ppermute x42 -> x43, waiting for transfers between devices: 63.3 us -> 64.6 us  [hop(): return lax.ppermute(v, axis, [(i, i ^ bit) for i in range(size)])]
    ppermute x42 -> x43, starting transfers between devices: 30.6 us -> 31.5 us  [hop(): return lax.ppermute(v, axis, [(i, i ^ bit) for i in range(size)])]
    unnamed x118 -> x112, local copies, waits for them, and re-layouts: 10.2 us -> 10.3 us
  transfers between devices with their start and end apart: 63 -> 64, of which waited for: 24 -> 24; matrix products, arithmetic and copies ran while one was open for 6% -> 5% of each run, Pallas kernels for 27% -> 27%
where the time goes in v4:
time: 272 us; the launch traced here: 271 us
  waiting for transfers between devices  88.6 us (33%)
  Pallas kernels  87.8 us (32%)
  starting transfers between devices  69.7 us (26%)
  local copies, waits for them, and re-layouts  20.2 us (7%)
  other arithmetic  3.79 us (1%)
    ppermute x43, waiting for transfers between devices, hop(): return lax.ppermute(v, axis, [(i, i ^ bit) for i in range(size)])  64.6 us
    pallas_call x14, Pallas kernels, call(): pl.pallas_call(kernel, out_shape=tuple(out_shape), **grid, in_specs=specs...  57.4 us
    ppermute x21, starting transfers between devices, shift(): lax.ppermute(v, 'ctx', [(i, (i + steps * stride) % size) for i in range(s...  38.1 us
    ppermute x43, starting transfers between devices, hop(): return lax.ppermute(v, axis, [(i, i ^ bit) for i in range(size)])  31.5 us
    ppermute x21, waiting for transfers between devices, shift(): lax.ppermute(v, 'ctx', [(i, (i + steps * stride) % size) for i in range(s...  24 us
    pallas_call x1, Pallas kernels, attention_backward(): pl.pallas_call(functools.partial(backward_kernel, count, blocks), out_sha...  16.4 us
    unnamed x112, local copies, waits for them, and re-layouts  10.3 us
    pallas_call x1, Pallas kernels, attention_forward(): pl.pallas_call(functools.partial(forward_kernel, count, blocks), out_shap...  10.1 us
  transfers between devices with their start and end apart: 64, of which 24 were waited for; matrix products, arithmetic and copies ran while one was open for 5% of the time, Pallas kernels for 27%

profile of v4, /device:TPU:0, one launch (start us, length us, event | category | flops | bytes accessed | tf_op | source)
XLA Modules:
  0.0 271.5 jit_solution(17858388913437822969)
XLA Ops:
  17.4 3.9 %bias_strip.1.strip_ref = f32[3,2048,128]{2,1,0:T(8,128)} custom-call(f32[32,3]{1,0:T(8,128)} %copy.38.table_ref), custom_call_target="tpu_custom_call" | custom-call | tf_op jit(solution)/shard_map/bias_strip/pallas_call | solution.py:126
  25.9 3.7 %project.1 = (bf16[4,192,768]{2,1,0:T(8,128)(2,1)}, bf16[4,3,64,256]{3,2,1,0:T(8,128)(2,1)}, bf16[4,3,64,384]{3,2,1,0:T(8,128)(2,1)}) custom-call(s32[3]{0:T(128)} %pad_add_fusion.place_ref, f32[1,768]{1,0:T(1,128)} %reshape.157.gain_ref, bf16[3,64,768]{2,1,0:T(8,128)(2,1)} %bitcast.69, bf16[3,64,768]{2,1,0:T(8,128)(2,1)} %collective-permute-done.refs_1_, ...), custom_call_target="tpu_custom_call" | custom-call | flops 754974720 | bytes 4328448 | tf_op jit(solution)/shard_map/project/pallas_call | solution.py:418
  32.6 12.5 %collective-permute-done.6.refs_2_.refs_6_ = bf16[4,3,64,384]{3,2,1,0:T(8,128)(2,1)} collective-permute-done((bf16[4,3,64,384]{3,2,1,0:T(8,128)(2,1)}, bf16[4,3,64,384]{3,2,1,0:T(8,128)(2,1)}, u32[]{:S(2)}, u32[]{:S(2)}) %collective-permute-start.6) | collective-permute-done | bytes 589856 | tf_op jit(solution)/shard_map/ppermute | solution.py:43
  49.8 10.1 %attention_forward.1 = (bf16[3,64,256]{2,1,0:T(8,128)(2,1)}, bf16[3,64,256]{2,1,0:T(8,128)(2,1)}, bf16[3,64,256]{2,1,0:T(8,128)(2,1)}, bf16[3,64,256]{2,1,0:T(8,128)(2,1)}, f32[3,3,256]{2,1,0:T(4,128)}) custom-call(s32[3,4]{1,0:T(4,128)} %bitcast.86, s32[3,4,4]{2,1,0:T(4,128)} %copy-done.41, f32[3,2048,128]{2,1,0:T(8,128)} %bias_strip.1.strip_ref, ...), custom_call_target="tpu_custom_call" | custom-call | flops 2415919104 | bytes 4718592 | tf_op jit(solution)/shard_map/attention_forward/pallas_call | solution.py:217
  59.9 6.9 %collective-permute-start.11 = (bf16[3,64,256]{2,1,0:T(8,128)(2,1)}, bf16[3,64,256]{2,1,0:T(8,128)(2,1)S(1)}, u32[]{:S(2)}, u32[]{:S(2)}) collective-permute-start(bf16[3,64,256]{2,1,0:T(8,128)(2,1)} %get-tuple-element.253), channel_id=1, source_target_pairs={{0,24},{2,26},{4,28},{6,30},{8,0},{10,2},{12,4},{14,6},{16,8},{18,... | collective-permute-start | bytes 294920 | tf_op jit(solution)/shard_map/ppermute | solution.py:60
  71.5 5.9 %collective-permute-done.12.refs_2_ = bf16[3,64,256]{2,1,0:T(8,128)(2,1)S(1)} collective-permute-done((bf16[3,64,256]{2,1,0:T(8,128)(2,1)}, bf16[3,64,256]{2,1,0:T(8,128)(2,1)S(1)}, u32[]{:S(2)}, u32[]{:S(2)}) %collective-permute-start.12) | collective-permute-done | bytes 98336 | tf_op jit(solution)/shard_map/ppermute | solution.py:60
  83.7 5.8 %collective-permute-done.15.refs_2_ = bf16[192,768]{1,0:T(8,128)(2,1)S(1)} collective-permute-done((bf16[192,768]{1,0:T(8,128)(2,1)}, bf16[192,768]{1,0:T(8,128)(2,1)S(1)}, u32[]{:S(2)}, u32[]{:S(2)}) %collective-permute-start.15) | collective-permute-done | bytes 294944 | tf_op jit(solution)/shard_map/ppermute | solution.py:43
  94.4 7.9 %feed.1 = (f32[192,768]{1,0:T(8,128)}, bf16[1,192,768]{2,1,0:T(8,128)(2,1)}, bf16[2,192,768]{2,1,0:T(8,128)(2,1)}, f32[192,768]{1,0:T(8,128)}, bf16[1,192,768]{2...) custom-call(s32[3]{0:T(128)} %pad_add_fusion.place_ref, ...), custom_call_target="tpu_custom_call" | custom-call | flops 3623878656 | bytes 10027008 | tf_op jit(solution)/shard_map/feed/pallas_call | solution.py:418
  102.9 4.7 %pair_grads.1 = (f32[384,1024]{1,0:T(8,128)}, bf16[384,1024]{1,0:T(8,128)(2,1)}) custom-call(s32[3]{0:T(128)} %pad_add_fusion.place_ref, bf16[192,768]{1,0:T(8,128)(2,1)} %get-tuple-element.266.refs_0_, bf16[192,768]{1,0:T(8,128)(2,1)} %copy-done.48, bf16[192,768]{1,0:T(8,128)(2,1)} %copy-done.47, bf16[192,768]{1,0:T(8,128)(2,1)} %copy-done.49, ...), custom_call_target="tpu_custom_call" | custom-call | flops 1207959552 | bytes 5111808 | tf_op jit(solution)/shard_map/pair_grads/pallas_call | solution.py:418
  111.2 3.4 %down_grads.1 = (f32[384,512]{1,0:T(8,128)}, bf16[384,512]{1,0:T(8,128)(2,1)}) custom-call(s32[3]{0:T(128)} %pad_add_fusion.place_ref, bf16[192,768]{1,0:T(8,128)(2,1)} %bitcast.7.refs_4_.refs_0_.g_ref, bf16[192,768]{1,0:T(8,128)(2,1)} %collective-permute-done.9.refs_5_.refs_1_, bf16[192,768]{1,0:T(8,128)(2,1)} %collective-permute-done.4.refs_6_.refs_2_, ...), custom_call_target="tpu_custom_call" | custom-call | flops 603979776 | bytes 3145728 | tf_op jit(solution)/shard_map/down_grads/pallas_call | solution.py:418
  114.6 3.7 %collective-permute-done.21.refs_2_ = bf16[192,768]{1,0:T(8,128)(2,1)S(1)} collective-permute-done((bf16[192,768]{1,0:T(8,128)(2,1)S(1)}, bf16[192,768]{1,0:T(8,128)(2,1)S(1)}, u32[]{:S(2)}, u32[]{:S(2)}) %collective-permute-start.21) | collective-permute-done | bytes 294944 | tf_op jit(solution)/shard_map/ppermute | solution.py:43
  119.0 3.6 %branch.1 = (f32[192,768]{1,0:T(8,128)}, bf16[192,768]{1,0:T(8,128)(2,1)}, f32[1,768]{1,0:T(1,128)}, bf16[3,64,256]{2,1,0:T(8,128)(2,1)}, bf16[3,64,256]{2,1,0:T...) custom-call(s32[3]{0:T(128)} %pad_add_fusion.place_ref, f32[1,768]{1,0:T(1,128)} %reshape.158.gain_ref, ...), custom_call_target="tpu_custom_call" | custom-call | flops 301989888 | bytes 5216256 | tf_op jit(solution)/shard_map/branch/pallas_call | solution.py:418
  123.2 3.2 %collective-permute-start.24 = (bf16[3,64,256]{2,1,0:T(8,128)(2,1)}, bf16[3,64,256]{2,1,0:T(8,128)(2,1)S(1)}, u32[]{:S(2)}, u32[]{:S(2)}) collective-permute-start(bf16[3,64,256]{2,1,0:T(8,128)(2,1)} %get-tuple-element.311), channel_id=1, source_target_pairs={{0,24},{2,26},{4,28},{6,30},{8,0},{10,2},{12,4},{14,6},{16,8},{18,... | collective-permute-start | bytes 294920 | tf_op jit(solution)/shard_map/ppermute | solution.py:60
  141.4 16.4 %attention_backward.1 = (bf16[4,3,64,256]{3,2,1,0:T(8,128)(2,1)}, f32[4,3,64,384]{3,2,1,0:T(8,128)}, bf16[1,4,3,64,384]{4,3,2,1,0:T(8,128)(2,1)}, bf16[2,4,3,64,384]{4,3,2,1,0:T(8,128)(2,1)}, f32[32,128]{1,0:T(8,128)}) custom-call(s32[3,4]{1,0:T(4,128)} %bitcast.87, s32[3,4,4]{2,1,0:T(4,128)} %copy-done.41, s32[3]{0:T(128)} %pad_add_fusion.place_ref, ...), custom_call_target="tpu_custom_call" | custom-call | flops 6039797760 | bytes 9437184 | tf_op jit(solution)/shard_map/attention_backward/pallas_call | solution.py:354
  168.3 11.6 %collective-permute-done.38 = bf16[1,96,768]{2,1,0:T(8,128)(2,1)S(1)} collective-permute-done((bf16[1,96,768]{2,1,0:T(8,128)(2,1)S(1)}, bf16[1,96,768]{2,1,0:T(8,128)(2,1)S(1)}, u32[]{:S(2)}, u32[]{:S(2)}) %collective-permute-start.38) | collective-permute-done | bytes 147488 | tf_op jit(solution)/shard_map/ppermute | solution.py:43
  180.7 6.5 %input_grads.1 = (f32[2,192,768]{2,1,0:T(8,128)}, bf16[2,192,768]{2,1,0:T(8,128)(2,1)}, f32[1,768]{1,0:T(1,128)}, f32[2,2,96,640]{3,2,1,0:T(8,128)}, bf16[2,2,96,640]{3,2,1,0:T(8,128)(2,1)}) custom-call(s32[3]{0:T(128)} %pad_add_fusion.place_ref, bf16[4,192,768]{2,1,0:T(8,128)(2,1)} %get-tuple-element.355.act_ref, ...), custom_call_target="tpu_custom_call" | custom-call | flops 1509949440 | bytes 9931776 | tf_op jit(solution)/shard_map/input_grads/pallas_call | solution.py:418
  192.2 6.2 %collective-permute-done.41 = bf16[2,96,896]{2,1,0:T(8,128)(2,1)S(1)} collective-permute-done((bf16[2,96,896]{2,1,0:T(8,128)(2,1)S(1)}, bf16[2,96,896]{2,1,0:T(8,128)(2,1)S(1)}, u32[]{:S(2)}, u32[]{:S(2)}) %collective-permute-start.41) | collective-permute-done | bytes 344096 | tf_op jit(solution)/shard_map/ppermute | solution.py:43
  201.1 9.9 %collective-permute-done.42 = bf16[1,96,640]{2,1,0:T(8,128)(2,1)S(1)} collective-permute-done((bf16[1,96,640]{2,1,0:T(8,128)(2,1)S(1)}, bf16[1,96,640]{2,1,0:T(8,128)(2,1)S(1)}, u32[]{:S(2)}, u32[]{:S(2)}) %collective-permute-start.42) | collective-permute-done | bytes 122912 | tf_op jit(solution)/shard_map/ppermute | solution.py:43
  216.9 3.9 %collective-permute-done.44 = bf16[96,640]{1,0:T(8,128)(2,1)S(1)} collective-permute-done((bf16[96,640]{1,0:T(8,128)(2,1)S(1)}, bf16[96,640]{1,0:T(8,128)(2,1)S(1)}, u32[]{:S(2)}, u32[]{:S(2)}) %collective-permute-start.44) | collective-permute-done | bytes 122912 | tf_op jit(solution)/shard_map/ppermute | solution.py:60
  220.8 4.9 %collective-permute-done.45 = bf16[96,640]{1,0:T(8,128)(2,1)S(1)} collective-permute-done((bf16[96,640]{1,0:T(8,128)(2,1)S(1)}, bf16[96,640]{1,0:T(8,128)(2,1)S(1)}, u32[]{:S(2)}, u32[]{:S(2)}) %collective-permute-start.45) | collective-permute-done | bytes 122912 | tf_op jit(solution)/shard_map/ppermute | solution.py:60
  236.4 3.5 %collective-permute-done.50 = bf16[96,512]{1,0:T(8,128)(2,1)S(1)} collective-permute-done((bf16[96,512]{1,0:T(8,128)(2,1)S(1)}, bf16[96,512]{1,0:T(8,128)(2,1)S(1)}, u32[]{:S(2)}, u32[]{:S(2)}) %collective-permute-start.50) | collective-permute-done | bytes 98336 | tf_op jit(solution)/shard_map/ppermute | solution.py:60
  246.2 8.2 %most_finish.1 = (f32[384,2048]{1,0:T(8,128)}, f32[384,2048]{1,0:T(8,128)}, f32[384,768]{1,0:T(8,128)}, f32[384,768]{1,0:T(8,128)}, f32[384,768]{1,0:T(8,128)}, ...) custom-call(s32[3]{0:T(128)} %pad_add_fusion.place_ref, bf16[4,96,1024]{2,1,0:T(8,128)(2,1)} %copy-done.2, ...), custom_call_target="tpu_custom_call" | custom-call | bytes 19070976 | tf_op jit(solution)/shard_map/most_finish/pallas_call | solution.py:418
  254.4 6.2 %collective-permute-done.59.got_ref = bf16[208,768]{1,0:T(8,128)(2,1)S(1)} collective-permute-done((bf16[208,768]{1,0:T(8,128)(2,1)S(1)}, bf16[208,768]{1,0:T(8,128)(2,1)S(1)}, u32[]{:S(2)}, u32[]{:S(2)}) %collective-permute-start.59) | collective-permute-done | bytes 319520 | tf_op jit(solution)/shard_map/ppermute | solution.py:43
  268.0 3.5 %low_finish.1 = f32[1024,768]{1,0:T(8,128)} custom-call(s32[3]{0:T(128)} %pad_add_fusion.place_ref, bf16[4,96,512]{2,1,0:T(8,128)(2,1)} %copy-done.5, bf16[4,96,512]{2,1,0:T(8,128)(2,1)} %copy-done.23, bf16[4,96,512]{2,1,0:T(8,128)(2,1)} %collective-permute-done.60.refs_2_, bf16[4,96,512]{2,1,0:T(8,128)(2,1)} %copy-done.24), custom_call_target="tpu_custom_call" | custom-call | bytes 4718592 | tf_op jit(solution)/shard_map/low_finish/pallas_call | solution.py:418
  (302 shorter events, 114.0 us)
Async XLA Ops:
  0.7 22.6 %collective-permute-start = (bf16[3,64,768]{2,1,0:T(8,128)(2,1)}, bf16[3,64,768]{2,1,0:T(8,128)(2,1)}, u32[]{:S(2)}, u32[]{:S(2)}) collective-permute-start(bf16[3,64,768]{2,1,0:T(8,128)(2,1)} %bitcast.66), channel_id=1, source_target_pairs={{0,8},{2,10},{4,12},{6,14},{8,16},{10,18},{12,20},{14,22},{16,24},... | collective-permute-start | bytes 884744 | tf_op jit(solution)/shard_map/ppermute | solution.py:60
  3.7 22.1 %collective-permute-start.1 = (bf16[3,64,768]{2,1,0:T(8,128)(2,1)}, bf16[3,64,768]{2,1,0:T(8,128)(2,1)}, u32[]{:S(2)}, u32[]{:S(2)}) collective-permute-start(bf16[3,64,768]{2,1,0:T(8,128)(2,1)} %bitcast.67), channel_id=1, source_target_pairs={{0,16},{2,18},{4,20},{6,22},{8,24},{10,26},{12,28},{14,30},{16,0},... | collective-permute-start | bytes 884744 | tf_op jit(solution)/shard_map/ppermute | solution.py:60
  6.3 19.5 %collective-permute-start.2 = (bf16[3,64,768]{2,1,0:T(8,128)(2,1)}, bf16[3,64,768]{2,1,0:T(8,128)(2,1)}, u32[]{:S(2)}, u32[]{:S(2)}) collective-permute-start(bf16[3,64,768]{2,1,0:T(8,128)(2,1)} %bitcast.68), channel_id=1, source_target_pairs={{0,24},{2,26},{4,28},{6,30},{8,0},{10,2},{12,4},{14,6},{16,8},{18,... | collective-permute-start | bytes 884744 | tf_op jit(solution)/shard_map/ppermute | solution.py:60
  31.1 17.1 %collective-permute-start.5 = (bf16[4,3,64,384]{3,2,1,0:T(8,128)(2,1)}, bf16[4,3,64,384]{3,2,1,0:T(8,128)(2,1)}, u32[]{:S(2)}, u32[]{:S(2)}) collective-permute-start(bf16[4,3,64,384]{3,2,1,0:T(8,128)(2,1)} %get-tuple-element.243.refs_0_.refs_4_), channel_id=1, source_target_pairs={{0,2},{2,0},{4,6},{6,4},{8,10},{10,8},{12,14},{14,12},{16,18},{18,... | collective-permute-start | bytes 1769480 | tf_op jit(solution)/shard_map/ppermute | solution.py:43
  31.1 17.1 %collective-permute-start.8 = (bf16[384,768]{1,0:T(8,128)(2,1)S(1)}, bf16[384,768]{1,0:T(8,128)(2,1)}, u32[]{:S(2)}, u32[]{:S(2)}) collective-permute-start(bf16[384,768]{1,0:T(8,128)(2,1)S(1)} %copy-done.21), channel_id=1, source_target_pairs={{0,1},{1,0},{2,3},{3,2},{4,5},{5,4},{6,7},{7,6},{8,9},{9,8},{10,11... | collective-permute-start | bytes 1769480 | tf_op jit(solution)/shard_map/ppermute | solution.py:43
  48.3 44.4 %collective-permute-start.17 = (bf16[384,1024]{1,0:T(8,128)(2,1)S(1)}, bf16[384,1024]{1,0:T(8,128)(2,1)S(1)}, u32[]{:S(2)}, u32[]{:S(2)}) collective-permute-start(bf16[384,1024]{1,0:T(8,128)(2,1)S(1)} %pad_maximum_fusion.refs_8_), channel_id=1, source_target_pairs={{0,1},{1,0},{2,3},{3,2},{4,5},{5,4},{6,7},{7,6},{8,9},{9,8},{10,11... | collective-permute-start | bytes 2359304 | tf_op jit(solution)/shard_map/ppermute | solution.py:43
  107.6 23.8 %collective-permute-start.25 = (bf16[384,1024]{1,0:T(8,128)(2,1)}, bf16[384,1024]{1,0:T(8,128)(2,1)S(1)}, u32[]{:S(2)}, u32[]{:S(2)}) collective-permute-start(bf16[384,1024]{1,0:T(8,128)(2,1)} %get-tuple-element.312), channel_id=1, source_target_pairs={{0,1},{1,0},{2,3},{3,2},{4,5},{5,4},{6,7},{7,6},{8,9},{9,8},{10,11... | collective-permute-start | bytes 2359304 | tf_op jit(solution)/shard_map/ppermute | solution.py:43
  109.6 19.8 %collective-permute-start.26 = (bf16[192,768]{1,0:T(8,128)(2,1)}, bf16[192,768]{1,0:T(8,128)(2,1)S(1)}, u32[]{:S(2)}, u32[]{:S(2)}) collective-permute-start(bf16[192,768]{1,0:T(8,128)(2,1)} %fusion.3), channel_id=1, source_target_pairs={{0,4},{2,6},{4,0},{6,2},{8,12},{10,14},{12,8},{14,10},{16,20},{18,... | collective-permute-start | bytes 884744 | tf_op jit(solution)/shard_map/ppermute | solution.py:43
  135.1 22.7 %collective-permute-start.28 = (bf16[96,1024]{1,0:T(8,128)(2,1)}, bf16[96,1024]{1,0:T(8,128)(2,1)S(1)}, u32[]{:S(2)}, u32[]{:S(2)}) collective-permute-start(bf16[96,1024]{1,0:T(8,128)(2,1)} %get-tuple-element.336), channel_id=1, source_target_pairs={{0,8},{2,10},{4,12},{6,14},{8,16},{10,18},{12,20},{14,22},{16,24},... | collective-permute-start | bytes 589832 | tf_op jit(solution)/shard_map/ppermute | solution.py:60
  136.8 21.1 %collective-permute-start.29 = (bf16[96,1024]{1,0:T(8,128)(2,1)}, bf16[96,1024]{1,0:T(8,128)(2,1)S(1)}, u32[]{:S(2)}, u32[]{:S(2)}) collective-permute-start(bf16[96,1024]{1,0:T(8,128)(2,1)} %get-tuple-element.337), channel_id=1, source_target_pairs={{0,16},{2,18},{4,20},{6,22},{8,24},{10,26},{12,28},{14,30},{16,0},... | collective-permute-start | bytes 589832 | tf_op jit(solution)/shard_map/ppermute | solution.py:60
  138.2 19.7 %collective-permute-start.30 = (bf16[96,1024]{1,0:T(8,128)(2,1)}, bf16[96,1024]{1,0:T(8,128)(2,1)S(1)}, u32[]{:S(2)}, u32[]{:S(2)}) collective-permute-start(bf16[96,1024]{1,0:T(8,128)(2,1)} %get-tuple-element.338), channel_id=1, source_target_pairs={{0,24},{2,26},{4,28},{6,30},{8,0},{10,2},{12,4},{14,6},{16,8},{18,... | collective-permute-start | bytes 589832 | tf_op jit(solution)/shard_map/ppermute | solution.py:60
  139.2 18.7 %collective-permute-start.31 = (bf16[384,512]{1,0:T(8,128)(2,1)}, bf16[384,512]{1,0:T(8,128)(2,1)S(1)}, u32[]{:S(2)}, u32[]{:S(2)}) collective-permute-start(bf16[384,512]{1,0:T(8,128)(2,1)} %get-tuple-element.339), channel_id=1, source_target_pairs={{0,1},{1,0},{2,3},{3,2},{4,5},{5,4},{6,7},{7,6},{8,9},{9,8},{10,11... | collective-permute-start | bytes 1179656 | tf_op jit(solution)/shard_map/ppermute | solution.py:43
  140.8 17.0 %collective-permute-start.32 = (bf16[1,2,96,768]{3,2,1,0:T(8,128)(2,1)S(1)}, bf16[1,2,96,768]{3,2,1,0:T(8,128)(2,1)S(1)}, u32[]{:S(2)}, u32[]{:S(2)}) collective-permute-start(bf16[1,2,96,768]{3,2,1,0:T(8,128)(2,1)S(1)} %slice.208), channel_id=1, source_target_pairs={{0,1},{1,0},{2,3},{3,2},{4,5},{5,4},{6,7},{7,6},{8,9},{9,8},{10,11... | collective-permute-start | bytes 884744 | tf_op jit(solution)/shard_map/ppermute | solution.py:43
  161.2 18.6 %collective-permute-start.34 = (bf16[4,3,64,384]{3,2,1,0:T(8,128)(2,1)S(1)}, bf16[4,3,64,384]{3,2,1,0:T(8,128)(2,1)S(1)}, u32[]{:S(2)}, u32[]{:S(2)}) collective-permute-start(bf16[4,3,64,384]{3,2,1,0:T(8,128)(2,1)S(1)} %fusion), channel_id=1, source_target_pairs={{0,4},{2,6},{4,0},{6,2},{8,12},{10,14},{12,8},{14,10},{16,20},{18,... | collective-permute-start | bytes 1769480 | tf_op jit(solution)/shard_map/ppermute | solution.py:43
  162.1 17.7 %collective-permute-start.38 = (bf16[1,96,768]{2,1,0:T(8,128)(2,1)S(1)}, bf16[1,96,768]{2,1,0:T(8,128)(2,1)S(1)}, u32[]{:S(2)}, u32[]{:S(2)}) collective-permute-start(bf16[1,96,768]{2,1,0:T(8,128)(2,1)S(1)} %slice.210), channel_id=1, source_target_pairs={{0,4},{2,6},{4,0},{6,2},{8,12},{10,14},{12,8},{14,10},{16,20},{18,... | collective-permute-start | bytes 442376 | tf_op jit(solution)/shard_map/ppermute | solution.py:43
  163.5 23.6 %collective-permute-start.35 = (bf16[96,1024]{1,0:T(8,128)(2,1)S(1)}, bf16[96,1024]{1,0:T(8,128)(2,1)S(1)}, u32[]{:S(2)}, u32[]{:S(2)}) collective-permute-start(bf16[96,1024]{1,0:T(8,128)(2,1)S(1)} %add_convert_fusion.3), channel_id=1, source_target_pairs={{0,8},{2,10},{4,12},{6,14},{8,16},{10,18},{12,20},{14,22},{16,24},... | collective-permute-start | bytes 589832 | tf_op jit(solution)/shard_map/ppermute | solution.py:60
  164.5 22.6 %collective-permute-start.36 = (bf16[96,1024]{1,0:T(8,128)(2,1)S(1)}, bf16[96,1024]{1,0:T(8,128)(2,1)S(1)}, u32[]{:S(2)}, u32[]{:S(2)}) collective-permute-start(bf16[96,1024]{1,0:T(8,128)(2,1)S(1)} %add_convert_fusion.3), channel_id=1, source_target_pairs={{0,16},{2,18},{4,20},{6,22},{8,24},{10,26},{12,28},{14,30},{16,0},... | collective-permute-start | bytes 589832 | tf_op jit(solution)/shard_map/ppermute | solution.py:60
  166.0 21.1 %collective-permute-start.37 = (bf16[96,1024]{1,0:T(8,128)(2,1)S(1)}, bf16[96,1024]{1,0:T(8,128)(2,1)S(1)}, u32[]{:S(2)}, u32[]{:S(2)}) collective-permute-start(bf16[96,1024]{1,0:T(8,128)(2,1)S(1)} %add_convert_fusion.3), channel_id=1, source_target_pairs={{0,24},{2,26},{4,28},{6,30},{8,0},{10,2},{12,4},{14,6},{16,8},{18,... | collective-permute-start | bytes 589832 | tf_op jit(solution)/shard_map/ppermute | solution.py:60
  188.7 22.4 %collective-permute-start.43 = (bf16[4,96,1024]{2,1,0:T(8,128)(2,1)S(1)}, bf16[4,96,1024]{2,1,0:T(8,128)(2,1)S(1)}, u32[]{:S(2)}, u32[]{:S(2)}) collective-permute-start(bf16[4,96,1024]{2,1,0:T(8,128)(2,1)S(1)} %pad_maximum_fusion.1.refs_0_), channel_id=1, source_target_pairs={{0,4},{2,6},{4,0},{6,2},{8,12},{10,14},{12,8},{14,10},{16,20},{18,... | collective-permute-start | bytes 2359304 | tf_op jit(solution)/shard_map/ppermute | solution.py:43
  191.1 25.8 %collective-permute-start.48 = (bf16[400,768]{1,0:T(8,128)(2,1)S(1)}, bf16[400,768]{1,0:T(8,128)(2,1)S(1)}, u32[]{:S(2)}, u32[]{:S(2)}) collective-permute-start(bf16[400,768]{1,0:T(8,128)(2,1)S(1)} %pad_maximum_fusion.2), channel_id=1, source_target_pairs={{0,8},{2,10},{4,12},{6,14},{8,0},{10,2},{12,4},{14,6},{16,24},{18,... | collective-permute-start | bytes 1843208 | tf_op jit(solution)/shard_map/ppermute | solution.py:43
  199.3 16.3 %collective-permute-start.47 = (bf16[96,1280]{1,0:T(8,128)(2,1)S(1)}, bf16[96,1280]{1,0:T(8,128)(2,1)S(1)}, u32[]{:S(2)}, u32[]{:S(2)}) collective-permute-start(bf16[96,1280]{1,0:T(8,128)(2,1)S(1)} %pad_maximum_fusion.5), channel_id=1, source_target_pairs={{0,16},{2,18},{4,20},{6,22},{8,24},{10,26},{12,28},{14,30},{16,0},... | collective-permute-start | bytes 737288 | tf_op jit(solution)/shard_map/ppermute | solution.py:43
  225.9 16.8 %collective-permute-start.55 = (bf16[96,3328]{1,0:T(8,128)(2,1)S(1)}, bf16[96,3328]{1,0:T(8,128)(2,1)S(1)}, u32[]{:S(2)}, u32[]{:S(2)}) collective-permute-start(bf16[96,3328]{1,0:T(8,128)(2,1)S(1)} %fusion.7.refs_4_), channel_id=1, source_target_pairs={{0,4},{2,6},{4,0},{6,2},{8,12},{10,14},{12,8},{14,10},{16,20},{18,... | collective-permute-start | bytes 1916936 | tf_op jit(solution)/shard_map/ppermute | solution.py:43
  240.5 20.1 %collective-permute-start.60 = (bf16[4,96,512]{2,1,0:T(8,128)(2,1)S(1)}, bf16[4,96,512]{2,1,0:T(8,128)(2,1)}, u32[]{:S(2)}, u32[]{:S(2)}) collective-permute-start(bf16[4,96,512]{2,1,0:T(8,128)(2,1)S(1)} %pad_maximum_fusion.3.refs_0_), channel_id=1, source_target_pairs={{0,4},{2,6},{4,0},{6,2},{8,12},{10,14},{12,8},{14,10},{16,20},{18,... | collective-permute-start | bytes 1179656 | tf_op jit(solution)/shard_map/ppermute | solution.py:43
  242.9 17.7 %collective-permute-start.59 = (bf16[208,768]{1,0:T(8,128)(2,1)S(1)}, bf16[208,768]{1,0:T(8,128)(2,1)S(1)}, u32[]{:S(2)}, u32[]{:S(2)}) collective-permute-start(bf16[208,768]{1,0:T(8,128)(2,1)S(1)} %pad_maximum_fusion.4), channel_id=1, source_target_pairs={{0,16},{2,18},{4,20},{6,22},{8,24},{10,26},{12,28},{14,30},{16,0},... | collective-permute-start | bytes 958472 | tf_op jit(solution)/shard_map/ppermute | solution.py:43
  (93 other events, 743.4 us)
